TPU v7x, 256 devices: a whole 4x4x8 slice. The times are simulated.
256 devices in a mesh: grp: 4 (over x), dev: 64 (over y, z, core).
Axes of the slice: x: 4, y: 4, z: 8, core: 2. Of those that a mesh axis runs over, the one named last changes fastest.
Arguments:
- orbitals: bfloat16 [512, 4, 128, 128], P(('grp', 'dev')), may hold values from -0.359375 to 0.359375
- domains: int32 [512, 4], replicated, may hold values from 0 to 19, as said below
- partners: int32 [512, 72], P(('grp', 'dev')), may hold values from 0 to 511, as said below
- active: int32 [512], P(('grp', 'dev')), may hold values from 1 to 64
- fock_terms: float32 [512, 72], P(('grp', 'dev')), may hold values from -0.5 to 0.5
- exchange_ints: bfloat16 [512, 128, 128], P(('grp', 'dev')), may hold values from -12 to 12
- pno_energies: float32 [512, 128], P(('grp', 'dev')), may hold values from 0.2 to 2
- occ_energies: float32 [512], P(('grp', 'dev')), may hold values from -1.6 to -0.5
- amplitudes: float32 [512, 128, 128], P(('grp', 'dev')), may hold values from -6 to 6
Outputs:
- updated: float32 [512, 128, 128], P(('grp', 'dev'))
- residual: float32 [512, 128, 128], P(('grp', 'dev'))
Inputs may be any that keep to these rules, and one draw needn't show every extreme that they name: Pairs are numbered group by group along grp, then device by device along dev, 2 to a device. For s < 64, partners[q, s] is a pair held by device s of q's group, and all pairs held by one device name the same pair in slot s. For s >= 64, partners[q, s] is held by the device with the same dev index in the group just before or just after q's group. `domains`: the 4 labels of a row are distinct and lie in 4 * g to 4 * g + 2 * 4 - 1, g the group of the pair.
All inputs are finite; a program needn't handle non-finite values.
Results may differ from a plain program's by a relative error of at most 0.023.
Values may be sent and summed in bfloat16 or wider, within the bound.
No kernel may reach another device: no remote copies, remote signals or barrier semaphores. Data moves between devices by JAX's collectives and lax.ppermute only.
A program may use at most 128 MiB of HBM per device.

v0:
```python
import functools

import jax
import jax.numpy as jnp
from jax import lax
from jax.experimental import pallas as pl
from jax.experimental.pallas import tpu as pltpu
from jax.sharding import PartitionSpec as P

N_Y, N_Z, N_CORE = 4, 8, 2
N_DEV = N_Y * N_Z * N_CORE
COUP_IN = 64
W = 128
OROWS = 512
BF16 = jnp.bfloat16
F32 = jnp.float32
SMEM = pl.BlockSpec(memory_space=pltpu.SMEM)
VMEM = pl.BlockSpec(memory_space=pltpu.VMEM)
ANY = pl.BlockSpec(memory_space=pl.ANY)
PARAMS = pltpu.CompilerParams(vmem_limit_bytes=40 * 1024 * 1024)


def place(y, z, c):
    return ((y % N_Y) * N_Z + z % N_Z) * N_CORE + c


def routes(move):
    return [
        (place(y, z, c), move(y, z, c))
        for y in range(N_Y)
        for z in range(N_Z)
        for c in range(N_CORE)
    ]


def send(x, move):
    return lax.ppermute(x, "dev", routes(move))


def swap(x):
    return send(x, lambda y, z, c: place(y, z, 1 - c))


def along_z(x, k):
    return send(x, lambda y, z, c: place(y, z + k if c == 0 else z - k, c))


def along_y(x, k):
    return send(x, lambda y, z, c: place(y + k, z, c))


def cost(products, nbytes):
    return pl.CostEstimate(flops=products * 2 * W**3 * 3, bytes_accessed=nbytes, transcendentals=0)


def bundle_kernel(orb_ref, amp_ref, out_ref):
    out_ref[:, pl.ds(0, OROWS), :] = orb_ref[...].reshape(2, OROWS, W)
    out_ref[:, pl.ds(OROWS, W), :] = amp_ref[...].astype(BF16)


def bundle(orbitals, amplitudes):
    return pl.pallas_call(
        bundle_kernel,
        out_shape=jax.ShapeDtypeStruct((2, OROWS + W, W), BF16),
        in_specs=[VMEM, VMEM],
        out_specs=VMEM,
        compiler_params=PARAMS,
        cost_estimate=cost(0, 700000),
    )(orbitals, amplitudes)


def turned_kernel(orb_ref, words_ref, out_ref):
    for q in range(2):
        for a in range(4):
            out_ref[pl.ds((q * 4 + a) * W, W), :] = orb_ref[q, a].T
    words = words_ref[...]
    high = words.astype(BF16).astype(F32)
    middle = (words - high).astype(BF16).astype(F32)
    low = words - high - middle
    row = lax.broadcasted_iota(jnp.int32, (16, W), 0)
    parts = jnp.where(row < 2, high, jnp.where(row < 4, middle, jnp.where(row < 6, low, 0.0)))
    out_ref[pl.ds(2 * OROWS, 16), :] = parts.astype(BF16)


def turned(orbitals, words):
    return pl.pallas_call(
        turned_kernel,
        out_shape=jax.ShapeDtypeStruct((2 * OROWS + 16, W), BF16),
        in_specs=[VMEM, VMEM],
        out_specs=VMEM,
        compiler_params=PARAMS,
        cost_estimate=cost(0, 600000),
    )(orbitals, words)


def block_rows(dom_ref, base, q_id, p_id, q, zero_row):
    labels = [dom_ref[q_id * 4 + a] for a in range(4)]
    rows = []
    for b in range(4):
        label = dom_ref[p_id * 4 + b]
        row = zero_row
        for a in range(4):
            row = jnp.where(labels[a] == label, base + (q * 4 + a) * W, row)
        rows.append(pl.multiple_of(row, W))
    return rows


def intersect(qbuf, rows, partner):
    left = jnp.concatenate(
        [
            jnp.concatenate([qbuf[pl.ds(row, W), :] for row in rows_q], axis=1)
            for rows_q in rows
        ],
        axis=0,
    )
    return jnp.dot(left, partner, preferred_element_type=F32).astype(BF16)


def weighted(inter, amps, w0, w1):
    half = jnp.dot(inter, amps, preferred_element_type=F32)
    return (half[:W] * w0).astype(BF16), (half[W:] * w1).astype(BF16)


def frame(halves, inters):
    return lax.dot_general(
        jnp.concatenate(halves, axis=1),
        jnp.concatenate(inters, axis=1),
        (((1,), (1,)), ((), ())),
        preferred_element_type=F32,
    )


def slot_of(pos_ref, chunk):
    step, mine = chunk
    y, z, c = pos_ref[1], pos_ref[2], pos_ref[3]
    zz = jnp.where(c == 0, z - step, z + step) & (N_Z - 1)
    lane = c if mine else 1 - c
    return (y * N_Z + zz) * N_CORE + lane


def owner_of(pos_ref, i):
    y, z, c = pos_ref[1], pos_ref[2], pos_ref[3]
    yy = (y - (i & 3)) & (N_Y - 1)
    lane = jnp.where(i < 4, c, 1 - c)
    return (yy * N_Z + z) * N_CORE + lane


def first_kernel(chunks, first, count, has_prev, *refs):
    n = len(chunks)
    pos_ref, dom_ref, word_ref = refs[:3]
    q_refs = refs[3 : 3 + count]
    p_refs = refs[3 + count : 3 + count + n]
    rest = refs[3 + count + n :]
    prev_ref = rest[0] if has_prev else None
    inter_ref, out_ref, qbuf, pbuf, q_sem, p_sem = rest[1 if has_prev else 0 :]
    step = pl.program_id(0)
    zero_row = count * 2 * OROWS

    @pl.when(step == 0)
    def _():
        p_copies = [
            pltpu.make_async_copy(p_refs[j], pbuf.at[j], p_sem.at[j]) for j in range(n)
        ]
        q_copies = [
            pltpu.make_async_copy(
                q_refs[k].at[pl.ds(0, 2 * OROWS)],
                qbuf.at[pl.ds(k * 2 * OROWS, 2 * OROWS)],
                q_sem.at[k],
            )
            for k in range(count)
        ]
        q_copies[0].start()
        for copy in p_copies:
            copy.start()
        for copy in q_copies[1:]:
            copy.start()
        qbuf[pl.ds(zero_row, W), :] = jnp.zeros((W, W), BF16)
        for copy in p_copies:
            copy.wait()

    base = pl.multiple_of(step * 2 * OROWS, 2 * OROWS)
    pltpu.make_async_copy(
        q_refs[0].at[pl.ds(0, 2 * OROWS)], qbuf.at[pl.ds(base, 2 * OROWS)], q_sem.at[step]
    ).wait()
    i = step + first
    group = pos_ref[0] * N_DEV
    q_id = (group + owner_of(pos_ref, i)) * 2
    halves, inters = [[], []], [[], []]
    for j, chunk in enumerate(chunks):
        slot = slot_of(pos_ref, chunk)
        row = word_ref[i * 2 * W + COUP_IN + slot].astype(jnp.int32)
        p_id = (group + slot) * 2 + row
        rows = [block_rows(dom_ref, base, q_id + q, p_id, q, zero_row) for q in range(2)]
        inter = intersect(qbuf, rows, pbuf[j, row, pl.ds(0, OROWS), :])
        inter_ref[0, j] = inter
        weights = [word_ref[(i * 2 + q) * W + slot] for q in range(2)]
        half = weighted(inter, pbuf[j, row, pl.ds(OROWS, W), :], *weights)
        for q in range(2):
            halves[q].append(half[q])
            inters[q].append(inter[q * W : (q + 1) * W])
    for q in range(2):
        total = frame(halves[q], inters[q])
        if has_prev:
            total = total + prev_ref[0, q]
        out_ref[0, q] = total.astype(out_ref.dtype)


def first_couple(pos, dom, words, turned_all, chunks, chunk_data, first, count, prev, out_type):
    n = len(chunks)
    whole = pl.BlockSpec((1, 2, W, W), lambda s: (s, 0, 0, 0))
    prev_spec = pl.BlockSpec((1, 2, W, W), lambda s: (s + first, 0, 0, 0))
    return pl.pallas_call(
        functools.partial(first_kernel, chunks, first, count, prev is not None),
        grid=(count,),
        out_shape=(
            jax.ShapeDtypeStruct((count, n, 2 * W, W), BF16),
            jax.ShapeDtypeStruct((count, 2, W, W), out_type),
        ),
        in_specs=[SMEM] * 3 + [ANY] * (count + n) + ([prev_spec] if prev is not None else []),
        out_specs=(pl.BlockSpec((1, n, 2 * W, W), lambda s: (s, 0, 0, 0)), whole),
        scratch_shapes=[
            pltpu.VMEM((count * 2 * OROWS + W, W), BF16),
            pltpu.VMEM((n, 2, OROWS + W, W), BF16),
            pltpu.SemaphoreType.DMA((count,)),
            pltpu.SemaphoreType.DMA((n,)),
        ],
        compiler_params=PARAMS,
        cost_estimate=cost(count * n * 2 * 6, 3000000),
    )(
        pos,
        dom,
        words,
        *turned_all[first : first + count],
        *chunk_data,
        *([prev] if prev is not None else []),
    )


def next_kernel(chunks, places, first, n_amps, has_prev, *refs):
    pos_ref, word_ref, inter_ref = refs[:3]
    amp_refs = refs[3 : 3 + n_amps]
    prev_ref = refs[3 + n_amps] if has_prev else None
    out_ref = refs[-1]
    i = pl.program_id(0) + first
    halves, inters = [[], []], [[], []]
    for j, chunk in enumerate(chunks):
        slot = slot_of(pos_ref, chunk)
        row = word_ref[i * 2 * W + COUP_IN + slot].astype(jnp.int32)
        weights = [word_ref[(i * 2 + q) * W + slot] for q in range(2)]
        which, offset = places[j]
        inter = inter_ref[0, j]
        half = weighted(inter, amp_refs[which][offset + row], *weights)
        for q in range(2):
            halves[q].append(half[q])
            inters[q].append(inter[q * W : (q + 1) * W])
    for q in range(2):
        total = frame(halves[q], inters[q])
        if has_prev:
            total = total + prev_ref[0, q]
        out_ref[0, q] = total.astype(out_ref.dtype)


def next_couple(pos, words, inter, chunks, places, amps, first, prev, out_type):
    count, n = inter.shape[:2]
    whole = pl.BlockSpec((1, 2, W, W), lambda s: (s, 0, 0, 0))
    prev_spec = pl.BlockSpec((1, 2, W, W), lambda s: (s + first, 0, 0, 0))
    return pl.pallas_call(
        functools.partial(next_kernel, chunks, places, first, len(amps), prev is not None),
        grid=(count,),
        out_shape=jax.ShapeDtypeStruct((count, 2, W, W), out_type),
        in_specs=[SMEM] * 2
        + [pl.BlockSpec((1, n, 2 * W, W), lambda s: (s, 0, 0, 0))]
        + [VMEM] * len(amps)
        + ([prev_spec] if prev is not None else []),
        out_specs=whole,
        compiler_params=PARAMS,
        cost_estimate=cost(count * n * 2 * 2, 3000000),
    )(pos, words, inter, *amps, *([prev] if prev is not None else []))


def cross_first_kernel(pos_ref, dom_ref, weight_ref, near_ref, own_ref, inter_ref, out_ref, qbuf):
    qbuf[pl.ds(0, 2 * OROWS), :] = own_ref[pl.ds(0, 2 * OROWS), :]
    qbuf[pl.ds(2 * OROWS, W), :] = jnp.zeros((W, W), BF16)
    group, place_here = pos_ref[0], (pos_ref[1] * N_Z + pos_ref[2]) * N_CORE + pos_ref[3]
    q_id = (group * N_DEV + place_here) * 2
    halves, inters = [[], []], [[], []]
    for j in range(4):
        there = jnp.clip(group + (1 if j >= 2 else -1), 0, 3)
        p_id = (there * N_DEV + place_here) * 2 + j % 2
        rows = [block_rows(dom_ref, 0, q_id + q, p_id, q, 2 * OROWS) for q in range(2)]
        pair = there * 2 + j % 2
        inter = intersect(qbuf, rows, near_ref[pair, pl.ds(0, OROWS), :])
        inter_ref[j] = inter
        half = weighted(
            inter, near_ref[pair, pl.ds(OROWS, W), :], weight_ref[j], weight_ref[4 + j]
        )
        for q in range(2):
            halves[q].append(half[q])
            inters[q].append(inter[q * W : (q + 1) * W])
    for q in range(2):
        out_ref[q] = frame(halves[q], inters[q])


def cross_first(pos, dom, weights, near, own):
    return pl.pallas_call(
        cross_first_kernel,
        out_shape=(
            jax.ShapeDtypeStruct((4, 2 * W, W), BF16),
            jax.ShapeDtypeStruct((2, W, W), F32),
        ),
        in_specs=[SMEM] * 3 + [VMEM] * 2,
        out_specs=(VMEM, VMEM),
        scratch_shapes=[pltpu.VMEM((2 * OROWS + W, W), BF16)],
        compiler_params=PARAMS,
        cost_estimate=cost(8 * 6, 2000000),
    )(pos, dom, weights, near, own)


def cross_next_kernel(weight_ref, inter_ref, below_ref, above_ref, out_ref):
    halves, inters = [[], []], [[], []]
    for j in range(4):
        amps = (below_ref if j < 2 else above_ref)[j % 2]
        inter = inter_ref[j]
        half = weighted(inter, amps, weight_ref[j], weight_ref[4 + j])
        for q in range(2):
            halves[q].append(half[q])
            inters[q].append(inter[q * W : (q + 1) * W])
    for q in range(2):
        out_ref[q] = frame(halves[q], inters[q])


def cross_next(weights, inter, below, above):
    return pl.pallas_call(
        cross_next_kernel,
        out_shape=jax.ShapeDtypeStruct((2, W, W), F32),
        in_specs=[SMEM] + [VMEM] * 3,
        out_specs=VMEM,
        compiler_params=PARAMS,
        cost_estimate=cost(8 * 2, 500000),
    )(weights, inter, below, above)


def gather_shares(mine, others):
    total = mine + swap(others).astype(F32)
    shares = [send_back(total[j].astype(BF16), j) for j in range(1, N_Y)]
    return total[0] + (shares[0].astype(F32) + shares[1].astype(F32) + shares[2].astype(F32))


def send_back(x, j):
    return along_y(x, -j)


def on_device(
    orbitals,
    domains,
    partners,
    active,
    fock_terms,
    exchange_ints,
    pno_energies,
    occ_energies,
    amplitudes,
):
    group = lax.axis_index("grp")
    dev = lax.axis_index("dev")
    pos = jnp.stack([group, dev // (N_Z * N_CORE), dev // N_CORE % N_Z, dev % N_CORE])
    pos = pos.astype(jnp.int32)
    dom = domains.reshape(-1)

    slots = jnp.arange(COUP_IN, dtype=jnp.int32)[None, :]
    live = jnp.where(slots < active[:, None], fock_terms[:, :COUP_IN], 0.0)
    wanted = (partners[:, :COUP_IN] % 2).astype(F32)
    words_own = jnp.tile(jnp.concatenate([live, wanted], axis=1), (8, 1))
    near_ids = ((group + jnp.array([-1, -1, 1, 1])) * N_DEV + dev) * 2 + jnp.array([0, 1, 0, 1])
    same = partners[:, None, COUP_IN:] == near_ids[None, :, None]
    cross_w = jnp.sum(jnp.where(same, fock_terms[:, None, COUP_IN:], 0.0), axis=2).reshape(8)

    mine = bundle(orbitals, amplitudes)
    turned_mine = turned(orbitals, words_own)
    ring_a = [mine]
    ring_b = [swap(mine)]
    for k in range(4):
        ring_a.append(along_z(ring_a[-1], 1))
        if k < 3:
            ring_b.append(along_z(ring_b[-1], 1))
    turned_all = [turned_mine] + [along_y(turned_mine, k) for k in range(1, N_Y)]
    turned_all = turned_all + [swap(x) for x in turned_all]
    near = lax.all_gather(mine, "grp", axis=0, tiled=True)

    words = jnp.stack([x[2 * OROWS :] for x in turned_all]).astype(F32)
    words = (words[:, 0:2] + words[:, 2:4] + words[:, 4:6]).reshape(-1)

    early = [(0, True), (1, True), (1, False), (2, True), (2, False)]
    early_data = [ring_a[0], ring_a[1], ring_b[1], ring_a[2], ring_b[2]]
    late = [(3, True), (3, False), (4, True)]
    late_data = [ring_a[3], ring_b[3], ring_a[4]]

    first = functools.partial(first_couple, pos, dom, words, turned_all)
    inter_early, part = first(early, early_data, 0, 8, None, F32)
    inter_other, others = first(late, late_data, 4, 4, part, BF16)
    inter_mine, own = first(late, late_data, 0, 4, part, F32)
    inter_cross, cross = cross_first(pos, dom, cross_w, near, turned_mine)

    denominator = pno_energies[:, :, None] + pno_energies[:, None, :] - occ_energies[:, None, None]
    integrals = exchange_ints.astype(F32)
    coupled = gather_shares(own, others) + cross
    residual = integrals + denominator * amplitudes - coupled
    current = amplitudes - residual / denominator

    sent = current.astype(BF16)
    below = lax.ppermute(sent, "grp", [(0, 1), (1, 2), (2, 3)])
    above = lax.ppermute(sent, "grp", [(1, 0), (2, 1), (3, 2)])
    far = along_z(sent, 4)
    both = jnp.concatenate([sent, swap(sent)], axis=0)
    steps = [along_z(both, k) for k in range(1, 4)]

    again = functools.partial(next_couple, pos, words)
    early_places = [(0, 0), (1, 0), (1, 2), (2, 0), (2, 2)]
    late_places = [(0, 0), (0, 2), (1, 0)]
    part = again(inter_early, early, early_places, [sent, steps[0], steps[1]], 0, None, F32)
    late_amps = [steps[2], far]
    others = again(inter_other, late, late_places, late_amps, 4, part, BF16)
    own = again(inter_mine, late, late_places, late_amps, 0, part, F32)
    cross = cross_next(cross_w, inter_cross, below, above)
    coupled = gather_shares(own, others) + cross
    residual = integrals + denominator * current - coupled
    updated = current - residual / denominator
    return updated, residual


def solution(mesh):
    placed = (
        P(("grp", "dev"), None, None, None),
        P(),
        P(("grp", "dev"), None),
        P(("grp", "dev")),
        P(("grp", "dev"), None),
        P(("grp", "dev"), None, None),
        P(("grp", "dev"), None),
        P(("grp", "dev")),
        P(("grp", "dev"), None, None),
    )
    return jax.shard_map(
        on_device,
        mesh=mesh,
        in_specs=placed,
        out_specs=(P(("grp", "dev"), None, None), P(("grp", "dev"), None, None)),
        check_vma=False,
    )
```

profile of v0, /device:TPU:1, one launch (start us, length us, event | category | flops | bytes accessed | tf_op | source)
XLA Modules:
  0.0 129.2 jit_solution(13391205809331154714)
XLA Ops:
  9.8 2.2 %collective-permute-start = (bf16[1040,128]{1,0:T(8,128)(2,1)S(1)}, bf16[1040,128]{1,0:T(8,128)(2,1)S(1)}, u32[]{:S(2)}, u32[]{:S(2)}) collective-permute-start(bf16[1040,128]{1,0:T(8,128)(2,1)S(1)} %shard_map.122.refs_3_.own_ref), channel_id=1, source_target_pairs={{0,16},{1,17},{2,18},{3,19},{4,20},{5,21},{6,22},{7,23},{8,24},{9,... | collective-permute-start | bytes 798728 | tf_op jit(solution)/shard_map/ppermute | solution.py:37
  12.0 2.6 %collective-permute-start.1 = (bf16[1040,128]{1,0:T(8,128)(2,1)S(1)}, bf16[1040,128]{1,0:T(8,128)(2,1)S(1)}, u32[]{:S(2)}, u32[]{:S(2)}) collective-permute-start(bf16[1040,128]{1,0:T(8,128)(2,1)S(1)} %shard_map.122.refs_3_.own_ref), channel_id=1, source_target_pairs={{0,32},{1,33},{2,34},{3,35},{4,36},{5,37},{6,38},{7,39},{8,40},{9,... | collective-permute-start | bytes 798728 | tf_op jit(solution)/shard_map/ppermute | solution.py:37
  15.7 1.5 %collective-permute-start.3 = (bf16[1040,128]{1,0:T(8,128)(2,1)S(1)}, bf16[1040,128]{1,0:T(8,128)(2,1)S(1)}, u32[]{:S(2)}, u32[]{:S(2)}) collective-permute-start(bf16[1040,128]{1,0:T(8,128)(2,1)S(1)} %shard_map.122.refs_3_.own_ref), channel_id=1, source_target_pairs={{0,1},{1,0},{2,3},{3,2},{4,5},{5,4},{6,7},{7,6},{8,9},{9,8},{10,11... | collective-permute-start | bytes 798728 | tf_op jit(solution)/shard_map/ppermute | solution.py:37
  20.1 5.7 %collective-permute-start.7 = (bf16[2,640,128]{2,1,0:T(8,128)(2,1)}, bf16[2,640,128]{2,1,0:T(8,128)(2,1)S(1)}, u32[]{:S(2)}, u32[]{:S(2)}) collective-permute-start(bf16[2,640,128]{2,1,0:T(8,128)(2,1)} %shard_map.123.refs_11_), channel_id=1, source_target_pairs={{0,2},{1,15},{2,4},{3,1},{4,6},{5,3},{6,8},{7,5},{8,10},{9,7},{10,... | collective-permute-start | bytes 983048 | tf_op jit(solution)/shard_map/ppermute | solution.py:37
  26.1 1.5 %collective-permute-start.4 = (bf16[1040,128]{1,0:T(8,128)(2,1)S(1)}, bf16[1040,128]{1,0:T(8,128)(2,1)S(1)}, u32[]{:S(2)}, u32[]{:S(2)}) collective-permute-start(bf16[1040,128]{1,0:T(8,128)(2,1)S(1)} %collective-permute-done.refs_4_), channel_id=1, source_target_pairs={{0,1},{1,0},{2,3},{3,2},{4,5},{5,4},{6,7},{7,6},{8,9},{9,8},{10,11... | collective-permute-start | bytes 798728 | tf_op jit(solution)/shard_map/ppermute | solution.py:37
  28.2 5.6 %collective-permute-start.11 = (bf16[2,640,128]{2,1,0:T(8,128)(2,1)S(1)}, bf16[2,640,128]{2,1,0:T(8,128)(2,1)S(1)}, u32[]{:S(2)}, u32[]{:S(2)}) collective-permute-start(bf16[2,640,128]{2,1,0:T(8,128)(2,1)S(1)} %collective-permute-done.10), channel_id=1, source_target_pairs={{0,2},{1,15},{2,4},{3,1},{4,6},{5,3},{6,8},{7,5},{8,10},{9,7},{10,... | collective-permute-start | bytes 983048 | tf_op jit(solution)/shard_map/ppermute | solution.py:37
  34.6 3.3 %collective-permute-done.11.refs_13_ = bf16[2,640,128]{2,1,0:T(8,128)(2,1)S(1)} collective-permute-done((bf16[2,640,128]{2,1,0:T(8,128)(2,1)S(1)}, bf16[2,640,128]{2,1,0:T(8,128)(2,1)S(1)}, u32[]{:S(2)}, u32[]{:S(2)}) %collective-permute-start.11) | collective-permute-done | bytes 327712 | tf_op jit(solution)/shard_map/ppermute | solution.py:37
  37.8 3.5 %collective-permute-start.12 = (bf16[2,640,128]{2,1,0:T(8,128)(2,1)S(1)}, bf16[2,640,128]{2,1,0:T(8,128)(2,1)S(1)}, u32[]{:S(2)}, u32[]{:S(2)}) collective-permute-start(bf16[2,640,128]{2,1,0:T(8,128)(2,1)S(1)} %collective-permute-done.11.refs_13_), channel_id=1, source_target_pairs={{0,2},{1,15},{2,4},{3,1},{4,6},{5,3},{6,8},{7,5},{8,10},{9,7},{10,... | collective-permute-start | bytes 983048 | tf_op jit(solution)/shard_map/ppermute | solution.py:37
  41.3 3.5 %collective-permute-start.9 = (bf16[2,640,128]{2,1,0:T(8,128)(2,1)S(1)}, bf16[2,640,128]{2,1,0:T(8,128)(2,1)S(1)}, u32[]{:S(2)}, u32[]{:S(2)}) collective-permute-start(bf16[2,640,128]{2,1,0:T(8,128)(2,1)S(1)} %collective-permute-done.8.refs_14_), channel_id=1, source_target_pairs={{0,2},{1,15},{2,4},{3,1},{4,6},{5,3},{6,8},{7,5},{8,10},{9,7},{10,... | collective-permute-start | bytes 983048 | tf_op jit(solution)/shard_map/ppermute | solution.py:37
  44.9 4.0 %collective-permute-done.9.refs_7_ = bf16[2,640,128]{2,1,0:T(8,128)(2,1)S(1)} collective-permute-done((bf16[2,640,128]{2,1,0:T(8,128)(2,1)S(1)}, bf16[2,640,128]{2,1,0:T(8,128)(2,1)S(1)}, u32[]{:S(2)}, u32[]{:S(2)}) %collective-permute-start.9) | collective-permute-done | bytes 327712 | tf_op jit(solution)/shard_map/ppermute | solution.py:37
  48.9 3.1 %collective-permute-start.14 = (bf16[2,640,128]{2,1,0:T(8,128)(2,1)S(1)}, bf16[2,640,128]{2,1,0:T(8,128)(2,1)S(1)}, u32[]{:S(2)}, u32[]{:S(2)}) collective-permute-start(bf16[2,640,128]{2,1,0:T(8,128)(2,1)S(1)} %collective-permute-done.9.refs_7_), channel_id=1, source_target_pairs={{0,2},{1,15},{2,4},{3,1},{4,6},{5,3},{6,8},{7,5},{8,10},{9,7},{10,... | collective-permute-start | bytes 983048 | tf_op jit(solution)/shard_map/ppermute | solution.py:37
  52.0 12.8 %shard_map.124 = (bf16[8,5,256,128]{3,2,1,0:T(8,128)(2,1)S(1)}, f32[8,2,128,128]{3,2,1,0:T(8,128)S(1)}) custom-call(s32[4]{0:T(128)S(1)} %pad_add_fusion.refs_0_.pos_ref, s32[2048]{0:T(1024)S(1)} %reshape.30.refs_1_.dom_ref, f32[2048]{0:T(1024)S(1)} %bitcast.68, bf16[1040,128]{1,0:T(8,128)(2,1)S(1)} %shard_map.122.refs_3_.own_ref, ...), custom_call_target="tpu_custom_call" | custom-call | flops 6039797760 | bytes 3000000 | tf_op jit(solution)/shard_map/pallas_call | solution.py:212
  64.9 4.9 %shard_map.126 = (bf16[4,3,256,128]{3,2,1,0:T(8,128)(2,1)S(1)}, bf16[4,2,128,128]{3,2,1,0:T(8,128)(2,1)S(1)}) custom-call(s32[4]{0:T(128)S(1)} %pad_add_fusion.refs_0_.pos_ref, s32[2048]{0:T(1024)S(1)} %reshape.30.refs_1_.dom_ref, f32[2048]{0:T(1024)S(1)} %bitcast.69, bf16[1040,128]{1,0:T(8,128)(2,1)S(1)} %collective-permute-done.3.refs_7_.refs_3_, ...), custom_call_target="tpu_custom_call" | custom-call | flops 1811939328 | bytes 3000000 | tf_op jit(solution)/shard_map/pallas_call | solution.py:212
  70.1 4.9 %shard_map.125 = (bf16[4,3,256,128]{3,2,1,0:T(8,128)(2,1)S(1)}, f32[4,2,128,128]{3,2,1,0:T(8,128)S(1)}) custom-call(s32[4]{0:T(128)S(1)} %pad_add_fusion.refs_0_.pos_ref, s32[2048]{0:T(1024)S(1)} %reshape.30.refs_1_.dom_ref, f32[2048]{0:T(1024)S(1)} %bitcast.70, bf16[1040,128]{1,0:T(8,128)(2,1)S(1)} %shard_map.122.refs_3_.own_ref, ...), custom_call_target="tpu_custom_call" | custom-call | flops 1811939328 | bytes 3000000 | tf_op jit(solution)/shard_map/pallas_call | solution.py:212
  75.2 1.6 %collective-permute-start.16 = (bf16[2,128,128]{2,1,0:T(8,128)(2,1)S(1)}, bf16[2,128,128]{2,1,0:T(8,128)(2,1)S(1)}, u32[]{:S(2)}, u32[]{:S(2)}) collective-permute-start(bf16[2,128,128]{2,1,0:T(8,128)(2,1)S(1)} %get-tuple-element.29), channel_id=1, source_target_pairs={{0,48},{1,49},{2,50},{3,51},{4,52},{5,53},{6,54},{7,55},{8,56},{9,... | collective-permute-start | bytes 196616 | tf_op jit(solution)/shard_map/ppermute | solution.py:37
  76.8 2.5 %collective-permute-start.17 = (bf16[2,128,128]{2,1,0:T(8,128)(2,1)S(1)}, bf16[2,128,128]{2,1,0:T(8,128)(2,1)S(1)}, u32[]{:S(2)}, u32[]{:S(2)}) collective-permute-start(bf16[2,128,128]{2,1,0:T(8,128)(2,1)S(1)} %get-tuple-element.31), channel_id=1, source_target_pairs={{0,32},{1,33},{2,34},{3,35},{4,36},{5,37},{6,38},{7,39},{8,40},{9,... | collective-permute-start | bytes 196616 | tf_op jit(solution)/shard_map/ppermute | solution.py:37
  80.2 1.3 %copy-done.3 = bf16[8,640,128]{2,1,0:T(8,128)(2,1)S(1)} copy-done((bf16[8,640,128]{2,1,0:T(8,128)(2,1)S(1)}, bf16[8,640,128]{2,1,0:T(8,128)(2,1)}, u32[]{:S(2)}) %copy-start.3) | copy-done | bytes 1310744
  81.5 1.7 %shard_map.127 = (bf16[4,256,128]{2,1,0:T(8,128)(2,1)S(1)}, f32[2,128,128]{2,1,0:T(8,128)S(1)}) custom-call(s32[4]{0:T(128)S(1)} %pad_add_fusion.refs_0_.pos_ref, s32[2048]{0:T(1024)S(1)} %reshape.30.refs_1_.dom_ref, f32[8]{0:T(128)S(1)} %reshape.32.weight_ref, bf16[8,640,128]{2,1,0:T(8,128)(2,1)S(1)} %copy-done.3, ...), custom_call_target="tpu_custom_call" | custom-call | flops 603979776 | bytes 2000000 | tf_op jit(solution)/shard_map/pallas_call | solution.py:305
  84.2 1.1 collective-permute-start.19
  86.2 3.0 %collective-permute-start.22 = (bf16[4,128,128]{2,1,0:T(8,128)(2,1)S(1)}, bf16[4,128,128]{2,1,0:T(8,128)(2,1)S(1)}, u32[]{:S(2)}, u32[]{:S(2)}) collective-permute-start(bf16[4,128,128]{2,1,0:T(8,128)(2,1)S(1)} %pad_maximum_fusion), channel_id=1, source_target_pairs={{0,2},{1,15},{2,4},{3,1},{4,6},{5,3},{6,8},{7,5},{8,10},{9,7},{10,... | collective-permute-start | bytes 393224 | tf_op jit(solution)/shard_map/ppermute | solution.py:37
  89.2 1.5 %collective-permute-start.23 = (bf16[4,128,128]{2,1,0:T(8,128)(2,1)S(1)}, bf16[4,128,128]{2,1,0:T(8,128)(2,1)S(1)}, u32[]{:S(2)}, u32[]{:S(2)}) collective-permute-start(bf16[4,128,128]{2,1,0:T(8,128)(2,1)S(1)} %pad_maximum_fusion), channel_id=1, source_target_pairs={{0,4},{1,13},{2,6},{3,15},{4,8},{5,1},{6,10},{7,3},{8,12},{9,5},{1... | collective-permute-start | bytes 393224 | tf_op jit(solution)/shard_map/ppermute | solution.py:37
  90.7 4.3 %collective-permute-start.21 = (bf16[2,128,128]{2,1,0:T(8,128)(2,1)S(1)}, bf16[2,128,128]{2,1,0:T(8,128)(2,1)S(1)}, u32[]{:S(2)}, u32[]{:S(2)}) collective-permute-start(bf16[2,128,128]{2,1,0:T(8,128)(2,1)S(1)} %get-tuple-element.22.refs_3_), channel_id=1, source_target_pairs={{0,8},{1,9},{2,10},{3,11},{4,12},{5,13},{6,14},{7,15},{8,0},{9,1},... | collective-permute-start | bytes 196616 | tf_op jit(solution)/shard_map/ppermute | solution.py:37
  95.0 1.3 collective-permute-start.20
  96.5 4.3 %shard_map.128.refs_5_ = f32[8,2,128,128]{3,2,1,0:T(8,128)S(1)} custom-call(s32[4]{0:T(128)S(1)} %pad_add_fusion.refs_0_.pos_ref, f32[2048]{0:T(1024)S(1)} %bitcast.71, bf16[8,5,256,128]{3,2,1,0:T(8,128)(2,1)S(1)} %copy-done.5, bf16[2,128,128]{2,1,0:T(8,128)(2,1)S(1)} %get-tuple-element.22.refs_3_, bf16[4,128,128]{2,1,0:T(8,128)(2,1)S(1)} %collective-permute-done.22.refs_4_, ...), custom_call_target="tpu_custom_call" | custom-call | flops 2013265920 | bytes 3000000 | tf_op jit(solution)/shard_map/pallas_call | solution.py:267
  100.8 1.5 %collective-permute-done.20.refs_3_ = bf16[4,128,128]{2,1,0:T(8,128)(2,1)S(1)} collective-permute-done((bf16[4,128,128]{2,1,0:T(8,128)(2,1)S(1)}, bf16[4,128,128]{2,1,0:T(8,128)(2,1)S(1)}, u32[]{:S(2)}, u32[]{:S(2)}) %collective-permute-start.20) | collective-permute-done | bytes 131104 | tf_op jit(solution)/shard_map/ppermute | solution.py:37
  102.2 2.1 %shard_map.130 = bf16[4,2,128,128]{3,2,1,0:T(8,128)(2,1)S(1)} custom-call(s32[4]{0:T(128)S(1)} %pad_add_fusion.refs_0_.pos_ref, f32[2048]{0:T(1024)S(1)} %bitcast.72, bf16[4,3,256,128]{3,2,1,0:T(8,128)(2,1)S(1)} %get-tuple-element.16.refs_2_, bf16[4,128,128]{2,1,0:T(8,128)(2,1)S(1)} %collective-permute-done.20.refs_3_, ...), custom_call_target="tpu_custom_call" | custom-call | flops 603979776 | bytes 3000000 | tf_op jit(solution)/shard_map/pallas_call | solution.py:267
  104.4 3.1 %collective-permute-start.24 = (bf16[4,2,128,128]{3,2,1,0:T(8,128)(2,1)S(1)}, bf16[4,2,128,128]{3,2,1,0:T(8,128)(2,1)S(1)}, u32[]{:S(2)}, u32[]{:S(2)}) collective-permute-start(bf16[4,2,128,128]{3,2,1,0:T(8,128)(2,1)S(1)} %shard_map.130), channel_id=1, source_target_pairs={{0,1},{1,0},{2,3},{3,2},{4,5},{5,4},{6,7},{7,6},{8,9},{9,8},{10,11... | collective-permute-start | bytes 786440 | tf_op jit(solution)/shard_map/ppermute | solution.py:37
  107.5 3.1 %collective-permute-start.28 = (bf16[2,128,128]{2,1,0:T(8,128)(2,1)S(1)}, bf16[2,128,128]{2,1,0:T(8,128)(2,1)S(1)}, u32[]{:S(2)}, u32[]{:S(2)}) collective-permute-start(bf16[2,128,128]{2,1,0:T(8,128)(2,1)S(1)} %get-tuple-element.22.refs_3_), channel_id=1, source_target_pairs={{0,64},{64,128},{128,192},{1,65},{65,129},{129,193},{2,66},{66,130... | collective-permute-start | bytes 196616 | tf_op jit(solution)/shard_map/ppermute | solution.py:411
  110.6 1.3 collective-permute-start.29
  111.9 2.2 %shard_map.129 = f32[4,2,128,128]{3,2,1,0:T(8,128)S(1)} custom-call(s32[4]{0:T(128)S(1)} %pad_add_fusion.refs_0_.pos_ref, f32[2048]{0:T(1024)S(1)} %bitcast.73, bf16[4,3,256,128]{3,2,1,0:T(8,128)(2,1)S(1)} %get-tuple-element.14.refs_2_, bf16[4,128,128]{2,1,0:T(8,128)(2,1)S(1)} %collective-permute-done.20.refs_3_, ...), custom_call_target="tpu_custom_call" | custom-call | flops 603979776 | bytes 3000000 | tf_op jit(solution)/shard_map/pallas_call | solution.py:267
  117.4 2.3 %collective-permute-done.26 = bf16[2,128,128]{2,1,0:T(8,128)(2,1)S(1)} collective-permute-done((bf16[2,128,128]{2,1,0:T(8,128)(2,1)S(1)}, bf16[2,128,128]{2,1,0:T(8,128)(2,1)S(1)}, u32[]{:S(2)}, u32[]{:S(2)}) %collective-permute-start.26) | collective-permute-done | bytes 65568 | tf_op jit(solution)/shard_map/ppermute | solution.py:37
  119.8 1.8 %collective-permute-done.27 = bf16[2,128,128]{2,1,0:T(8,128)(2,1)S(1)} collective-permute-done((bf16[2,128,128]{2,1,0:T(8,128)(2,1)S(1)}, bf16[2,128,128]{2,1,0:T(8,128)(2,1)S(1)}, u32[]{:S(2)}, u32[]{:S(2)}) %collective-permute-start.27) | collective-permute-done | bytes 65568 | tf_op jit(solution)/shard_map/ppermute | solution.py:37
  (96 shorter events, 15.7 us)
Async XLA Ops:
  7.2 73.1 %all-gather.2.cloned.1.call-start = ((), (), s32[]{:S(2)}) async-start(), calls=%async_computation | async-start | bytes 1638400 | tf_op jit(solution)/shard_map/all_gather | solution.py:388
  9.8 10.3 %collective-permute-start = (bf16[1040,128]{1,0:T(8,128)(2,1)S(1)}, bf16[1040,128]{1,0:T(8,128)(2,1)S(1)}, u32[]{:S(2)}, u32[]{:S(2)}) collective-permute-start(bf16[1040,128]{1,0:T(8,128)(2,1)S(1)} %shard_map.122.refs_3_.own_ref), channel_id=1, source_target_pairs={{0,16},{1,17},{2,18},{3,19},{4,20},{5,21},{6,22},{7,23},{8,24},{9,... | collective-permute-start | bytes 798728 | tf_op jit(solution)/shard_map/ppermute | solution.py:37
  12.0 14.1 %collective-permute-start.1 = (bf16[1040,128]{1,0:T(8,128)(2,1)S(1)}, bf16[1040,128]{1,0:T(8,128)(2,1)S(1)}, u32[]{:S(2)}, u32[]{:S(2)}) collective-permute-start(bf16[1040,128]{1,0:T(8,128)(2,1)S(1)} %shard_map.122.refs_3_.own_ref), channel_id=1, source_target_pairs={{0,32},{1,33},{2,34},{3,35},{4,36},{5,37},{6,38},{7,39},{8,40},{9,... | collective-permute-start | bytes 798728 | tf_op jit(solution)/shard_map/ppermute | solution.py:37
  14.6 13.1 %collective-permute-start.2 = (bf16[1040,128]{1,0:T(8,128)(2,1)S(1)}, bf16[1040,128]{1,0:T(8,128)(2,1)S(1)}, u32[]{:S(2)}, u32[]{:S(2)}) collective-permute-start(bf16[1040,128]{1,0:T(8,128)(2,1)S(1)} %shard_map.122.refs_3_.own_ref), channel_id=1, source_target_pairs={{0,48},{1,49},{2,50},{3,51},{4,52},{5,53},{6,54},{7,55},{8,56},{9,... | collective-permute-start | bytes 798728 | tf_op jit(solution)/shard_map/ppermute | solution.py:37
  15.7 12.1 %collective-permute-start.3 = (bf16[1040,128]{1,0:T(8,128)(2,1)S(1)}, bf16[1040,128]{1,0:T(8,128)(2,1)S(1)}, u32[]{:S(2)}, u32[]{:S(2)}) collective-permute-start(bf16[1040,128]{1,0:T(8,128)(2,1)S(1)} %shard_map.122.refs_3_.own_ref), channel_id=1, source_target_pairs={{0,1},{1,0},{2,3},{3,2},{4,5},{5,4},{6,7},{7,6},{8,9},{9,8},{10,11... | collective-permute-start | bytes 798728 | tf_op jit(solution)/shard_map/ppermute | solution.py:37
  18.9 9.3 %collective-permute-start.10 = (bf16[2,640,128]{2,1,0:T(8,128)(2,1)}, bf16[2,640,128]{2,1,0:T(8,128)(2,1)S(1)}, u32[]{:S(2)}, u32[]{:S(2)}) collective-permute-start(bf16[2,640,128]{2,1,0:T(8,128)(2,1)} %shard_map.123.refs_11_), channel_id=1, source_target_pairs={{0,1},{1,0},{2,3},{3,2},{4,5},{5,4},{6,7},{7,6},{8,9},{9,8},{10,11... | collective-permute-start | bytes 983048 | tf_op jit(solution)/shard_map/ppermute | solution.py:37
  20.1 13.7 %collective-permute-start.7 = (bf16[2,640,128]{2,1,0:T(8,128)(2,1)}, bf16[2,640,128]{2,1,0:T(8,128)(2,1)S(1)}, u32[]{:S(2)}, u32[]{:S(2)}) collective-permute-start(bf16[2,640,128]{2,1,0:T(8,128)(2,1)} %shard_map.123.refs_11_), channel_id=1, source_target_pairs={{0,2},{1,15},{2,4},{3,1},{4,6},{5,3},{6,8},{7,5},{8,10},{9,7},{10,... | collective-permute-start | bytes 983048 | tf_op jit(solution)/shard_map/ppermute | solution.py:37
  26.1 8.4 %collective-permute-start.4 = (bf16[1040,128]{1,0:T(8,128)(2,1)S(1)}, bf16[1040,128]{1,0:T(8,128)(2,1)S(1)}, u32[]{:S(2)}, u32[]{:S(2)}) collective-permute-start(bf16[1040,128]{1,0:T(8,128)(2,1)S(1)} %collective-permute-done.refs_4_), channel_id=1, source_target_pairs={{0,1},{1,0},{2,3},{3,2},{4,5},{5,4},{6,7},{7,6},{8,9},{9,8},{10,11... | collective-permute-start | bytes 798728 | tf_op jit(solution)/shard_map/ppermute | solution.py:37
  27.7 6.9 %collective-permute-start.5 = (bf16[1040,128]{1,0:T(8,128)(2,1)S(1)}, bf16[1040,128]{1,0:T(8,128)(2,1)S(1)}, u32[]{:S(2)}, u32[]{:S(2)}) collective-permute-start(bf16[1040,128]{1,0:T(8,128)(2,1)S(1)} %collective-permute-done.1.refs_5_), channel_id=1, source_target_pairs={{0,1},{1,0},{2,3},{3,2},{4,5},{5,4},{6,7},{7,6},{8,9},{9,8},{10,11... | collective-permute-start | bytes 798728 | tf_op jit(solution)/shard_map/ppermute | solution.py:37
  27.8 17.1 %collective-permute-start.6 = (bf16[1040,128]{1,0:T(8,128)(2,1)S(1)}, bf16[1040,128]{1,0:T(8,128)(2,1)S(1)}, u32[]{:S(2)}, u32[]{:S(2)}) collective-permute-start(bf16[1040,128]{1,0:T(8,128)(2,1)S(1)} %collective-permute-done.2.refs_6_), channel_id=1, source_target_pairs={{0,1},{1,0},{2,3},{3,2},{4,5},{5,4},{6,7},{7,6},{8,9},{9,8},{10,11... | collective-permute-start | bytes 798728 | tf_op jit(solution)/shard_map/ppermute | solution.py:37
  28.2 9.6 %collective-permute-start.11 = (bf16[2,640,128]{2,1,0:T(8,128)(2,1)S(1)}, bf16[2,640,128]{2,1,0:T(8,128)(2,1)S(1)}, u32[]{:S(2)}, u32[]{:S(2)}) collective-permute-start(bf16[2,640,128]{2,1,0:T(8,128)(2,1)S(1)} %collective-permute-done.10), channel_id=1, source_target_pairs={{0,2},{1,15},{2,4},{3,1},{4,6},{5,3},{6,8},{7,5},{8,10},{9,7},{10,... | collective-permute-start | bytes 983048 | tf_op jit(solution)/shard_map/ppermute | solution.py:37
  33.8 7.5 %collective-permute-start.8 = (bf16[2,640,128]{2,1,0:T(8,128)(2,1)S(1)}, bf16[2,640,128]{2,1,0:T(8,128)(2,1)S(1)}, u32[]{:S(2)}, u32[]{:S(2)}) collective-permute-start(bf16[2,640,128]{2,1,0:T(8,128)(2,1)S(1)} %collective-permute-done.7.refs_12_), channel_id=1, source_target_pairs={{0,2},{1,15},{2,4},{3,1},{4,6},{5,3},{6,8},{7,5},{8,10},{9,7},{10,... | collective-permute-start | bytes 983048 | tf_op jit(solution)/shard_map/ppermute | solution.py:37
  37.8 14.2 %collective-permute-start.12 = (bf16[2,640,128]{2,1,0:T(8,128)(2,1)S(1)}, bf16[2,640,128]{2,1,0:T(8,128)(2,1)S(1)}, u32[]{:S(2)}, u32[]{:S(2)}) collective-permute-start(bf16[2,640,128]{2,1,0:T(8,128)(2,1)S(1)} %collective-permute-done.11.refs_13_), channel_id=1, source_target_pairs={{0,2},{1,15},{2,4},{3,1},{4,6},{5,3},{6,8},{7,5},{8,10},{9,7},{10,... | collective-permute-start | bytes 983048 | tf_op jit(solution)/shard_map/ppermute | solution.py:37
  41.3 7.5 %collective-permute-start.9 = (bf16[2,640,128]{2,1,0:T(8,128)(2,1)S(1)}, bf16[2,640,128]{2,1,0:T(8,128)(2,1)S(1)}, u32[]{:S(2)}, u32[]{:S(2)}) collective-permute-start(bf16[2,640,128]{2,1,0:T(8,128)(2,1)S(1)} %collective-permute-done.8.refs_14_), channel_id=1, source_target_pairs={{0,2},{1,15},{2,4},{3,1},{4,6},{5,3},{6,8},{7,5},{8,10},{9,7},{10,... | collective-permute-start | bytes 983048 | tf_op jit(solution)/shard_map/ppermute | solution.py:37
  48.9 16.0 %collective-permute-start.14 = (bf16[2,640,128]{2,1,0:T(8,128)(2,1)S(1)}, bf16[2,640,128]{2,1,0:T(8,128)(2,1)S(1)}, u32[]{:S(2)}, u32[]{:S(2)}) collective-permute-start(bf16[2,640,128]{2,1,0:T(8,128)(2,1)S(1)} %collective-permute-done.9.refs_7_), channel_id=1, source_target_pairs={{0,2},{1,15},{2,4},{3,1},{4,6},{5,3},{6,8},{7,5},{8,10},{9,7},{10,... | collective-permute-start | bytes 983048 | tf_op jit(solution)/shard_map/ppermute | solution.py:37
  52.0 12.9 %collective-permute-start.13 = (bf16[2,640,128]{2,1,0:T(8,128)(2,1)S(1)}, bf16[2,640,128]{2,1,0:T(8,128)(2,1)S(1)}, u32[]{:S(2)}, u32[]{:S(2)}) collective-permute-start(bf16[2,640,128]{2,1,0:T(8,128)(2,1)S(1)} %collective-permute-done.12.refs_15_), channel_id=1, source_target_pairs={{0,2},{1,15},{2,4},{3,1},{4,6},{5,3},{6,8},{7,5},{8,10},{9,7},{10,... | collective-permute-start | bytes 983048 | tf_op jit(solution)/shard_map/ppermute | solution.py:37
  69.8 5.2 %collective-permute-start.15 = (bf16[4,2,128,128]{3,2,1,0:T(8,128)(2,1)S(1)}, bf16[4,2,128,128]{3,2,1,0:T(8,128)(2,1)S(1)}, u32[]{:S(2)}, u32[]{:S(2)}) collective-permute-start(bf16[4,2,128,128]{3,2,1,0:T(8,128)(2,1)S(1)} %get-tuple-element.12), channel_id=1, source_target_pairs={{0,1},{1,0},{2,3},{3,2},{4,5},{5,4},{6,7},{7,6},{8,9},{9,8},{10,11... | collective-permute-start | bytes 786440 | tf_op jit(solution)/shard_map/ppermute | solution.py:37
  75.2 8.1 %collective-permute-start.16 = (bf16[2,128,128]{2,1,0:T(8,128)(2,1)S(1)}, bf16[2,128,128]{2,1,0:T(8,128)(2,1)S(1)}, u32[]{:S(2)}, u32[]{:S(2)}) collective-permute-start(bf16[2,128,128]{2,1,0:T(8,128)(2,1)S(1)} %get-tuple-element.29), channel_id=1, source_target_pairs={{0,48},{1,49},{2,50},{3,51},{4,52},{5,53},{6,54},{7,55},{8,56},{9,... | collective-permute-start | bytes 196616 | tf_op jit(solution)/shard_map/ppermute | solution.py:37
  76.8 6.5 %collective-permute-start.17 = (bf16[2,128,128]{2,1,0:T(8,128)(2,1)S(1)}, bf16[2,128,128]{2,1,0:T(8,128)(2,1)S(1)}, u32[]{:S(2)}, u32[]{:S(2)}) collective-permute-start(bf16[2,128,128]{2,1,0:T(8,128)(2,1)S(1)} %get-tuple-element.31), channel_id=1, source_target_pairs={{0,32},{1,33},{2,34},{3,35},{4,36},{5,37},{6,38},{7,39},{8,40},{9,... | collective-permute-start | bytes 196616 | tf_op jit(solution)/shard_map/ppermute | solution.py:37
  79.2 4.8 %collective-permute-start.18 = (bf16[2,128,128]{2,1,0:T(8,128)(2,1)S(1)}, bf16[2,128,128]{2,1,0:T(8,128)(2,1)S(1)}, u32[]{:S(2)}, u32[]{:S(2)}) collective-permute-start(bf16[2,128,128]{2,1,0:T(8,128)(2,1)S(1)} %get-tuple-element.30), channel_id=1, source_target_pairs={{0,16},{1,17},{2,18},{3,19},{4,20},{5,21},{6,22},{7,23},{8,24},{9,... | collective-permute-start | bytes 196616 | tf_op jit(solution)/shard_map/ppermute | solution.py:37
  81.5 14.9 %copy-start.5 = (bf16[8,5,256,128]{3,2,1,0:T(8,128)(2,1)S(1)}, bf16[8,5,256,128]{3,2,1,0:T(8,128)(2,1)}, u32[]{:S(2)}) copy-start(bf16[8,5,256,128]{3,2,1,0:T(8,128)(2,1)} %copy-done.4) | copy-start | bytes 7864324
  84.2 2.0 %collective-permute-start.19 = (bf16[2,128,128]{2,1,0:T(8,128)(2,1)S(1)}, bf16[2,128,128]{2,1,0:T(8,128)(2,1)S(1)}, u32[]{:S(2)}, u32[]{:S(2)}) collective-permute-start(bf16[2,128,128]{2,1,0:T(8,128)(2,1)S(1)} %get-tuple-element.22.refs_3_), channel_id=1, source_target_pairs={{0,1},{1,0},{2,3},{3,2},{4,5},{5,4},{6,7},{7,6},{8,9},{9,8},{10,11... | collective-permute-start | bytes 196616 | tf_op jit(solution)/shard_map/ppermute | solution.py:37
  86.2 10.1 %collective-permute-start.22 = (bf16[4,128,128]{2,1,0:T(8,128)(2,1)S(1)}, bf16[4,128,128]{2,1,0:T(8,128)(2,1)S(1)}, u32[]{:S(2)}, u32[]{:S(2)}) collective-permute-start(bf16[4,128,128]{2,1,0:T(8,128)(2,1)S(1)} %pad_maximum_fusion), channel_id=1, source_target_pairs={{0,2},{1,15},{2,4},{3,1},{4,6},{5,3},{6,8},{7,5},{8,10},{9,7},{10,... | collective-permute-start | bytes 393224 | tf_op jit(solution)/shard_map/ppermute | solution.py:37
  89.2 7.2 %collective-permute-start.23 = (bf16[4,128,128]{2,1,0:T(8,128)(2,1)S(1)}, bf16[4,128,128]{2,1,0:T(8,128)(2,1)S(1)}, u32[]{:S(2)}, u32[]{:S(2)}) collective-permute-start(bf16[4,128,128]{2,1,0:T(8,128)(2,1)S(1)} %pad_maximum_fusion), channel_id=1, source_target_pairs={{0,4},{1,13},{2,6},{3,15},{4,8},{5,1},{6,10},{7,3},{8,12},{9,5},{1... | collective-permute-start | bytes 393224 | tf_op jit(solution)/shard_map/ppermute | solution.py:37
  90.7 10.0 %collective-permute-start.21 = (bf16[2,128,128]{2,1,0:T(8,128)(2,1)S(1)}, bf16[2,128,128]{2,1,0:T(8,128)(2,1)S(1)}, u32[]{:S(2)}, u32[]{:S(2)}) collective-permute-start(bf16[2,128,128]{2,1,0:T(8,128)(2,1)S(1)} %get-tuple-element.22.refs_3_), channel_id=1, source_target_pairs={{0,8},{1,9},{2,10},{3,11},{4,12},{5,13},{6,14},{7,15},{8,0},{9,1},... | collective-permute-start | bytes 196616 | tf_op jit(solution)/shard_map/ppermute | solution.py:37
  95.0 7.2 %collective-permute-start.20 = (bf16[4,128,128]{2,1,0:T(8,128)(2,1)S(1)}, bf16[4,128,128]{2,1,0:T(8,128)(2,1)S(1)}, u32[]{:S(2)}, u32[]{:S(2)}) collective-permute-start(bf16[4,128,128]{2,1,0:T(8,128)(2,1)S(1)} %pad_maximum_fusion), channel_id=1, source_target_pairs={{0,6},{1,11},{2,8},{3,13},{4,10},{5,15},{6,12},{7,1},{8,14},{9,3},... | collective-permute-start | bytes 393224 | tf_op jit(solution)/shard_map/ppermute | solution.py:37
  104.4 9.7 %collective-permute-start.24 = (bf16[4,2,128,128]{3,2,1,0:T(8,128)(2,1)S(1)}, bf16[4,2,128,128]{3,2,1,0:T(8,128)(2,1)S(1)}, u32[]{:S(2)}, u32[]{:S(2)}) collective-permute-start(bf16[4,2,128,128]{3,2,1,0:T(8,128)(2,1)S(1)} %shard_map.130), channel_id=1, source_target_pairs={{0,1},{1,0},{2,3},{3,2},{4,5},{5,4},{6,7},{7,6},{8,9},{9,8},{10,11... | collective-permute-start | bytes 786440 | tf_op jit(solution)/shard_map/ppermute | solution.py:37
  107.5 8.9 %collective-permute-start.28 = (bf16[2,128,128]{2,1,0:T(8,128)(2,1)S(1)}, bf16[2,128,128]{2,1,0:T(8,128)(2,1)S(1)}, u32[]{:S(2)}, u32[]{:S(2)}) collective-permute-start(bf16[2,128,128]{2,1,0:T(8,128)(2,1)S(1)} %get-tuple-element.22.refs_3_), channel_id=1, source_target_pairs={{0,64},{64,128},{128,192},{1,65},{65,129},{129,193},{2,66},{66,130... | collective-permute-start | bytes 196616 | tf_op jit(solution)/shard_map/ppermute | solution.py:411
  110.6 5.8 %collective-permute-start.29 = (bf16[2,128,128]{2,1,0:T(8,128)(2,1)S(1)}, bf16[2,128,128]{2,1,0:T(8,128)(2,1)S(1)}, u32[]{:S(2)}, u32[]{:S(2)}) collective-permute-start(bf16[2,128,128]{2,1,0:T(8,128)(2,1)S(1)} %get-tuple-element.22.refs_3_), channel_id=1, source_target_pairs={{64,0},{128,64},{192,128},{65,1},{129,65},{193,129},{66,2},{130,66... | collective-permute-start | bytes 196616 | tf_op jit(solution)/shard_map/ppermute | solution.py:412
  114.2 3.2 %collective-permute-start.25 = (bf16[2,128,128]{2,1,0:T(8,128)(2,1)S(1)}, bf16[2,128,128]{2,1,0:T(8,128)(2,1)S(1)}, u32[]{:S(2)}, u32[]{:S(2)}) collective-permute-start(bf16[2,128,128]{2,1,0:T(8,128)(2,1)S(1)} %get-tuple-element.26), channel_id=1, source_target_pairs={{0,48},{1,49},{2,50},{3,51},{4,52},{5,53},{6,54},{7,55},{8,56},{9,... | collective-permute-start | bytes 196616 | tf_op jit(solution)/shard_map/ppermute | solution.py:37
  115.2 4.6 %collective-permute-start.26 = (bf16[2,128,128]{2,1,0:T(8,128)(2,1)S(1)}, bf16[2,128,128]{2,1,0:T(8,128)(2,1)S(1)}, u32[]{:S(2)}, u32[]{:S(2)}) collective-permute-start(bf16[2,128,128]{2,1,0:T(8,128)(2,1)S(1)} %get-tuple-element.28), channel_id=1, source_target_pairs={{0,32},{1,33},{2,34},{3,35},{4,36},{5,37},{6,38},{7,39},{8,40},{9,... | collective-permute-start | bytes 196616 | tf_op jit(solution)/shard_map/ppermute | solution.py:37
  116.3 5.3 %collective-permute-start.27 = (bf16[2,128,128]{2,1,0:T(8,128)(2,1)S(1)}, bf16[2,128,128]{2,1,0:T(8,128)(2,1)S(1)}, u32[]{:S(2)}, u32[]{:S(2)}) collective-permute-start(bf16[2,128,128]{2,1,0:T(8,128)(2,1)S(1)} %get-tuple-element.27), channel_id=1, source_target_pairs={{0,16},{1,17},{2,18},{3,19},{4,20},{5,21},{6,22},{7,23},{8,24},{9,... | collective-permute-start | bytes 196616 | tf_op jit(solution)/shard_map/ppermute | solution.py:37
  (12 other events, 64.5 us)
Sparse Core Ops, SparseCore 0:
  19.0 26.5 all-gather.1
where the time goes:
time: 131 us; the launch traced here: 129 us
  starting transfers between devices  57.4 us (44%)
  Pallas kernels  34.7 us (26%)
  waiting for transfers between devices  15.2 us (12%)
  between operations  14.4 us (11%)
  local copies, waits for them, and re-layouts  4.55 us (3%)
  other arithmetic  2.96 us (2%)
    ppermute x28, starting transfers between devices, send(): return lax.ppermute(x, 'dev', routes(move))  52.9 us
    pallas_call x3, Pallas kernels, first_couple(): pl.pallas_call(functools.partial(first_kernel, chunks, first, count, prev...  22.6 us
    ppermute x28, waiting for transfers between devices, send(): return lax.ppermute(x, 'dev', routes(move))  15.1 us
    pallas_call x3, Pallas kernels, next_couple(): pl.pallas_call(functools.partial(next_kernel, chunks, places, first, len(...  8.63 us
    unnamed x34, local copies, waits for them, and re-layouts  4.11 us
    ppermute x1, starting transfers between devices, on_device(): below = lax.ppermute(sent, 'grp', [(0, 1), (1, 2), (2, 3)])  3.1 us
  transfers between devices with their start and end apart: 31, of which 10 were waited for; matrix products, arithmetic and copies ran while one was open for 1% of the time, Pallas kernels for 25%

commit v1 on v0

v1 whole, which is shorter than its diff:
```python
import functools

import jax
import jax.numpy as jnp
from jax import lax
from jax.experimental import pallas as pl
from jax.experimental.pallas import tpu as pltpu
from jax.sharding import PartitionSpec as P

N_Y, N_Z, N_CORE = 4, 8, 2
N_DEV = N_Y * N_Z * N_CORE
COUP_IN = 64
ROWS = 256
PLACE = ROWS + 128
LABELS = PLACE + 8
QROWS = 8 * 2 * 512
GROUPS = {1: 4, 2: 4, 3: 2, 5: 2}
W = 128
OROWS = 512
BF16 = jnp.bfloat16
F32 = jnp.float32
SMEM = pl.BlockSpec(memory_space=pltpu.SMEM)
VMEM = pl.BlockSpec(memory_space=pltpu.VMEM)
ANY = pl.BlockSpec(memory_space=pl.ANY)
PARAMS = pltpu.CompilerParams(vmem_limit_bytes=40 * 1024 * 1024)


def place(y, z, c):
    return ((y % N_Y) * N_Z + z % N_Z) * N_CORE + c


def routes(move):
    return [
        (place(y, z, c), move(y, z, c))
        for y in range(N_Y)
        for z in range(N_Z)
        for c in range(N_CORE)
    ]


def send(x, move):
    return lax.ppermute(x, "dev", routes(move))


def swap(x):
    return send(x, lambda y, z, c: place(y, z, 1 - c))


def along_z(x, k):
    return send(x, lambda y, z, c: place(y, z + k if c == 0 else z - k, c))


def along_y(x, k):
    return send(x, lambda y, z, c: place(y + k, z, c))


def cost(microseconds):
    return pl.CostEstimate(
        flops=int(microseconds * 1.15e9), bytes_accessed=1024, transcendentals=0
    )


def bundle_kernel(orb_ref, amp_ref, out_ref, amps, sems):
    copies = [pltpu.make_async_copy(amp_ref, amps, sems.at[4])]
    for q in range(2):
        for a in range(4):
            copies.append(
                pltpu.make_async_copy(
                    orb_ref.at[q, a], out_ref.at[q, pl.ds(a * W, W)], sems.at[q * 4 + a + 5]
                )
            )
    for copy in copies:
        copy.start()
    copies[0].wait()
    out_ref[:, pl.ds(OROWS, W), :] = amps[...].astype(BF16)
    for copy in copies[1:]:
        copy.wait()


def bundle(orbitals, amplitudes):
    far = pl.BlockSpec(memory_space=pltpu.HBM)
    return pl.pallas_call(
        bundle_kernel,
        out_shape=jax.ShapeDtypeStruct((2, OROWS + W, W), BF16),
        in_specs=[far, far],
        out_specs=VMEM,
        scratch_shapes=[pltpu.VMEM((2, W, W), F32), pltpu.SemaphoreType.DMA((13,))],
        compiler_params=PARAMS,
        cost_estimate=cost(1),
    )(orbitals, amplitudes)


def turned_kernel(active_ref, own_ref, fock_ref, partner_ref, out_ref, words):
    for q in range(2):
        for a in range(4):
            out_ref[pl.ds((q * 4 + a) * W, W), :] = own_ref[q, pl.ds(a * W, W), :].T
    words[...] = jnp.zeros((16, W), F32)
    slot = lax.broadcasted_iota(jnp.int32, (1, COUP_IN), 1)
    for q in range(2):
        fock = fock_ref[pl.ds(q, 1), pl.ds(0, COUP_IN)]
        fock = jnp.where(slot < active_ref[q], fock, 0.0)
        high = fock.astype(BF16).astype(F32)
        middle = (fock - high).astype(BF16).astype(F32)
        words[pl.ds(q, 1), pl.ds(0, COUP_IN)] = high
        words[pl.ds(2 + q, 1), pl.ds(0, COUP_IN)] = middle
        words[pl.ds(4 + q, 1), pl.ds(0, COUP_IN)] = fock - high - middle
        wanted = (partner_ref[pl.ds(q, 1), pl.ds(0, COUP_IN)] & 1).astype(F32)
        words[pl.ds(q, 1), pl.ds(COUP_IN, COUP_IN)] = wanted
    out_ref[pl.ds(2 * OROWS, 16), :] = words[...].astype(BF16)


def turned(active, own, fock_terms, partners):
    return pl.pallas_call(
        turned_kernel,
        out_shape=jax.ShapeDtypeStruct((2 * OROWS + 16, W), BF16),
        in_specs=[SMEM, VMEM, VMEM, VMEM],
        out_specs=VMEM,
        scratch_shapes=[pltpu.VMEM((16, W), F32)],
        compiler_params=PARAMS,
        cost_estimate=cost(1),
    )(active, own, fock_terms, partners)


def block_rows(tab_ref, base, q_id, p_id, q, zero_row, start=LABELS):
    labels = [tab_ref[start + q_id * 4 + a] for a in range(4)]
    rows = []
    for b in range(4):
        label = tab_ref[start + p_id * 4 + b]
        row = zero_row
        for a in range(4):
            row = jnp.where(labels[a] == label, base + (q * 4 + a) * W, row)
        rows.append(pl.multiple_of(row, W))
    return rows


def intersect(qbuf, rows, partner):
    left = jnp.concatenate(
        [
            jnp.concatenate([qbuf[pl.ds(row, W), :] for row in rows_q], axis=1)
            for rows_q in rows
        ],
        axis=0,
    )
    return jnp.dot(left, partner, preferred_element_type=F32).astype(BF16)


def weighted(inter, amps, w0, w1):
    half = jnp.dot(inter, amps, preferred_element_type=F32)
    return (half[:W] * w0).astype(BF16), (half[W:] * w1).astype(BF16)


def frame(halves, inters):
    return lax.dot_general(
        jnp.concatenate(halves, axis=1),
        jnp.concatenate(inters, axis=1),
        (((1,), (1,)), ((), ())),
        preferred_element_type=F32,
    )


def place_of(tab_ref):
    return [tab_ref[PLACE + k].astype(jnp.int32) for k in range(4)]


def slot_of(pos, chunk):
    step, mine = chunk
    _, y, z, c = pos
    zz = jnp.where(c == 0, z - step, z + step) & (N_Z - 1)
    lane = c if mine else 1 - c
    return (y * N_Z + zz) * N_CORE + lane


def owner_of(pos, i):
    _, y, z, c = pos
    yy = (y - (i & 3)) & (N_Y - 1)
    lane = jnp.where(i < 4, c, 1 - c)
    return (yy * N_Z + z) * N_CORE + lane


def halves_into(hbuf, at, i, tab_ref, found, amps, inter_of):
    for j, (slot, row) in enumerate(found):
        weights = [tab_ref[(i * 2 + q) * 16 + (slot & 15)] for q in range(2)]
        half = weighted(inter_of(j), amps(j, row), *weights)
        for q in range(2):
            hbuf[at, q, :, pl.ds(j * W, W)] = half[q]


def frames_into(outs, prev_ref, hbuf, at, i, inter_of, n):
    for q in range(2):
        total = frame([hbuf[at, q]], [inter_of(j, q) for j in range(n)])
        if prev_ref is not None:
            total = total + prev_ref[i, q]
        outs[0][i, q] = total
        if len(outs) == 2:
            outs[1][i & 3, q] = total.astype(BF16)


def pack_kernel(*refs):
    parts, out_ref, sems = refs[:8], refs[8], refs[9]
    copies = [
        pltpu.make_async_copy(
            parts[k].at[pl.ds(0, 2 * OROWS)],
            out_ref.at[pl.ds(k * 2 * OROWS, 2 * OROWS)],
            sems.at[k],
        )
        for k in range(8)
    ]
    for copy in copies:
        copy.start()
    out_ref[pl.ds(QROWS, W), :] = jnp.zeros((W, W), BF16)
    for copy in copies:
        copy.wait()


def pack(parts):
    return pl.pallas_call(
        pack_kernel,
        out_shape=jax.ShapeDtypeStruct((QROWS + W, W), BF16),
        in_specs=[ANY] * 8,
        out_specs=VMEM,
        scratch_shapes=[pltpu.SemaphoreType.DMA((8,))],
        compiler_params=PARAMS,
        cost_estimate=cost(1),
    )(*parts)


def wanted_rows(pos, tab_ref, chunks, i):
    found = []
    for chunk in chunks:
        slot = slot_of(pos, chunk)
        row = tab_ref[ROWS + i * 16 + (slot & 15)].astype(jnp.int32)
        found.append((slot, row))
    return found


def first_kernel(chunks, places, n_data, has_prev, n_out, group_of, *refs):
    n = len(chunks)
    tab_ref = refs[0]
    qbuf = refs[1]
    p_refs = refs[2 : 2 + n_data]
    rest = refs[2 + n_data :]
    prev_ref = rest[0] if has_prev else None
    rest = rest[1 if has_prev else 0 :]
    inter_ref, outs, (hbuf, ibuf) = rest[0], rest[1 : 1 + n_out], rest[1 + n_out :]
    pos = place_of(tab_ref)

    def intersections(i, at):
        base = pl.multiple_of(i * 2 * OROWS, 2 * OROWS)
        q_id = owner_of(pos, i) * 2
        for j, (slot, row) in enumerate(wanted_rows(pos, tab_ref, chunks, i)):
            p_id = slot * 2 + row
            rows = [block_rows(tab_ref, base, q_id + q, p_id, q, QROWS) for q in range(2)]
            inter = intersect(
                qbuf, rows, p_refs[places[j][0]][places[j][1] + row, pl.ds(0, OROWS), :]
            )
            ibuf[at, j] = inter
            inter_ref[i, j] = inter

    def halves(i, at):
        found = wanted_rows(pos, tab_ref, chunks, i)
        amps = lambda j, row: p_refs[places[j][0]][places[j][1] + row, pl.ds(OROWS, W), :]
        halves_into(hbuf, at, i, tab_ref, found, amps, lambda j: ibuf[at, j])

    def frames(i, at):
        inter_of = lambda j, q: ibuf[at, j, pl.ds(q * W, W), :]
        frames_into(outs, prev_ref, hbuf, at, i, inter_of, n)

    in_turn([intersections, halves, frames], 8, group_of, (2, 1, 0))


def in_turn(stages, count, group_of, order):
    depth, count = len(stages), count // group_of

    def tick(s, parity):
        for k in order:
            if isinstance(s, int) and not 0 <= s - k < count:
                continue
            for t in range(group_of):
                stages[k]((s - k) * group_of + t, (parity + k) % 2 * group_of + t)

    start = depth - 1 + (count - depth + 1) % 2
    for s in range(start):
        tick(s, s % 2)

    @pl.loop(0, (count - start) // 2)
    def _(pair):
        tick(start + 2 * pair, start % 2)
        tick(start + 2 * pair + 1, (start + 1) % 2)

    for s in range(count, count + depth - 1):
        tick(s, s % 2)


def out_shapes(last):
    if not last:
        return (jax.ShapeDtypeStruct((8, 2, W, W), F32),)
    return (jax.ShapeDtypeStruct((8, 2, W, W), F32), jax.ShapeDtypeStruct((4, 2, W, W), BF16))


def first_couple(table, packed, chunks, places, data, prev, last):
    n = len(chunks)
    group_of = GROUPS[n]
    shapes = out_shapes(last)
    kernel = functools.partial(
        first_kernel, chunks, places, len(data), prev is not None, len(shapes), group_of
    )
    return pl.pallas_call(
        kernel,
        out_shape=(jax.ShapeDtypeStruct((8, n, 2 * W, W), BF16),) + shapes,
        in_specs=[SMEM] + [VMEM] * (1 + len(data) + (prev is not None)),
        out_specs=(VMEM,) * (1 + len(shapes)),
        scratch_shapes=[
            pltpu.VMEM((2 * group_of, 2, W, n * W), BF16),
            pltpu.VMEM((2 * group_of, n, 2 * W, W), BF16),
        ],
        compiler_params=PARAMS,
        cost_estimate=cost(1 + 1.7 * n),
    )(table, packed, *data, *([prev] if prev is not None else []))


def next_kernel(chunks, inter_at, places, n_inter, n_amps, has_prev, n_out, group_of, *refs):
    n = len(chunks)
    tab_ref = refs[0]
    inter_refs = refs[1 : 1 + n_inter]
    amp_refs = refs[1 + n_inter : 1 + n_inter + n_amps]
    prev_ref = refs[1 + n_inter + n_amps] if has_prev else None
    outs, hbuf = refs[-1 - n_out : -1], refs[-1]
    pos = place_of(tab_ref)

    def halves(i, at):
        found = wanted_rows(pos, tab_ref, chunks, i)
        amps = lambda j, row: amp_refs[places[j][0]][places[j][1] + row]
        inter_of = lambda j: inter_refs[inter_at[j][0]][i, inter_at[j][1]]
        halves_into(hbuf, at, i, tab_ref, found, amps, inter_of)

    def frames(i, at):
        inter_of = lambda j, q: inter_refs[inter_at[j][0]][i, inter_at[j][1], pl.ds(q * W, W), :]
        frames_into(outs, prev_ref, hbuf, at, i, inter_of, n)

    in_turn([halves, frames], 8, group_of, (0, 1))


def next_couple(table, inters, chunks, inter_at, places, amps, prev, last):
    n = len(chunks)
    group_of = GROUPS[n]
    shapes = out_shapes(last)
    kernel = functools.partial(
        next_kernel,
        chunks,
        inter_at,
        places,
        len(inters),
        len(amps),
        prev is not None,
        len(shapes),
        group_of,
    )
    return pl.pallas_call(
        kernel,
        out_shape=shapes,
        in_specs=[SMEM] + [VMEM] * (len(inters) + len(amps) + (prev is not None)),
        out_specs=(VMEM,) * len(shapes),
        scratch_shapes=[pltpu.VMEM((2 * group_of, 2, W, n * W), BF16)],
        compiler_params=PARAMS,
        cost_estimate=cost(1 + n),
    )(table, *inters, *amps, *([prev] if prev is not None else []))


def cross_first_kernel(tab_ref, below_ref, above_ref, own_ref, inter_ref, out_ref, qbuf):
    qbuf[pl.ds(0, 2 * OROWS), :] = own_ref[pl.ds(0, 2 * OROWS), :]
    qbuf[pl.ds(2 * OROWS, W), :] = jnp.zeros((W, W), BF16)
    group, y, z, c = [tab_ref[k].astype(jnp.int32) for k in range(4)]
    place_here = (y * N_Z + z) * N_CORE + c
    q_id = (group * N_DEV + place_here) * 2
    halves, inters = [[], []], [[], []]
    for j in range(4):
        there = jnp.clip(group + (1 if j >= 2 else -1), 0, 3)
        p_id = (there * N_DEV + place_here) * 2 + j % 2
        rows = [block_rows(tab_ref, 0, q_id + q, p_id, q, 2 * OROWS, 16) for q in range(2)]
        near_ref = below_ref if j < 2 else above_ref
        inter = intersect(qbuf, rows, near_ref[j % 2, pl.ds(0, OROWS), :])
        inter_ref[j] = inter
        half = weighted(
            inter, near_ref[j % 2, pl.ds(OROWS, W), :], tab_ref[8 + j], tab_ref[12 + j]
        )
        for q in range(2):
            halves[q].append(half[q])
            inters[q].append(inter[q * W : (q + 1) * W])
    for q in range(2):
        out_ref[q] = frame(halves[q], inters[q])


def cross_first(table, below, above, own):
    return pl.pallas_call(
        cross_first_kernel,
        out_shape=(
            jax.ShapeDtypeStruct((4, 2 * W, W), BF16),
            jax.ShapeDtypeStruct((2, W, W), F32),
        ),
        in_specs=[SMEM] + [VMEM] * 3,
        out_specs=(VMEM, VMEM),
        scratch_shapes=[pltpu.VMEM((2 * OROWS + W, W), BF16)],
        compiler_params=PARAMS,
        cost_estimate=cost(2),
    )(table, below, above, own)


def cross_next_kernel(tab_ref, inter_ref, below_ref, above_ref, out_ref):
    halves, inters = [[], []], [[], []]
    for j in range(4):
        amps = (below_ref if j < 2 else above_ref)[j % 2]
        inter = inter_ref[j]
        half = weighted(inter, amps, tab_ref[8 + j], tab_ref[12 + j])
        for q in range(2):
            halves[q].append(half[q])
            inters[q].append(inter[q * W : (q + 1) * W])
    for q in range(2):
        out_ref[q] = frame(halves[q], inters[q])


def cross_next(table, inter, below, above):
    return pl.pallas_call(
        cross_next_kernel,
        out_shape=jax.ShapeDtypeStruct((2, W, W), F32),
        in_specs=[SMEM] + [VMEM] * 3,
        out_specs=VMEM,
        compiler_params=PARAMS,
        cost_estimate=cost(1),
    )(table, inter, below, above)


def gather_shares(mine, others):
    total = mine[:N_Y] + swap(others).astype(F32)
    shares = [send_back(total[j].astype(BF16), j) for j in range(1, N_Y)]
    return total[0] + (shares[0].astype(F32) + shares[1].astype(F32) + shares[2].astype(F32))


def send_back(x, j):
    return along_y(x, -j)


def on_device(
    orbitals,
    domains,
    partners,
    active,
    fock_terms,
    exchange_ints,
    pno_energies,
    occ_energies,
    amplitudes,
):
    group = lax.axis_index("grp")
    dev = lax.axis_index("dev")
    pos = jnp.stack([group, dev // (N_Z * N_CORE), dev // N_CORE % N_Z, dev % N_CORE])
    near_ids = ((group + jnp.array([-1, -1, 1, 1])) * N_DEV + dev) * 2 + jnp.array([0, 1, 0, 1])
    same = partners[:, None, COUP_IN:] == near_ids[None, :, None]
    cross_w = jnp.sum(jnp.where(same, fock_terms[:, None, COUP_IN:], 0.0), axis=2).reshape(8)

    mine = bundle(orbitals, amplitudes)
    other = swap(mine)
    ring_a, ring_b = [mine], [other]
    for k in range(4):
        ring_a.append(along_z(ring_a[-1], 1))
        if k < 3:
            ring_b.append(along_z(ring_b[-1], 1))
    mine_then, _ = lax.optimization_barrier((mine, other))
    turned_mine = turned(active, mine_then, fock_terms, partners)
    from_below, from_above = along_y(turned_mine, 1), along_y(turned_mine, 3)
    _, from_below, from_above = lax.optimization_barrier((ring_b[1], from_below, from_above))
    passed = jnp.where(pos[3] == 0, from_below, from_above)
    from_far = send(passed, lambda y, z, c: place(y + 1 if c == 0 else y - 1, z, c))
    _, from_far = lax.optimization_barrier((ring_b[2], from_far))
    turned_all = [turned_mine, from_below, from_far, from_above]
    turned_all = turned_all + [swap(x) for x in turned_all]
    mine_later, _ = lax.optimization_barrier((mine, ring_b[2]))
    below = lax.ppermute(mine_later, "grp", [(0, 1), (1, 2), (2, 3), (3, 0)])
    above = lax.ppermute(mine_later, "grp", [(1, 0), (2, 1), (3, 2), (0, 3)])

    words = jnp.stack([x[2 * OROWS :] for x in turned_all]).astype(F32)
    words = words[:, 0:2] + words[:, 2:4] + words[:, 4:6]
    column = pos[1] * 16
    weights = lax.dynamic_slice_in_dim(words, column, 16, 2)
    wanted = lax.dynamic_slice_in_dim(words[:, 0], COUP_IN + column, 16, 1)
    labels = domains.astype(F32)
    here = lax.dynamic_slice_in_dim(labels, group * N_DEV * 2, N_DEV * 2, 0)
    spot = jnp.concatenate([pos.astype(F32), jnp.zeros(4, F32)])
    table = jnp.concatenate([weights.reshape(-1), wanted.reshape(-1), spot, here.reshape(-1)])
    cross_table = jnp.concatenate([spot, cross_w, labels.reshape(-1)])
    packed = pack(turned_all)

    chunks_1 = [(0, True), (1, True), (1, False), (2, True), (2, False)]
    places_1 = [(0, 0), (1, 0), (2, 0), (3, 0), (4, 0)]
    chunks_2 = [(3, True), (3, False)]
    places_2 = [(0, 0), (1, 0)]
    chunks_3 = [(4, True)]

    first = functools.partial(first_couple, table, packed)
    data_1 = [mine, ring_a[1], ring_b[1], ring_a[2], ring_b[2]]
    inter_1, part = first(chunks_1, places_1, data_1, None, False)
    inter_cross, cross = cross_first(cross_table, below, above, turned_mine)
    inter_2, part = first(chunks_2, places_2, [ring_a[3], ring_b[3]], part, False)
    part, cross = lax.optimization_barrier((part, cross))
    inter_3, own, others = first(chunks_3, [(0, 0)], [ring_a[4]], part, True)

    denominator = pno_energies[:, :, None] + pno_energies[:, None, :] - occ_energies[:, None, None]
    integrals = exchange_ints.astype(F32)
    coupled = gather_shares(own, others) + cross
    residual = integrals + denominator * amplitudes - coupled
    current = amplitudes - residual / denominator

    sent = current.astype(BF16)
    both = jnp.concatenate([sent, swap(sent)], axis=0)
    steps = [along_z(both, 1), along_z(both, 2)]
    steps.append(along_z(jnp.concatenate([steps[0], steps[1][:2]], axis=0), 2))
    sent_later, _ = lax.optimization_barrier((sent, steps[1]))
    below = lax.ppermute(sent_later, "grp", [(0, 1), (1, 2), (2, 3), (3, 0)])
    above = lax.ppermute(sent_later, "grp", [(1, 0), (2, 1), (3, 2), (0, 3)])

    (part,) = next_couple(
        table,
        [inter_1],
        chunks_1,
        [(0, j) for j in range(5)],
        [(0, 0), (1, 0), (1, 2), (2, 0), (2, 2)],
        [sent, steps[0], steps[1]],
        None,
        False,
    )
    cross = cross_next(cross_table, inter_cross, below, above)
    part, cross = lax.optimization_barrier((part, cross))
    own, others = next_couple(
        table,
        [inter_2, inter_3],
        chunks_2 + chunks_3,
        [(0, 0), (0, 1), (1, 0)],
        [(0, 0), (0, 2), (0, 4)],
        [steps[2]],
        part,
        True,
    )
    coupled = gather_shares(own, others) + cross
    residual = integrals + denominator * current - coupled
    updated = current - residual / denominator
    return updated, residual


def solution(mesh):
    placed = (
        P(("grp", "dev"), None, None, None),
        P(),
        P(("grp", "dev"), None),
        P(("grp", "dev")),
        P(("grp", "dev"), None),
        P(("grp", "dev"), None, None),
        P(("grp", "dev"), None),
        P(("grp", "dev")),
        P(("grp", "dev"), None, None),
    )
    return jax.shard_map(
        on_device,
        mesh=mesh,
        in_specs=placed,
        out_specs=(P(("grp", "dev"), None, None), P(("grp", "dev"), None, None)),
        check_vma=False,
    )
```

time: 131 us -> 96.8 us (0.74); the launches traced: 129 us -> 96.5 us
  Pallas kernels: 34.7 us -> 19.7 us
  between operations: 14.4 us -> 1.02 us
  starting transfers between devices: 57.4 us -> 47.8 us
  waiting for transfers between devices: 15.2 us -> 23.3 us
  other arithmetic: 2.96 us -> 1.51 us
    pallas_call x6, Pallas kernels: 31.2 us -> 15.2 us  [the longest x3 10.8 us: first_couple(): pl.pallas_call(kernel, out_shape=(jax.ShapeDtypeStruct((8, n, 2 * W, W),...]
    ppermute x28 -> x27, starting transfers between devices: 52.9 us -> 42.8 us  [send(): return lax.ppermute(x, 'dev', routes(move))]
    ppermute x28 -> x27, waiting for transfers between devices: 15.1 us -> 23.3 us  [send(): return lax.ppermute(x, 'dev', routes(move))]
    unnamed x34 -> x31, local copies, waits for them, and re-layouts: 4.11 us -> 1.96 us
    ppermute x2 -> x4, starting transfers between devices: 4.4 us -> 5.02 us  [the longest x1 2.55 us: on_device(): above = lax.ppermute(mine_later, 'grp', [(1, 0), (2, 1), (3, 2), (0, 3)])]
  transfers between devices with their start and end apart: 31 -> 31, of which waited for: 10 -> 13; matrix products, arithmetic and copies ran while one was open for 1% -> 2% of each run, Pallas kernels for 25% -> 15%
where the time goes in v1:
time: 96.8 us; the launch traced here: 96.5 us
  starting transfers between devices  47.8 us (49%)
  waiting for transfers between devices  23.3 us (24%)
  Pallas kernels  19.7 us (20%)
  local copies, waits for them, and re-layouts  3.28 us (3%)
  other arithmetic  1.51 us (2%)
  between operations  1.02 us (1%)
    ppermute x27, starting transfers between devices, send(): return lax.ppermute(x, 'dev', routes(move))  42.8 us
    ppermute x27, waiting for transfers between devices, send(): return lax.ppermute(x, 'dev', routes(move))  23.3 us
    pallas_call x3, Pallas kernels, first_couple(): pl.pallas_call(kernel, out_shape=(jax.ShapeDtypeStruct((8, n, 2 * W, W),...  10.8 us
    pallas_call x2, Pallas kernels, next_couple(): pl.pallas_call(kernel, out_shape=shapes, in_specs=[SMEM] + [VMEM] * (len(...  4.16 us
    ppermute x1, starting transfers between devices, on_device(): above = lax.ppermute(mine_later, 'grp', [(1, 0), (2, 1), (3, 2), (0, 3)])  2.55 us
    ppermute x1, starting transfers between devices, on_device(): above = lax.ppermute(sent_later, 'grp', [(1, 0), (2, 1), (3, 2), (0, 3)])  2.47 us
    pallas_call x1, Pallas kernels, cross_first(): pl.pallas_call(cross_first_kernel, out_shape=(jax.ShapeDtypeStruct((4, 2...  2.14 us
    unnamed x31, local copies, waits for them, and re-layouts  1.96 us
  transfers between devices with their start and end apart: 31, of which 13 were waited for; matrix products, arithmetic and copies ran while one was open for 2% of the time, Pallas kernels for 15%

profile of v1, /device:TPU:1, one launch (start us, length us, event | category | flops | bytes accessed | tf_op | source)
XLA Modules:
  0.0 96.5 jit_solution(4660260519971648965)
XLA Ops:
  3.2 3.3 %collective-permute-start = (bf16[2,640,128]{2,1,0:T(8,128)(2,1)S(1)}, bf16[2,640,128]{2,1,0:T(8,128)(2,1)S(1)}, u32[]{:S(2)}, u32[]{:S(2)}) collective-permute-start(bf16[2,640,128]{2,1,0:T(8,128)(2,1)S(1)} %shard_map.122.own_ref.refs_2_), channel_id=1, source_target_pairs={{0,1},{1,0},{2,3},{3,2},{4,5},{5,4},{6,7},{7,6},{8,9},{9,8},{10,11... | collective-permute-start | bytes 983048 | tf_op jit(solution)/shard_map/ppermute | solution.py:42
  6.5 3.8 %collective-permute-start.10 = (bf16[2,640,128]{2,1,0:T(8,128)(2,1)S(1)}, bf16[2,640,128]{2,1,0:T(8,128)(2,1)S(1)}, u32[]{:S(2)}, u32[]{:S(2)}) collective-permute-start(bf16[2,640,128]{2,1,0:T(8,128)(2,1)S(1)} %shard_map.122.own_ref.refs_2_), channel_id=1, source_target_pairs={{0,2},{1,15},{2,4},{3,1},{4,6},{5,3},{6,8},{7,5},{8,10},{9,7},{10,... | collective-permute-start | bytes 983048 | tf_op jit(solution)/shard_map/ppermute | solution.py:42
  11.2 2.8 %collective-permute-start.3 = (bf16[1040,128]{1,0:T(8,128)(2,1)S(1)}, bf16[1040,128]{1,0:T(8,128)(2,1)S(1)}, u32[]{:S(2)}, u32[]{:S(2)}) collective-permute-start(bf16[1040,128]{1,0:T(8,128)(2,1)S(1)} %shard_map.123.refs_0_.own_ref), channel_id=1, source_target_pairs={{0,48},{1,49},{2,50},{3,51},{4,52},{5,53},{6,54},{7,55},{8,56},{9,... | collective-permute-start | bytes 798728 | tf_op jit(solution)/shard_map/ppermute | solution.py:42
  16.1 1.4 %collective-permute-start.11 = (bf16[2,640,128]{2,1,0:T(8,128)(2,1)S(1)}, bf16[2,640,128]{2,1,0:T(8,128)(2,1)S(1)}, u32[]{:S(2)}, u32[]{:S(2)}) collective-permute-start(bf16[2,640,128]{2,1,0:T(8,128)(2,1)S(1)} %collective-permute-done.10.refs_3_), channel_id=1, source_target_pairs={{0,2},{1,15},{2,4},{3,1},{4,6},{5,3},{6,8},{7,5},{8,10},{9,7},{10,... | collective-permute-start | bytes 983048 | tf_op jit(solution)/shard_map/ppermute | solution.py:42
  17.8 3.0 %collective-permute-done.2.refs_1_ = bf16[1040,128]{1,0:T(8,128)(2,1)S(1)} collective-permute-done((bf16[1040,128]{1,0:T(8,128)(2,1)S(1)}, bf16[1040,128]{1,0:T(8,128)(2,1)S(1)}, u32[]{:S(2)}, u32[]{:S(2)}) %collective-permute-start.2) | collective-permute-done | bytes 266272 | tf_op jit(solution)/shard_map/ppermute | solution.py:42
  20.9 2.2 %collective-permute-start.5 = (bf16[1040,128]{1,0:T(8,128)(2,1)S(1)}, bf16[1040,128]{1,0:T(8,128)(2,1)S(1)}, u32[]{:S(2)}, u32[]{:S(2)}) collective-permute-start(bf16[1040,128]{1,0:T(8,128)(2,1)S(1)} %broadcast_select_fusion), channel_id=1, source_target_pairs={{0,16},{1,49},{2,18},{3,51},{4,20},{5,53},{6,22},{7,55},{8,24},{9,... | collective-permute-start | bytes 798728 | tf_op jit(solution)/shard_map/ppermute | solution.py:42
  23.0 2.0 %collective-permute-start.4 = (bf16[2,640,128]{2,1,0:T(8,128)(2,1)S(1)}, bf16[2,640,128]{2,1,0:T(8,128)(2,1)}, u32[]{:S(2)}, u32[]{:S(2)}) collective-permute-start(bf16[2,640,128]{2,1,0:T(8,128)(2,1)S(1)} %collective-permute-done.1.refs_4_), channel_id=1, source_target_pairs={{0,2},{1,15},{2,4},{3,1},{4,6},{5,3},{6,8},{7,5},{8,10},{9,7},{10,... | collective-permute-start | bytes 983048 | tf_op jit(solution)/shard_map/ppermute | solution.py:42
  26.5 2.9 %collective-permute-start.12 = (bf16[2,640,128]{2,1,0:T(8,128)(2,1)S(1)}, bf16[2,640,128]{2,1,0:T(8,128)(2,1)}, u32[]{:S(2)}, u32[]{:S(2)}) collective-permute-start(bf16[2,640,128]{2,1,0:T(8,128)(2,1)S(1)} %collective-permute-done.11.refs_5_), channel_id=1, source_target_pairs={{0,2},{1,15},{2,4},{3,1},{4,6},{5,3},{6,8},{7,5},{8,10},{9,7},{10,... | collective-permute-start | bytes 983048 | tf_op jit(solution)/shard_map/ppermute | solution.py:42
  29.4 1.4 %collective-permute-start.8 = (bf16[1040,128]{1,0:T(8,128)(2,1)S(1)}, bf16[1040,128]{1,0:T(8,128)(2,1)S(1)}, u32[]{:S(2)}, u32[]{:S(2)}) collective-permute-start(bf16[1040,128]{1,0:T(8,128)(2,1)S(1)} %collective-permute-done.5.refs_2_), channel_id=1, source_target_pairs={{0,1},{1,0},{2,3},{3,2},{4,5},{5,4},{6,7},{7,6},{8,9},{9,8},{10,11... | collective-permute-start | bytes 798728 | tf_op jit(solution)/shard_map/ppermute | solution.py:42
  30.8 2.5 %collective-permute-start.16 = (bf16[2,640,128]{2,1,0:T(8,128)(2,1)S(1)}, bf16[2,640,128]{2,1,0:T(8,128)(2,1)}, u32[]{:S(2)}, u32[]{:S(2)}) collective-permute-start(bf16[2,640,128]{2,1,0:T(8,128)(2,1)S(1)} %shard_map.122.own_ref.refs_2_), channel_id=1, source_target_pairs={{64,0},{128,64},{192,128},{0,192},{65,1},{129,65},{193,129},{1,193... | collective-permute-start | bytes 983048 | tf_op jit(solution)/shard_map/ppermute | solution.py:478
  33.4 3.2 %collective-permute-start.14 = (bf16[2,640,128]{2,1,0:T(8,128)(2,1)}, bf16[2,640,128]{2,1,0:T(8,128)(2,1)}, u32[]{:S(2)}, u32[]{:S(2)}) collective-permute-start(bf16[2,640,128]{2,1,0:T(8,128)(2,1)} %collective-permute-done.4.refs_6_), channel_id=1, source_target_pairs={{0,2},{1,15},{2,4},{3,1},{4,6},{5,3},{6,8},{7,5},{8,10},{9,7},{10,... | collective-permute-start | bytes 983048 | tf_op jit(solution)/shard_map/ppermute | solution.py:42
  38.0 5.5 %shard_map.125 = (bf16[8,5,256,128]{3,2,1,0:T(8,128)(2,1)S(1)}, f32[8,2,128,128]{3,2,1,0:T(8,128)S(1)}) custom-call(f32[904]{0:T(1024)S(1)} %concatenate.15.refs_0_, bf16[8320,128]{1,0:T(8,128)(2,1)S(1)} %shard_map.124.refs_1_, bf16[2,640,128]{2,1,0:T(8,128)(2,1)S(1)} %shard_map.122.own_ref.refs_2_, ...), custom_call_target="tpu_custom_call" | custom-call | flops 10924999680 | bytes 1024 | tf_op jit(solution)/shard_map/pallas_call | solution.py:307
  43.6 2.9 %shard_map.126 = (bf16[8,2,256,128]{3,2,1,0:T(8,128)(2,1)S(1)}, f32[8,2,128,128]{3,2,1,0:T(8,128)S(1)}) custom-call(f32[904]{0:T(1024)S(1)} %concatenate.15.refs_0_, bf16[8320,128]{1,0:T(8,128)(2,1)S(1)} %shard_map.124.refs_1_, bf16[2,640,128]{2,1,0:T(8,128)(2,1)} %collective-permute-done.12.refs_2_, bf16[2,640,128]{2,1,0:T(8,128)(2,1)} %collective-permute-done.14.refs_3_, ...), custom_call_target="tpu_custom_call" | custom-call | flops 5059999744 | bytes 1024 | tf_op jit(solution)/shard_map/pallas_call | solution.py:307
  46.6 2.1 %shard_map.127 = (bf16[4,256,128]{2,1,0:T(8,128)(2,1)S(1)}, f32[2,128,128]{2,1,0:T(8,128)S(1)}) custom-call(f32[2064]{0:T(1024)S(1)} %concatenate.16.tab_ref, bf16[2,640,128]{2,1,0:T(8,128)(2,1)} %collective-permute-done.15.below_ref, bf16[2,640,128]{2,1,0:T(8,128)(2,1)} %collective-permute-done.16.above_ref, bf16[1040,128]{1,0:T(8,128)(2,1)S(1)} %shard_map.123.refs_0_.own_ref), custom_call_target="tpu_custom_call" | custom-call | flops 2300000000 | bytes 1024 | tf_op jit(solution)/shard_map/pallas_call | solution.py:394
  48.8 2.3 %shard_map.128 = (bf16[8,1,256,128]{3,2,1,0:T(8,128)(2,1)S(1)}, f32[8,2,128,128]{3,2,1,0:T(8,128)S(1)}, bf16[4,2,128,128]{3,2,1,0:T(8,128)(2,1)S(1)}) custom-call(f32[904]{0:T(1024)S(1)} %concatenate.15.refs_0_, bf16[8320,128]{1,0:T(8,128)(2,1)S(1)} %shard_map.124.refs_1_, bf16[2,640,128]{2,1,0:T(8,128)(2,1)} %collective-permute-done.13.refs_2_, ...), custom_call_target="tpu_custom_call" | custom-call | flops 3104999936 | bytes 1024 | tf_op jit(solution)/shard_map/pallas_call | solution.py:307
  51.1 3.4 %collective-permute-start.17 = (bf16[4,2,128,128]{3,2,1,0:T(8,128)(2,1)S(1)}, bf16[4,2,128,128]{3,2,1,0:T(8,128)(2,1)S(1)}, u32[]{:S(2)}, u32[]{:S(2)}) collective-permute-start(bf16[4,2,128,128]{3,2,1,0:T(8,128)(2,1)S(1)} %get-tuple-element.33), channel_id=1, source_target_pairs={{0,1},{1,0},{2,3},{3,2},{4,5},{5,4},{6,7},{7,6},{8,9},{9,8},{10,11... | collective-permute-start | bytes 786440 | tf_op jit(solution)/shard_map/ppermute | solution.py:42
  54.5 1.2 %collective-permute-done.17 = bf16[4,2,128,128]{3,2,1,0:T(8,128)(2,1)S(1)} collective-permute-done((bf16[4,2,128,128]{3,2,1,0:T(8,128)(2,1)S(1)}, bf16[4,2,128,128]{3,2,1,0:T(8,128)(2,1)S(1)}, u32[]{:S(2)}, u32[]{:S(2)}) %collective-permute-start.17) | collective-permute-done | bytes 262176 | tf_op jit(solution)/shard_map/ppermute | solution.py:42
  57.8 1.2 %collective-permute-done.18 = bf16[2,128,128]{2,1,0:T(8,128)(2,1)S(1)} collective-permute-done((bf16[2,128,128]{2,1,0:T(8,128)(2,1)S(1)}, bf16[2,128,128]{2,1,0:T(8,128)(2,1)S(1)}, u32[]{:S(2)}, u32[]{:S(2)}) %collective-permute-start.18) | collective-permute-done | bytes 65568 | tf_op jit(solution)/shard_map/ppermute | solution.py:42
  59.0 1.9 %collective-permute-done.20 = bf16[2,128,128]{2,1,0:T(8,128)(2,1)S(1)} collective-permute-done((bf16[2,128,128]{2,1,0:T(8,128)(2,1)S(1)}, bf16[2,128,128]{2,1,0:T(8,128)(2,1)S(1)}, u32[]{:S(2)}, u32[]{:S(2)}) %collective-permute-start.20) | collective-permute-done | bytes 65568 | tf_op jit(solution)/shard_map/ppermute | solution.py:42
  62.2 2.3 %collective-permute-start.21 = (bf16[2,128,128]{2,1,0:T(8,128)(2,1)S(1)}, bf16[2,128,128]{2,1,0:T(8,128)(2,1)S(1)}, u32[]{:S(2)}, u32[]{:S(2)}) collective-permute-start(bf16[2,128,128]{2,1,0:T(8,128)(2,1)S(1)} %get-tuple-element.39.refs_2_), channel_id=1, source_target_pairs={{0,1},{1,0},{2,3},{3,2},{4,5},{5,4},{6,7},{7,6},{8,9},{9,8},{10,11... | collective-permute-start | bytes 196616 | tf_op jit(solution)/shard_map/ppermute | solution.py:42
  65.4 2.2 %collective-permute-start.23 = (bf16[4,128,128]{2,1,0:T(8,128)(2,1)S(1)}, bf16[4,128,128]{2,1,0:T(8,128)(2,1)S(1)}, u32[]{:S(2)}, u32[]{:S(2)}) collective-permute-start(bf16[4,128,128]{2,1,0:T(8,128)(2,1)S(1)} %pad_maximum_fusion.1), channel_id=1, source_target_pairs={{0,4},{1,13},{2,6},{3,15},{4,8},{5,1},{6,10},{7,3},{8,12},{9,5},{1... | collective-permute-start | bytes 393224 | tf_op jit(solution)/shard_map/ppermute | solution.py:42
  68.2 4.0 %collective-permute-done.23.refs_4_ = bf16[4,128,128]{2,1,0:T(8,128)(2,1)S(1)} collective-permute-done((bf16[4,128,128]{2,1,0:T(8,128)(2,1)S(1)}, bf16[4,128,128]{2,1,0:T(8,128)(2,1)S(1)}, u32[]{:S(2)}, u32[]{:S(2)}) %collective-permute-start.23) | collective-permute-done | bytes 131104 | tf_op jit(solution)/shard_map/ppermute | solution.py:42
  72.2 2.5 %collective-permute-start.26 = (bf16[2,128,128]{2,1,0:T(8,128)(2,1)S(1)}, bf16[2,128,128]{2,1,0:T(8,128)(2,1)S(1)}, u32[]{:S(2)}, u32[]{:S(2)}) collective-permute-start(bf16[2,128,128]{2,1,0:T(8,128)(2,1)S(1)} %get-tuple-element.39.refs_2_), channel_id=1, source_target_pairs={{64,0},{128,64},{192,128},{0,192},{65,1},{129,65},{193,129},{1,193... | collective-permute-start | bytes 196616 | tf_op jit(solution)/shard_map/ppermute | solution.py:518
  74.7 2.4 %collective-permute-start.24 = (bf16[6,128,128]{2,1,0:T(8,128)(2,1)S(1)}, bf16[6,128,128]{2,1,0:T(8,128)(2,1)S(1)}, u32[]{:S(2)}, u32[]{:S(2)}) collective-permute-start(bf16[6,128,128]{2,1,0:T(8,128)(2,1)S(1)} %pad_maximum_fusion), channel_id=1, source_target_pairs={{0,4},{1,13},{2,6},{3,15},{4,8},{5,1},{6,10},{7,3},{8,12},{9,5},{1... | collective-permute-start | bytes 589832 | tf_op jit(solution)/shard_map/ppermute | solution.py:42
  77.2 2.4 %shard_map.129.refs_4_ = f32[8,2,128,128]{3,2,1,0:T(8,128)S(1)} custom-call(f32[904]{0:T(1024)S(1)} %concatenate.15.refs_0_, bf16[8,5,256,128]{3,2,1,0:T(8,128)(2,1)S(1)} %get-tuple-element.37.refs_1_, bf16[2,128,128]{2,1,0:T(8,128)(2,1)S(1)} %get-tuple-element.39.refs_2_, bf16[4,128,128]{2,1,0:T(8,128)(2,1)S(1)} %collective-permute-done.22.refs_3_, ...), custom_call_target="tpu_custom_call" | custom-call | flops 6899999744 | bytes 1024 | tf_op jit(solution)/shard_map/pallas_call | solution.py:358
  80.6 2.5 %collective-permute-done.24.refs_3_ = bf16[6,128,128]{2,1,0:T(8,128)(2,1)S(1)} collective-permute-done((bf16[6,128,128]{2,1,0:T(8,128)(2,1)S(1)}, bf16[6,128,128]{2,1,0:T(8,128)(2,1)S(1)}, u32[]{:S(2)}, u32[]{:S(2)}) %collective-permute-start.24) | collective-permute-done | bytes 196640 | tf_op jit(solution)/shard_map/ppermute | solution.py:42
  83.1 1.8 %shard_map.131 = (f32[8,2,128,128]{3,2,1,0:T(8,128)S(1)}, bf16[4,2,128,128]{3,2,1,0:T(8,128)(2,1)S(1)}) custom-call(f32[904]{0:T(1024)S(1)} %concatenate.15.refs_0_, bf16[8,2,256,128]{3,2,1,0:T(8,128)(2,1)S(1)} %get-tuple-element.35.refs_1_, bf16[8,1,256,128]{3,2,1,0:T(8,128)(2,1)S(1)} %get-tuple-element.36.refs_2_, ...), custom_call_target="tpu_custom_call" | custom-call | flops 4600000000 | bytes 1024 | tf_op jit(solution)/shard_map/pallas_call | solution.py:358
  84.9 1.5 %collective-permute-start.27 = (bf16[4,2,128,128]{3,2,1,0:T(8,128)(2,1)S(1)}, bf16[4,2,128,128]{3,2,1,0:T(8,128)(2,1)S(1)}, u32[]{:S(2)}, u32[]{:S(2)}) collective-permute-start(bf16[4,2,128,128]{3,2,1,0:T(8,128)(2,1)S(1)} %get-tuple-element.42), channel_id=1, source_target_pairs={{0,1},{1,0},{2,3},{3,2},{4,5},{5,4},{6,7},{7,6},{8,9},{9,8},{10,11... | collective-permute-start | bytes 786440 | tf_op jit(solution)/shard_map/ppermute | solution.py:42
  86.3 1.2 %collective-permute-done.27 = bf16[4,2,128,128]{3,2,1,0:T(8,128)(2,1)S(1)} collective-permute-done((bf16[4,2,128,128]{3,2,1,0:T(8,128)(2,1)S(1)}, bf16[4,2,128,128]{3,2,1,0:T(8,128)(2,1)S(1)}, u32[]{:S(2)}, u32[]{:S(2)}) %collective-permute-start.27) | collective-permute-done | bytes 262176 | tf_op jit(solution)/shard_map/ppermute | solution.py:42
  87.6 1.8 %collective-permute-start.28 = (bf16[2,128,128]{2,1,0:T(8,128)(2,1)S(1)}, bf16[2,128,128]{2,1,0:T(8,128)(2,1)S(1)}, u32[]{:S(2)}, u32[]{:S(2)}) collective-permute-start(bf16[2,128,128]{2,1,0:T(8,128)(2,1)S(1)} %get-tuple-element.52), channel_id=1, source_target_pairs={{0,48},{1,49},{2,50},{3,51},{4,52},{5,53},{6,54},{7,55},{8,56},{9,... | collective-permute-start | bytes 196616 | tf_op jit(solution)/shard_map/ppermute | solution.py:42
  89.4 1.3 %collective-permute-start.29 = (bf16[2,128,128]{2,1,0:T(8,128)(2,1)S(1)}, bf16[2,128,128]{2,1,0:T(8,128)(2,1)S(1)}, u32[]{:S(2)}, u32[]{:S(2)}) collective-permute-start(bf16[2,128,128]{2,1,0:T(8,128)(2,1)S(1)} %get-tuple-element.54), channel_id=1, source_target_pairs={{0,32},{1,33},{2,34},{3,35},{4,36},{5,37},{6,38},{7,39},{8,40},{9,... | collective-permute-start | bytes 196616 | tf_op jit(solution)/shard_map/ppermute | solution.py:42
  90.8 4.9 %collective-permute-done.30 = bf16[2,128,128]{2,1,0:T(8,128)(2,1)S(1)} collective-permute-done((bf16[2,128,128]{2,1,0:T(8,128)(2,1)S(1)}, bf16[2,128,128]{2,1,0:T(8,128)(2,1)S(1)}, u32[]{:S(2)}, u32[]{:S(2)}) %collective-permute-start.30) | collective-permute-done | bytes 65568 | tf_op jit(solution)/shard_map/ppermute | solution.py:42
  (104 shorter events, 15.7 us)
Async XLA Ops:
  3.2 7.3 %collective-permute-start = (bf16[2,640,128]{2,1,0:T(8,128)(2,1)S(1)}, bf16[2,640,128]{2,1,0:T(8,128)(2,1)S(1)}, u32[]{:S(2)}, u32[]{:S(2)}) collective-permute-start(bf16[2,640,128]{2,1,0:T(8,128)(2,1)S(1)} %shard_map.122.own_ref.refs_2_), channel_id=1, source_target_pairs={{0,1},{1,0},{2,3},{3,2},{4,5},{5,4},{6,7},{7,6},{8,9},{9,8},{10,11... | collective-permute-start | bytes 983048 | tf_op jit(solution)/shard_map/ppermute | solution.py:42
  6.5 9.6 %collective-permute-start.10 = (bf16[2,640,128]{2,1,0:T(8,128)(2,1)S(1)}, bf16[2,640,128]{2,1,0:T(8,128)(2,1)S(1)}, u32[]{:S(2)}, u32[]{:S(2)}) collective-permute-start(bf16[2,640,128]{2,1,0:T(8,128)(2,1)S(1)} %shard_map.122.own_ref.refs_2_), channel_id=1, source_target_pairs={{0,2},{1,15},{2,4},{3,1},{4,6},{5,3},{6,8},{7,5},{8,10},{9,7},{10,... | collective-permute-start | bytes 983048 | tf_op jit(solution)/shard_map/ppermute | solution.py:42
  11.2 6.6 %collective-permute-start.3 = (bf16[1040,128]{1,0:T(8,128)(2,1)S(1)}, bf16[1040,128]{1,0:T(8,128)(2,1)S(1)}, u32[]{:S(2)}, u32[]{:S(2)}) collective-permute-start(bf16[1040,128]{1,0:T(8,128)(2,1)S(1)} %shard_map.123.refs_0_.own_ref), channel_id=1, source_target_pairs={{0,48},{1,49},{2,50},{3,51},{4,52},{5,53},{6,54},{7,55},{8,56},{9,... | collective-permute-start | bytes 798728 | tf_op jit(solution)/shard_map/ppermute | solution.py:42
  14.0 6.8 %collective-permute-start.2 = (bf16[1040,128]{1,0:T(8,128)(2,1)S(1)}, bf16[1040,128]{1,0:T(8,128)(2,1)S(1)}, u32[]{:S(2)}, u32[]{:S(2)}) collective-permute-start(bf16[1040,128]{1,0:T(8,128)(2,1)S(1)} %shard_map.123.refs_0_.own_ref), channel_id=1, source_target_pairs={{0,16},{1,17},{2,18},{3,19},{4,20},{5,21},{6,22},{7,23},{8,24},{9,... | collective-permute-start | bytes 798728 | tf_op jit(solution)/shard_map/ppermute | solution.py:42
  14.0 6.8 %collective-permute-start.1 = (bf16[2,640,128]{2,1,0:T(8,128)(2,1)S(1)}, bf16[2,640,128]{2,1,0:T(8,128)(2,1)S(1)}, u32[]{:S(2)}, u32[]{:S(2)}) collective-permute-start(bf16[2,640,128]{2,1,0:T(8,128)(2,1)S(1)} %collective-permute-done), channel_id=1, source_target_pairs={{0,2},{1,15},{2,4},{3,1},{4,6},{5,3},{6,8},{7,5},{8,10},{9,7},{10,... | collective-permute-start | bytes 983048 | tf_op jit(solution)/shard_map/ppermute | solution.py:42
  16.1 9.5 %collective-permute-start.11 = (bf16[2,640,128]{2,1,0:T(8,128)(2,1)S(1)}, bf16[2,640,128]{2,1,0:T(8,128)(2,1)S(1)}, u32[]{:S(2)}, u32[]{:S(2)}) collective-permute-start(bf16[2,640,128]{2,1,0:T(8,128)(2,1)S(1)} %collective-permute-done.10.refs_3_), channel_id=1, source_target_pairs={{0,2},{1,15},{2,4},{3,1},{4,6},{5,3},{6,8},{7,5},{8,10},{9,7},{10,... | collective-permute-start | bytes 983048 | tf_op jit(solution)/shard_map/ppermute | solution.py:42
  20.9 5.6 %collective-permute-start.5 = (bf16[1040,128]{1,0:T(8,128)(2,1)S(1)}, bf16[1040,128]{1,0:T(8,128)(2,1)S(1)}, u32[]{:S(2)}, u32[]{:S(2)}) collective-permute-start(bf16[1040,128]{1,0:T(8,128)(2,1)S(1)} %broadcast_select_fusion), channel_id=1, source_target_pairs={{0,16},{1,49},{2,18},{3,51},{4,20},{5,53},{6,22},{7,55},{8,24},{9,... | collective-permute-start | bytes 798728 | tf_op jit(solution)/shard_map/ppermute | solution.py:42
  23.0 6.3 %collective-permute-start.4 = (bf16[2,640,128]{2,1,0:T(8,128)(2,1)S(1)}, bf16[2,640,128]{2,1,0:T(8,128)(2,1)}, u32[]{:S(2)}, u32[]{:S(2)}) collective-permute-start(bf16[2,640,128]{2,1,0:T(8,128)(2,1)S(1)} %collective-permute-done.1.refs_4_), channel_id=1, source_target_pairs={{0,2},{1,15},{2,4},{3,1},{4,6},{5,3},{6,8},{7,5},{8,10},{9,7},{10,... | collective-permute-start | bytes 983048 | tf_op jit(solution)/shard_map/ppermute | solution.py:42
  25.0 5.8 %collective-permute-start.6 = (bf16[1040,128]{1,0:T(8,128)(2,1)S(1)}, bf16[1040,128]{1,0:T(8,128)(2,1)S(1)}, u32[]{:S(2)}, u32[]{:S(2)}) collective-permute-start(bf16[1040,128]{1,0:T(8,128)(2,1)S(1)} %shard_map.123.refs_0_.own_ref), channel_id=1, source_target_pairs={{0,1},{1,0},{2,3},{3,2},{4,5},{5,4},{6,7},{7,6},{8,9},{9,8},{10,11... | collective-permute-start | bytes 798728 | tf_op jit(solution)/shard_map/ppermute | solution.py:42
  25.0 8.3 %collective-permute-start.7 = (bf16[1040,128]{1,0:T(8,128)(2,1)S(1)}, bf16[1040,128]{1,0:T(8,128)(2,1)S(1)}, u32[]{:S(2)}, u32[]{:S(2)}) collective-permute-start(bf16[1040,128]{1,0:T(8,128)(2,1)S(1)} %collective-permute-done.2.refs_1_), channel_id=1, source_target_pairs={{0,1},{1,0},{2,3},{3,2},{4,5},{5,4},{6,7},{7,6},{8,9},{9,8},{10,11... | collective-permute-start | bytes 798728 | tf_op jit(solution)/shard_map/ppermute | solution.py:42
  25.6 11.8 %collective-permute-start.9 = (bf16[1040,128]{1,0:T(8,128)(2,1)S(1)}, bf16[1040,128]{1,0:T(8,128)(2,1)S(1)}, u32[]{:S(2)}, u32[]{:S(2)}) collective-permute-start(bf16[1040,128]{1,0:T(8,128)(2,1)S(1)} %collective-permute-done.3.refs_3_), channel_id=1, source_target_pairs={{0,1},{1,0},{2,3},{3,2},{4,5},{5,4},{6,7},{7,6},{8,9},{9,8},{10,11... | collective-permute-start | bytes 798728 | tf_op jit(solution)/shard_map/ppermute | solution.py:42
  26.5 6.9 %collective-permute-start.12 = (bf16[2,640,128]{2,1,0:T(8,128)(2,1)S(1)}, bf16[2,640,128]{2,1,0:T(8,128)(2,1)}, u32[]{:S(2)}, u32[]{:S(2)}) collective-permute-start(bf16[2,640,128]{2,1,0:T(8,128)(2,1)S(1)} %collective-permute-done.11.refs_5_), channel_id=1, source_target_pairs={{0,2},{1,15},{2,4},{3,1},{4,6},{5,3},{6,8},{7,5},{8,10},{9,7},{10,... | collective-permute-start | bytes 983048 | tf_op jit(solution)/shard_map/ppermute | solution.py:42
  29.4 7.2 %collective-permute-start.8 = (bf16[1040,128]{1,0:T(8,128)(2,1)S(1)}, bf16[1040,128]{1,0:T(8,128)(2,1)S(1)}, u32[]{:S(2)}, u32[]{:S(2)}) collective-permute-start(bf16[1040,128]{1,0:T(8,128)(2,1)S(1)} %collective-permute-done.5.refs_2_), channel_id=1, source_target_pairs={{0,1},{1,0},{2,3},{3,2},{4,5},{5,4},{6,7},{7,6},{8,9},{9,8},{10,11... | collective-permute-start | bytes 798728 | tf_op jit(solution)/shard_map/ppermute | solution.py:42
  30.8 15.8 %collective-permute-start.16 = (bf16[2,640,128]{2,1,0:T(8,128)(2,1)S(1)}, bf16[2,640,128]{2,1,0:T(8,128)(2,1)}, u32[]{:S(2)}, u32[]{:S(2)}) collective-permute-start(bf16[2,640,128]{2,1,0:T(8,128)(2,1)S(1)} %shard_map.122.own_ref.refs_2_), channel_id=1, source_target_pairs={{64,0},{128,64},{192,128},{0,192},{65,1},{129,65},{193,129},{1,193... | collective-permute-start | bytes 983048 | tf_op jit(solution)/shard_map/ppermute | solution.py:478
  33.4 13.2 %collective-permute-start.15 = (bf16[2,640,128]{2,1,0:T(8,128)(2,1)S(1)}, bf16[2,640,128]{2,1,0:T(8,128)(2,1)}, u32[]{:S(2)}, u32[]{:S(2)}) collective-permute-start(bf16[2,640,128]{2,1,0:T(8,128)(2,1)S(1)} %shard_map.122.own_ref.refs_2_), channel_id=1, source_target_pairs={{0,64},{64,128},{128,192},{192,0},{1,65},{65,129},{129,193},{193,1... | collective-permute-start | bytes 983048 | tf_op jit(solution)/shard_map/ppermute | solution.py:477
  33.4 10.2 %collective-permute-start.14 = (bf16[2,640,128]{2,1,0:T(8,128)(2,1)}, bf16[2,640,128]{2,1,0:T(8,128)(2,1)}, u32[]{:S(2)}, u32[]{:S(2)}) collective-permute-start(bf16[2,640,128]{2,1,0:T(8,128)(2,1)} %collective-permute-done.4.refs_6_), channel_id=1, source_target_pairs={{0,2},{1,15},{2,4},{3,1},{4,6},{5,3},{6,8},{7,5},{8,10},{9,7},{10,... | collective-permute-start | bytes 983048 | tf_op jit(solution)/shard_map/ppermute | solution.py:42
  36.6 12.1 %collective-permute-start.13 = (bf16[2,640,128]{2,1,0:T(8,128)(2,1)}, bf16[2,640,128]{2,1,0:T(8,128)(2,1)}, u32[]{:S(2)}, u32[]{:S(2)}) collective-permute-start(bf16[2,640,128]{2,1,0:T(8,128)(2,1)} %collective-permute-done.12.refs_2_), channel_id=1, source_target_pairs={{0,2},{1,15},{2,4},{3,1},{4,6},{5,3},{6,8},{7,5},{8,10},{9,7},{10,... | collective-permute-start | bytes 983048 | tf_op jit(solution)/shard_map/ppermute | solution.py:42
  48.7 13.3 %copy-start.1 = (f32[2,128,128]{2,1,0:T(8,128)S(1)}, f32[2,128,128]{2,1,0:T(8,128)}, u32[]{:S(2)}) copy-start(f32[2,128,128]{2,1,0:T(8,128)} %amp_ref.1) | copy-start | bytes 393220
  51.1 4.6 %collective-permute-start.17 = (bf16[4,2,128,128]{3,2,1,0:T(8,128)(2,1)S(1)}, bf16[4,2,128,128]{3,2,1,0:T(8,128)(2,1)S(1)}, u32[]{:S(2)}, u32[]{:S(2)}) collective-permute-start(bf16[4,2,128,128]{3,2,1,0:T(8,128)(2,1)S(1)} %get-tuple-element.33), channel_id=1, source_target_pairs={{0,1},{1,0},{2,3},{3,2},{4,5},{5,4},{6,7},{7,6},{8,9},{9,8},{10,11... | collective-permute-start | bytes 786440 | tf_op jit(solution)/shard_map/ppermute | solution.py:42
  55.8 3.2 %collective-permute-start.18 = (bf16[2,128,128]{2,1,0:T(8,128)(2,1)S(1)}, bf16[2,128,128]{2,1,0:T(8,128)(2,1)S(1)}, u32[]{:S(2)}, u32[]{:S(2)}) collective-permute-start(bf16[2,128,128]{2,1,0:T(8,128)(2,1)S(1)} %get-tuple-element.55), channel_id=1, source_target_pairs={{0,48},{1,49},{2,50},{3,51},{4,52},{5,53},{6,54},{7,55},{8,56},{9,... | collective-permute-start | bytes 196616 | tf_op jit(solution)/shard_map/ppermute | solution.py:42
  56.5 4.3 %collective-permute-start.20 = (bf16[2,128,128]{2,1,0:T(8,128)(2,1)S(1)}, bf16[2,128,128]{2,1,0:T(8,128)(2,1)S(1)}, u32[]{:S(2)}, u32[]{:S(2)}) collective-permute-start(bf16[2,128,128]{2,1,0:T(8,128)(2,1)S(1)} %get-tuple-element.56), channel_id=1, source_target_pairs={{0,16},{1,17},{2,18},{3,19},{4,20},{5,21},{6,22},{7,23},{8,24},{9,... | collective-permute-start | bytes 196616 | tf_op jit(solution)/shard_map/ppermute | solution.py:42
  57.3 4.7 %collective-permute-start.19 = (bf16[2,128,128]{2,1,0:T(8,128)(2,1)S(1)}, bf16[2,128,128]{2,1,0:T(8,128)(2,1)S(1)}, u32[]{:S(2)}, u32[]{:S(2)}) collective-permute-start(bf16[2,128,128]{2,1,0:T(8,128)(2,1)S(1)} %get-tuple-element.57), channel_id=1, source_target_pairs={{0,32},{1,33},{2,34},{3,35},{4,36},{5,37},{6,38},{7,39},{8,40},{9,... | collective-permute-start | bytes 196616 | tf_op jit(solution)/shard_map/ppermute | solution.py:42
  62.2 3.2 %collective-permute-start.21 = (bf16[2,128,128]{2,1,0:T(8,128)(2,1)S(1)}, bf16[2,128,128]{2,1,0:T(8,128)(2,1)S(1)}, u32[]{:S(2)}, u32[]{:S(2)}) collective-permute-start(bf16[2,128,128]{2,1,0:T(8,128)(2,1)S(1)} %get-tuple-element.39.refs_2_), channel_id=1, source_target_pairs={{0,1},{1,0},{2,3},{3,2},{4,5},{5,4},{6,7},{7,6},{8,9},{9,8},{10,11... | collective-permute-start | bytes 196616 | tf_op jit(solution)/shard_map/ppermute | solution.py:42
  65.4 6.8 %collective-permute-start.23 = (bf16[4,128,128]{2,1,0:T(8,128)(2,1)S(1)}, bf16[4,128,128]{2,1,0:T(8,128)(2,1)S(1)}, u32[]{:S(2)}, u32[]{:S(2)}) collective-permute-start(bf16[4,128,128]{2,1,0:T(8,128)(2,1)S(1)} %pad_maximum_fusion.1), channel_id=1, source_target_pairs={{0,4},{1,13},{2,6},{3,15},{4,8},{5,1},{6,10},{7,3},{8,12},{9,5},{1... | collective-permute-start | bytes 393224 | tf_op jit(solution)/shard_map/ppermute | solution.py:42
  67.6 7.0 %collective-permute-start.22 = (bf16[4,128,128]{2,1,0:T(8,128)(2,1)S(1)}, bf16[4,128,128]{2,1,0:T(8,128)(2,1)S(1)}, u32[]{:S(2)}, u32[]{:S(2)}) collective-permute-start(bf16[4,128,128]{2,1,0:T(8,128)(2,1)S(1)} %pad_maximum_fusion.1), channel_id=1, source_target_pairs={{0,2},{1,15},{2,4},{3,1},{4,6},{5,3},{6,8},{7,5},{8,10},{9,7},{10,... | collective-permute-start | bytes 393224 | tf_op jit(solution)/shard_map/ppermute | solution.py:42
  72.2 7.3 %collective-permute-start.26 = (bf16[2,128,128]{2,1,0:T(8,128)(2,1)S(1)}, bf16[2,128,128]{2,1,0:T(8,128)(2,1)S(1)}, u32[]{:S(2)}, u32[]{:S(2)}) collective-permute-start(bf16[2,128,128]{2,1,0:T(8,128)(2,1)S(1)} %get-tuple-element.39.refs_2_), channel_id=1, source_target_pairs={{64,0},{128,64},{192,128},{0,192},{65,1},{129,65},{193,129},{1,193... | collective-permute-start | bytes 196616 | tf_op jit(solution)/shard_map/ppermute | solution.py:518
  74.7 4.9 %collective-permute-start.25 = (bf16[2,128,128]{2,1,0:T(8,128)(2,1)S(1)}, bf16[2,128,128]{2,1,0:T(8,128)(2,1)S(1)}, u32[]{:S(2)}, u32[]{:S(2)}) collective-permute-start(bf16[2,128,128]{2,1,0:T(8,128)(2,1)S(1)} %get-tuple-element.39.refs_2_), channel_id=1, source_target_pairs={{0,64},{64,128},{128,192},{192,0},{1,65},{65,129},{129,193},{193,1... | collective-permute-start | bytes 196616 | tf_op jit(solution)/shard_map/ppermute | solution.py:517
  74.7 8.3 %collective-permute-start.24 = (bf16[6,128,128]{2,1,0:T(8,128)(2,1)S(1)}, bf16[6,128,128]{2,1,0:T(8,128)(2,1)S(1)}, u32[]{:S(2)}, u32[]{:S(2)}) collective-permute-start(bf16[6,128,128]{2,1,0:T(8,128)(2,1)S(1)} %pad_maximum_fusion), channel_id=1, source_target_pairs={{0,4},{1,13},{2,6},{3,15},{4,8},{5,1},{6,10},{7,3},{8,12},{9,5},{1... | collective-permute-start | bytes 589832 | tf_op jit(solution)/shard_map/ppermute | solution.py:42
  84.9 2.6 %collective-permute-start.27 = (bf16[4,2,128,128]{3,2,1,0:T(8,128)(2,1)S(1)}, bf16[4,2,128,128]{3,2,1,0:T(8,128)(2,1)S(1)}, u32[]{:S(2)}, u32[]{:S(2)}) collective-permute-start(bf16[4,2,128,128]{3,2,1,0:T(8,128)(2,1)S(1)} %get-tuple-element.42), channel_id=1, source_target_pairs={{0,1},{1,0},{2,3},{3,2},{4,5},{5,4},{6,7},{7,6},{8,9},{9,8},{10,11... | collective-permute-start | bytes 786440 | tf_op jit(solution)/shard_map/ppermute | solution.py:42
  87.6 3.2 %collective-permute-start.28 = (bf16[2,128,128]{2,1,0:T(8,128)(2,1)S(1)}, bf16[2,128,128]{2,1,0:T(8,128)(2,1)S(1)}, u32[]{:S(2)}, u32[]{:S(2)}) collective-permute-start(bf16[2,128,128]{2,1,0:T(8,128)(2,1)S(1)} %get-tuple-element.52), channel_id=1, source_target_pairs={{0,48},{1,49},{2,50},{3,51},{4,52},{5,53},{6,54},{7,55},{8,56},{9,... | collective-permute-start | bytes 196616 | tf_op jit(solution)/shard_map/ppermute | solution.py:42
  89.4 6.3 %collective-permute-start.30 = (bf16[2,128,128]{2,1,0:T(8,128)(2,1)S(1)}, bf16[2,128,128]{2,1,0:T(8,128)(2,1)S(1)}, u32[]{:S(2)}, u32[]{:S(2)}) collective-permute-start(bf16[2,128,128]{2,1,0:T(8,128)(2,1)S(1)} %get-tuple-element.53), channel_id=1, source_target_pairs={{0,16},{1,17},{2,18},{3,19},{4,20},{5,21},{6,22},{7,23},{8,24},{9,... | collective-permute-start | bytes 196616 | tf_op jit(solution)/shard_map/ppermute | solution.py:42
  89.4 6.3 %collective-permute-start.29 = (bf16[2,128,128]{2,1,0:T(8,128)(2,1)S(1)}, bf16[2,128,128]{2,1,0:T(8,128)(2,1)S(1)}, u32[]{:S(2)}, u32[]{:S(2)}) collective-permute-start(bf16[2,128,128]{2,1,0:T(8,128)(2,1)S(1)} %get-tuple-element.54), channel_id=1, source_target_pairs={{0,32},{1,33},{2,34},{3,35},{4,36},{5,37},{6,38},{7,39},{8,40},{9,... | collective-permute-start | bytes 196616 | tf_op jit(solution)/shard_map/ppermute | solution.py:42
  (11 other events, 97.3 us)

commit v2 on v1

--- a/solution.py
+++ b/solution.py
@@ -14,7 +14,7 @@
 PLACE = ROWS + 128
 LABELS = PLACE + 8
 QROWS = 8 * 2 * 512
-GROUPS = {1: 4, 2: 4, 3: 2, 5: 2}
+GROUPS = {1: 4, 2: 4, 3: 2, 4: 2, 5: 2}
 W = 128
 OROWS = 512
 BF16 = jnp.bfloat16
@@ -22,7 +22,7 @@
 SMEM = pl.BlockSpec(memory_space=pltpu.SMEM)
 VMEM = pl.BlockSpec(memory_space=pltpu.VMEM)
 ANY = pl.BlockSpec(memory_space=pl.ANY)
-PARAMS = pltpu.CompilerParams(vmem_limit_bytes=40 * 1024 * 1024)
+PARAMS = pltpu.CompilerParams(vmem_limit_bytes=20 * 1024 * 1024)
 
 
 def place(y, z, c):
@@ -314,7 +314,7 @@
             pltpu.VMEM((2 * group_of, n, 2 * W, W), BF16),
         ],
         compiler_params=PARAMS,
-        cost_estimate=cost(1 + 1.7 * n),
+        cost_estimate=cost(0.8 + 0.96 * n),
     )(table, packed, *data, *([prev] if prev is not None else []))
 
 
@@ -362,7 +362,7 @@
         out_specs=(VMEM,) * len(shapes),
         scratch_shapes=[pltpu.VMEM((2 * group_of, 2, W, n * W), BF16)],
         compiler_params=PARAMS,
-        cost_estimate=cost(1 + n),
+        cost_estimate=cost(0.4 + 0.4 * n),
     )(table, *inters, *amps, *([prev] if prev is not None else []))
 
 
@@ -431,7 +431,7 @@
 
 def gather_shares(mine, others):
     total = mine[:N_Y] + swap(others).astype(F32)
-    shares = [send_back(total[j].astype(BF16), j) for j in range(1, N_Y)]
+    shares = [send_back(total[j].astype(BF16), j) for j in (2, 1, 3)]
     return total[0] + (shares[0].astype(F32) + shares[1].astype(F32) + shares[2].astype(F32))
 
 
@@ -460,22 +460,20 @@
     mine = bundle(orbitals, amplitudes)
     other = swap(mine)
     ring_a, ring_b = [mine], [other]
-    for k in range(4):
+    for _ in range(3):
         ring_a.append(along_z(ring_a[-1], 1))
-        if k < 3:
-            ring_b.append(along_z(ring_b[-1], 1))
+        ring_b.append(along_z(ring_b[-1], 1))
     mine_then, _ = lax.optimization_barrier((mine, other))
     turned_mine = turned(active, mine_then, fock_terms, partners)
     from_below, from_above = along_y(turned_mine, 1), along_y(turned_mine, 3)
     _, from_below, from_above = lax.optimization_barrier((ring_b[1], from_below, from_above))
     passed = jnp.where(pos[3] == 0, from_below, from_above)
     from_far = send(passed, lambda y, z, c: place(y + 1 if c == 0 else y - 1, z, c))
-    _, from_far = lax.optimization_barrier((ring_b[2], from_far))
+    below = lax.ppermute(mine, "grp", [(0, 1), (1, 2), (2, 3), (3, 0)])
+    above = lax.ppermute(mine, "grp", [(1, 0), (2, 1), (3, 2), (0, 3)])
+    _, below, above, from_far = lax.optimization_barrier((ring_b[2], below, above, from_far))
     turned_all = [turned_mine, from_below, from_far, from_above]
     turned_all = turned_all + [swap(x) for x in turned_all]
-    mine_later, _ = lax.optimization_barrier((mine, ring_b[2]))
-    below = lax.ppermute(mine_later, "grp", [(0, 1), (1, 2), (2, 3), (3, 0)])
-    above = lax.ppermute(mine_later, "grp", [(1, 0), (2, 1), (3, 2), (0, 3)])
 
     words = jnp.stack([x[2 * OROWS :] for x in turned_all]).astype(F32)
     words = words[:, 0:2] + words[:, 2:4] + words[:, 4:6]
@@ -498,8 +496,10 @@
     first = functools.partial(first_couple, table, packed)
     data_1 = [mine, ring_a[1], ring_b[1], ring_a[2], ring_b[2]]
     inter_1, part = first(chunks_1, places_1, data_1, None, False)
+    last_hop, part = lax.optimization_barrier((ring_a[3], part))
+    ring_a.append(along_z(last_hop, 1))
+    inter_2, part = first(chunks_2, places_2, [ring_a[3], ring_b[3]], part, False)
     inter_cross, cross = cross_first(cross_table, below, above, turned_mine)
-    inter_2, part = first(chunks_2, places_2, [ring_a[3], ring_b[3]], part, False)
     part, cross = lax.optimization_barrier((part, cross))
     inter_3, own, others = first(chunks_3, [(0, 0)], [ring_a[4]], part, True)
 
@@ -511,11 +511,9 @@
 
     sent = current.astype(BF16)
     both = jnp.concatenate([sent, swap(sent)], axis=0)
-    steps = [along_z(both, 1), along_z(both, 2)]
-    steps.append(along_z(jnp.concatenate([steps[0], steps[1][:2]], axis=0), 2))
-    sent_later, _ = lax.optimization_barrier((sent, steps[1]))
-    below = lax.ppermute(sent_later, "grp", [(0, 1), (1, 2), (2, 3), (3, 0)])
-    above = lax.ppermute(sent_later, "grp", [(1, 0), (2, 1), (3, 2), (0, 3)])
+    third, second, first_step = [along_z(both, k) for k in (3, 2, 1)]
+    steps = [first_step, second, third]
+    far = along_z(third[:2], 1)
 
     (part,) = next_couple(
         table,
@@ -527,15 +525,18 @@
         None,
         False,
     )
+    near, _ = lax.optimization_barrier((sent, third))
+    below = lax.ppermute(near, "grp", [(0, 1), (1, 2), (2, 3), (3, 0)])
+    above = lax.ppermute(near, "grp", [(1, 0), (2, 1), (3, 2), (0, 3)])
+    part, below, above = lax.optimization_barrier((part, below, above))
     cross = cross_next(cross_table, inter_cross, below, above)
-    part, cross = lax.optimization_barrier((part, cross))
     own, others = next_couple(
         table,
         [inter_2, inter_3],
         chunks_2 + chunks_3,
         [(0, 0), (0, 1), (1, 0)],
-        [(0, 0), (0, 2), (0, 4)],
-        [steps[2]],
+        [(0, 0), (0, 2), (1, 0)],
+        [steps[2], far],
         part,
         True,
     )

time: 96.8 us -> 91.8 us (0.948)
  waiting for transfers between devices: 23.3 us -> 11.4 us
  starting transfers between devices: 47.8 us -> 54.8 us
    ppermute x27 -> x28, waiting for transfers between devices: 23.3 us -> 11 us  [send(): return lax.ppermute(x, 'dev', routes(move))]
    ppermute x27 -> x28, starting transfers between devices: 42.8 us -> 50.6 us  [send(): return lax.ppermute(x, 'dev', routes(move))]
    unnamed x31 -> x35, local copies, waits for them, and re-layouts: 1.96 us -> 2.68 us
  transfers between devices with their start and end apart: 31 -> 32, of which waited for: 13 -> 14; matrix products, arithmetic and copies ran while one was open for 2% -> 2% of each run, Pallas kernels for 15% -> 16%
where the time goes in v2:
time: 91.8 us; the launch traced here: 91.6 us
  starting transfers between devices  54.8 us (60%)
  Pallas kernels  18.9 us (21%)
  waiting for transfers between devices  11.4 us (12%)
  local copies, waits for them, and re-layouts  4 us (4%)
  other arithmetic  1.48 us (2%)
  between operations  1.04 us (1%)
    ppermute x28, starting transfers between devices, send(): return lax.ppermute(x, 'dev', routes(move))  50.6 us
    ppermute x28, waiting for transfers between devices, send(): return lax.ppermute(x, 'dev', routes(move))  11 us
    pallas_call x3, Pallas kernels, first_couple(): pl.pallas_call(kernel, out_shape=(jax.ShapeDtypeStruct((8, n, 2 * W, W),...  10.5 us
    pallas_call x2, Pallas kernels, next_couple(): pl.pallas_call(kernel, out_shape=shapes, in_specs=[SMEM] + [VMEM] * (len(...  4.16 us
    unnamed x35, local copies, waits for them, and re-layouts  2.68 us
    ppermute x1, starting transfers between devices, on_device(): above = lax.ppermute(mine, 'grp', [(1, 0), (2, 1), (3, 2), (0, 3)])  2.48 us
  transfers between devices with their start and end apart: 32, of which 14 were waited for; matrix products, arithmetic and copies ran while one was open for 2% of the time, Pallas kernels for 16%

profile of v2, /device:TPU:1, one launch (start us, length us, event | category | flops | bytes accessed | tf_op | source)
XLA Modules:
  0.0 91.6 jit_solution(6589304554789596647)
XLA Ops:
  3.2 3.3 %collective-permute-start = (bf16[2,640,128]{2,1,0:T(8,128)(2,1)S(1)}, bf16[2,640,128]{2,1,0:T(8,128)(2,1)S(1)}, u32[]{:S(2)}, u32[]{:S(2)}) collective-permute-start(bf16[2,640,128]{2,1,0:T(8,128)(2,1)S(1)} %shard_map.122.own_ref.refs_2_), channel_id=1, source_target_pairs={{0,1},{1,0},{2,3},{3,2},{4,5},{5,4},{6,7},{7,6},{8,9},{9,8},{10,11... | collective-permute-start | bytes 983048 | tf_op jit(solution)/shard_map/ppermute | solution.py:42
  6.5 3.8 %collective-permute-start.12 = (bf16[2,640,128]{2,1,0:T(8,128)(2,1)S(1)}, bf16[2,640,128]{2,1,0:T(8,128)(2,1)S(1)}, u32[]{:S(2)}, u32[]{:S(2)}) collective-permute-start(bf16[2,640,128]{2,1,0:T(8,128)(2,1)S(1)} %shard_map.122.own_ref.refs_2_), channel_id=1, source_target_pairs={{0,2},{1,15},{2,4},{3,1},{4,6},{5,3},{6,8},{7,5},{8,10},{9,7},{10,... | collective-permute-start | bytes 983048 | tf_op jit(solution)/shard_map/ppermute | solution.py:42
  10.4 2.5 %collective-permute-start.6 = (bf16[2,640,128]{2,1,0:T(8,128)(2,1)S(1)}, bf16[2,640,128]{2,1,0:T(8,128)(2,1)S(1)}, u32[]{:S(2)}, u32[]{:S(2)}) collective-permute-start(bf16[2,640,128]{2,1,0:T(8,128)(2,1)S(1)} %shard_map.122.own_ref.refs_2_), channel_id=1, source_target_pairs={{64,0},{128,64},{192,128},{0,192},{65,1},{129,65},{193,129},{1,193... | collective-permute-start | bytes 983048 | tf_op jit(solution)/shard_map/ppermute | solution.py:473
  13.7 2.8 %collective-permute-start.3 = (bf16[1040,128]{1,0:T(8,128)(2,1)S(1)}, bf16[1040,128]{1,0:T(8,128)(2,1)S(1)}, u32[]{:S(2)}, u32[]{:S(2)}) collective-permute-start(bf16[1040,128]{1,0:T(8,128)(2,1)S(1)} %shard_map.123.refs_0_.own_ref), channel_id=1, source_target_pairs={{0,48},{1,49},{2,50},{3,51},{4,52},{5,53},{6,54},{7,55},{8,56},{9,... | collective-permute-start | bytes 798728 | tf_op jit(solution)/shard_map/ppermute | solution.py:42
  18.3 1.6 %collective-permute-done.3.refs_3_ = bf16[1040,128]{1,0:T(8,128)(2,1)S(1)} collective-permute-done((bf16[1040,128]{1,0:T(8,128)(2,1)S(1)}, bf16[1040,128]{1,0:T(8,128)(2,1)S(1)}, u32[]{:S(2)}, u32[]{:S(2)}) %collective-permute-start.3) | collective-permute-done | bytes 266272 | tf_op jit(solution)/shard_map/ppermute | solution.py:42
  19.9 3.4 %collective-permute-start.13 = (bf16[2,640,128]{2,1,0:T(8,128)(2,1)S(1)}, bf16[2,640,128]{2,1,0:T(8,128)(2,1)}, u32[]{:S(2)}, u32[]{:S(2)}) collective-permute-start(bf16[2,640,128]{2,1,0:T(8,128)(2,1)S(1)} %collective-permute-done.12.refs_3_), channel_id=1, source_target_pairs={{0,2},{1,15},{2,4},{3,1},{4,6},{5,3},{6,8},{7,5},{8,10},{9,7},{10,... | collective-permute-start | bytes 983048 | tf_op jit(solution)/shard_map/ppermute | solution.py:42
  23.6 3.2 %collective-permute-start.7 = (bf16[1040,128]{1,0:T(8,128)(2,1)S(1)}, bf16[1040,128]{1,0:T(8,128)(2,1)S(1)}, u32[]{:S(2)}, u32[]{:S(2)}) collective-permute-start(bf16[1040,128]{1,0:T(8,128)(2,1)S(1)} %broadcast_select_fusion), channel_id=1, source_target_pairs={{0,16},{1,49},{2,18},{3,51},{4,20},{5,53},{6,22},{7,55},{8,24},{9,... | collective-permute-start | bytes 798728 | tf_op jit(solution)/shard_map/ppermute | solution.py:42
  30.2 2.1 %collective-permute-start.14 = (bf16[2,640,128]{2,1,0:T(8,128)(2,1)}, bf16[2,640,128]{2,1,0:T(8,128)(2,1)}, u32[]{:S(2)}, u32[]{:S(2)}) collective-permute-start(bf16[2,640,128]{2,1,0:T(8,128)(2,1)} %collective-permute-done.13.refs_5_), channel_id=1, source_target_pairs={{0,2},{1,15},{2,4},{3,1},{4,6},{5,3},{6,8},{7,5},{8,10},{9,7},{10,... | collective-permute-start | bytes 983048 | tf_op jit(solution)/shard_map/ppermute | solution.py:42
  32.9 2.4 %collective-permute-start.16 = (bf16[2,640,128]{2,1,0:T(8,128)(2,1)}, bf16[2,640,128]{2,1,0:T(8,128)(2,1)}, u32[]{:S(2)}, u32[]{:S(2)}) collective-permute-start(bf16[2,640,128]{2,1,0:T(8,128)(2,1)} %collective-permute-done.4.refs_6_), channel_id=1, source_target_pairs={{0,2},{1,15},{2,4},{3,1},{4,6},{5,3},{6,8},{7,5},{8,10},{9,7},{10,... | collective-permute-start | bytes 983048 | tf_op jit(solution)/shard_map/ppermute | solution.py:42
  36.1 5.7 %shard_map.125 = (bf16[8,5,256,128]{3,2,1,0:T(8,128)(2,1)S(1)}, f32[8,2,128,128]{3,2,1,0:T(8,128)S(1)}) custom-call(f32[904]{0:T(1024)S(1)} %concatenate.12.refs_0_, bf16[8320,128]{1,0:T(8,128)(2,1)S(1)} %shard_map.124.refs_1_, bf16[2,640,128]{2,1,0:T(8,128)(2,1)S(1)} %shard_map.122.own_ref.refs_2_, ...), custom_call_target="tpu_custom_call" | custom-call | flops 6440000000 | bytes 1024 | tf_op jit(solution)/shard_map/pallas_call | solution.py:307
  41.8 1.8 %collective-permute-start.15 = (bf16[2,640,128]{2,1,0:T(8,128)(2,1)}, bf16[2,640,128]{2,1,0:T(8,128)(2,1)S(1)}, u32[]{:S(2)}, u32[]{:S(2)}) collective-permute-start(bf16[2,640,128]{2,1,0:T(8,128)(2,1)} %collective-permute-done.14.refs_2_), channel_id=1, source_target_pairs={{0,2},{1,15},{2,4},{3,1},{4,6},{5,3},{6,8},{7,5},{8,10},{9,7},{10,... | collective-permute-start | bytes 983048 | tf_op jit(solution)/shard_map/ppermute | solution.py:42
  43.6 1.7 %shard_map.127 = (bf16[4,256,128]{2,1,0:T(8,128)(2,1)S(1)}, f32[2,128,128]{2,1,0:T(8,128)S(1)}) custom-call(f32[2064]{0:T(1024)S(1)} %concatenate.13.tab_ref, bf16[2,640,128]{2,1,0:T(8,128)(2,1)S(1)} %copy-done.5, bf16[2,640,128]{2,1,0:T(8,128)(2,1)S(1)} %collective-permute-done.6.above_ref, bf16[1040,128]{1,0:T(8,128)(2,1)S(1)} %shard_map.123.refs_0_.own_ref), custom_call_target="tpu_custom_call" | custom-call | flops 2300000000 | bytes 1024 | tf_op jit(solution)/shard_map/pallas_call | solution.py:394
  45.3 2.9 %shard_map.126 = (bf16[8,2,256,128]{3,2,1,0:T(8,128)(2,1)S(1)}, f32[8,2,128,128]{3,2,1,0:T(8,128)S(1)}) custom-call(f32[904]{0:T(1024)S(1)} %concatenate.12.refs_0_, bf16[8320,128]{1,0:T(8,128)(2,1)S(1)} %shard_map.124.refs_1_, bf16[2,640,128]{2,1,0:T(8,128)(2,1)} %collective-permute-done.14.refs_2_, bf16[2,640,128]{2,1,0:T(8,128)(2,1)} %collective-permute-done.16.refs_3_, ...), custom_call_target="tpu_custom_call" | custom-call | flops 3128000000 | bytes 1024 | tf_op jit(solution)/shard_map/pallas_call | solution.py:307
  48.3 1.9 %shard_map.128 = (bf16[8,1,256,128]{3,2,1,0:T(8,128)(2,1)S(1)}, f32[8,2,128,128]{3,2,1,0:T(8,128)S(1)}, bf16[4,2,128,128]{3,2,1,0:T(8,128)(2,1)S(1)}) custom-call(f32[904]{0:T(1024)S(1)} %concatenate.12.refs_0_, bf16[8320,128]{1,0:T(8,128)(2,1)S(1)} %shard_map.124.refs_1_, bf16[2,640,128]{2,1,0:T(8,128)(2,1)S(1)} %collective-permute-done.15.refs_2_, ...), custom_call_target="tpu_custom_call" | custom-call | flops 2024000000 | bytes 1024 | tf_op jit(solution)/shard_map/pallas_call | solution.py:307
  50.2 1.3 %collective-permute-start.17 = (bf16[4,2,128,128]{3,2,1,0:T(8,128)(2,1)S(1)}, bf16[4,2,128,128]{3,2,1,0:T(8,128)(2,1)S(1)}, u32[]{:S(2)}, u32[]{:S(2)}) collective-permute-start(bf16[4,2,128,128]{3,2,1,0:T(8,128)(2,1)S(1)} %get-tuple-element.40), channel_id=1, source_target_pairs={{0,1},{1,0},{2,3},{3,2},{4,5},{5,4},{6,7},{7,6},{8,9},{9,8},{10,11... | collective-permute-start | bytes 786440 | tf_op jit(solution)/shard_map/ppermute | solution.py:42
  51.5 1.2 %collective-permute-done.17 = bf16[4,2,128,128]{3,2,1,0:T(8,128)(2,1)S(1)} collective-permute-done((bf16[4,2,128,128]{3,2,1,0:T(8,128)(2,1)S(1)}, bf16[4,2,128,128]{3,2,1,0:T(8,128)(2,1)S(1)}, u32[]{:S(2)}, u32[]{:S(2)}) %collective-permute-start.17) | collective-permute-done | bytes 262176 | tf_op jit(solution)/shard_map/ppermute | solution.py:42
  52.7 2.6 %collective-permute-start.18 = (bf16[2,128,128]{2,1,0:T(8,128)(2,1)S(1)}, bf16[2,128,128]{2,1,0:T(8,128)(2,1)S(1)}, u32[]{:S(2)}, u32[]{:S(2)}) collective-permute-start(bf16[2,128,128]{2,1,0:T(8,128)(2,1)S(1)} %get-tuple-element.63), channel_id=1, source_target_pairs={{0,32},{1,33},{2,34},{3,35},{4,36},{5,37},{6,38},{7,39},{8,40},{9,... | collective-permute-start | bytes 196616 | tf_op jit(solution)/shard_map/ppermute | solution.py:42
  55.4 1.3 %collective-permute-start.20 = (bf16[2,128,128]{2,1,0:T(8,128)(2,1)S(1)}, bf16[2,128,128]{2,1,0:T(8,128)(2,1)S(1)}, u32[]{:S(2)}, u32[]{:S(2)}) collective-permute-start(bf16[2,128,128]{2,1,0:T(8,128)(2,1)S(1)} %get-tuple-element.64), channel_id=1, source_target_pairs={{0,16},{1,17},{2,18},{3,19},{4,20},{5,21},{6,22},{7,23},{8,24},{9,... | collective-permute-start | bytes 196616 | tf_op jit(solution)/shard_map/ppermute | solution.py:42
  56.6 1.4 %collective-permute-start.19 = (bf16[2,128,128]{2,1,0:T(8,128)(2,1)S(1)}, bf16[2,128,128]{2,1,0:T(8,128)(2,1)S(1)}, u32[]{:S(2)}, u32[]{:S(2)}) collective-permute-start(bf16[2,128,128]{2,1,0:T(8,128)(2,1)S(1)} %get-tuple-element.65), channel_id=1, source_target_pairs={{0,48},{1,49},{2,50},{3,51},{4,52},{5,53},{6,54},{7,55},{8,56},{9,... | collective-permute-start | bytes 196616 | tf_op jit(solution)/shard_map/ppermute | solution.py:42
  58.0 1.6 %collective-permute-done.20 = bf16[2,128,128]{2,1,0:T(8,128)(2,1)S(1)} collective-permute-done((bf16[2,128,128]{2,1,0:T(8,128)(2,1)S(1)}, bf16[2,128,128]{2,1,0:T(8,128)(2,1)S(1)}, u32[]{:S(2)}, u32[]{:S(2)}) %collective-permute-start.20) | collective-permute-done | bytes 65568 | tf_op jit(solution)/shard_map/ppermute | solution.py:42
  60.0 2.1 %collective-permute-start.21 = (bf16[2,128,128]{2,1,0:T(8,128)(2,1)S(1)}, bf16[2,128,128]{2,1,0:T(8,128)(2,1)S(1)}, u32[]{:S(2)}, u32[]{:S(2)}) collective-permute-start(bf16[2,128,128]{2,1,0:T(8,128)(2,1)S(1)} %get-tuple-element.45.refs_2_), channel_id=1, source_target_pairs={{0,1},{1,0},{2,3},{3,2},{4,5},{5,4},{6,7},{7,6},{8,9},{9,8},{10,11... | collective-permute-start | bytes 196616 | tf_op jit(solution)/shard_map/ppermute | solution.py:42
  63.0 2.3 %collective-permute-start.22 = (bf16[4,128,128]{2,1,0:T(8,128)(2,1)S(1)}, bf16[4,128,128]{2,1,0:T(8,128)(2,1)S(1)}, u32[]{:S(2)}, u32[]{:S(2)}) collective-permute-start(bf16[4,128,128]{2,1,0:T(8,128)(2,1)S(1)} %pad_maximum_fusion), channel_id=1, source_target_pairs={{0,6},{1,11},{2,8},{3,13},{4,10},{5,15},{6,12},{7,1},{8,14},{9,3},... | collective-permute-start | bytes 393224 | tf_op jit(solution)/shard_map/ppermute | solution.py:42
  65.3 3.2 %collective-permute-start.25 = (bf16[4,128,128]{2,1,0:T(8,128)(2,1)S(1)}, bf16[4,128,128]{2,1,0:T(8,128)(2,1)S(1)}, u32[]{:S(2)}, u32[]{:S(2)}) collective-permute-start(bf16[4,128,128]{2,1,0:T(8,128)(2,1)S(1)} %pad_maximum_fusion), channel_id=1, source_target_pairs={{0,4},{1,13},{2,6},{3,15},{4,8},{5,1},{6,10},{7,3},{8,12},{9,5},{1... | collective-permute-start | bytes 393224 | tf_op jit(solution)/shard_map/ppermute | solution.py:42
  70.6 4.1 %collective-permute-start.23 = (bf16[2,128,128]{2,1,0:T(8,128)(2,1)S(1)}, bf16[2,128,128]{2,1,0:T(8,128)(2,1)S(1)}, u32[]{:S(2)}, u32[]{:S(2)}) collective-permute-start(bf16[2,128,128]{2,1,0:T(8,128)(2,1)S(1)} %slice.119), channel_id=1, source_target_pairs={{0,2},{1,15},{2,4},{3,1},{4,6},{5,3},{6,8},{7,5},{8,10},{9,7},{10,... | collective-permute-start | bytes 196616 | tf_op jit(solution)/shard_map/ppermute | solution.py:42
  74.9 2.4 %shard_map.129.refs_5_ = f32[8,2,128,128]{3,2,1,0:T(8,128)S(1)} custom-call(f32[904]{0:T(1024)S(1)} %concatenate.12.refs_0_, bf16[8,5,256,128]{3,2,1,0:T(8,128)(2,1)S(1)} %get-tuple-element.44.refs_1_, bf16[2,128,128]{2,1,0:T(8,128)(2,1)S(1)} %get-tuple-element.45.refs_2_, bf16[4,128,128]{2,1,0:T(8,128)(2,1)S(1)} %collective-permute-done.24.refs_3_, ...), custom_call_target="tpu_custom_call" | custom-call | flops 2760000000 | bytes 1024 | tf_op jit(solution)/shard_map/pallas_call | solution.py:358
  77.5 1.8 %shard_map.130 = (f32[8,2,128,128]{3,2,1,0:T(8,128)S(1)}, bf16[4,2,128,128]{3,2,1,0:T(8,128)(2,1)S(1)}) custom-call(f32[904]{0:T(1024)S(1)} %concatenate.12.refs_0_, bf16[8,2,256,128]{3,2,1,0:T(8,128)(2,1)S(1)} %get-tuple-element.42.refs_1_, bf16[8,1,256,128]{3,2,1,0:T(8,128)(2,1)S(1)} %get-tuple-element.43.refs_2_, ...), custom_call_target="tpu_custom_call" | custom-call | flops 1840000000 | bytes 1024 | tf_op jit(solution)/shard_map/pallas_call | solution.py:358
  79.3 3.7 %collective-permute-start.28 = (bf16[4,2,128,128]{3,2,1,0:T(8,128)(2,1)S(1)}, bf16[4,2,128,128]{3,2,1,0:T(8,128)(2,1)S(1)}, u32[]{:S(2)}, u32[]{:S(2)}) collective-permute-start(bf16[4,2,128,128]{3,2,1,0:T(8,128)(2,1)S(1)} %get-tuple-element.48), channel_id=1, source_target_pairs={{0,1},{1,0},{2,3},{3,2},{4,5},{5,4},{6,7},{7,6},{8,9},{9,8},{10,11... | collective-permute-start | bytes 786440 | tf_op jit(solution)/shard_map/ppermute | solution.py:42
  83.0 1.2 %collective-permute-done.28 = bf16[4,2,128,128]{3,2,1,0:T(8,128)(2,1)S(1)} collective-permute-done((bf16[4,2,128,128]{3,2,1,0:T(8,128)(2,1)S(1)}, bf16[4,2,128,128]{3,2,1,0:T(8,128)(2,1)S(1)}, u32[]{:S(2)}, u32[]{:S(2)}) %collective-permute-start.28) | collective-permute-done | bytes 262176 | tf_op jit(solution)/shard_map/ppermute | solution.py:42
  84.3 1.0 %collective-permute-start.29 = (bf16[2,128,128]{2,1,0:T(8,128)(2,1)S(1)}, bf16[2,128,128]{2,1,0:T(8,128)(2,1)S(1)}, u32[]{:S(2)}, u32[]{:S(2)}) collective-permute-start(bf16[2,128,128]{2,1,0:T(8,128)(2,1)S(1)} %get-tuple-element.60), channel_id=1, source_target_pairs={{0,32},{1,33},{2,34},{3,35},{4,36},{5,37},{6,38},{7,39},{8,40},{9,... | collective-permute-start | bytes 196616 | tf_op jit(solution)/shard_map/ppermute | solution.py:42
  85.3 2.0 %collective-permute-start.31 = (bf16[2,128,128]{2,1,0:T(8,128)(2,1)S(1)}, bf16[2,128,128]{2,1,0:T(8,128)(2,1)S(1)}, u32[]{:S(2)}, u32[]{:S(2)}) collective-permute-start(bf16[2,128,128]{2,1,0:T(8,128)(2,1)S(1)} %get-tuple-element.61), channel_id=1, source_target_pairs={{0,16},{1,17},{2,18},{3,19},{4,20},{5,21},{6,22},{7,23},{8,24},{9,... | collective-permute-start | bytes 196616 | tf_op jit(solution)/shard_map/ppermute | solution.py:42
  88.0 1.0 %shard_map.131 = f32[2,128,128]{2,1,0:T(8,128)S(1)} custom-call(f32[2064]{0:T(1024)S(1)} %concatenate.13.tab_ref, bf16[4,256,128]{2,1,0:T(8,128)(2,1)S(1)} %get-tuple-element.49.inter_ref, bf16[2,128,128]{2,1,0:T(8,128)(2,1)S(1)} %collective-permute-done.26.below_ref, bf16[2,128,128]{2,1,0:T(8,128)(2,1)S(1)} %collective-permute-done.27.above_ref), custom_call_target="tpu_custom_call" | custom-call | flops 1150000000 | bytes 1024 | tf_op jit(solution)/shard_map/pallas_call | solution.py:422
  89.0 1.8 %collective-permute-done.31 = bf16[2,128,128]{2,1,0:T(8,128)(2,1)S(1)} collective-permute-done((bf16[2,128,128]{2,1,0:T(8,128)(2,1)S(1)}, bf16[2,128,128]{2,1,0:T(8,128)(2,1)S(1)}, u32[]{:S(2)}, u32[]{:S(2)}) %collective-permute-start.31) | collective-permute-done | bytes 65568 | tf_op jit(solution)/shard_map/ppermute | solution.py:42
  (109 shorter events, 15.6 us)
Async XLA Ops:
  3.2 9.8 %collective-permute-start = (bf16[2,640,128]{2,1,0:T(8,128)(2,1)S(1)}, bf16[2,640,128]{2,1,0:T(8,128)(2,1)S(1)}, u32[]{:S(2)}, u32[]{:S(2)}) collective-permute-start(bf16[2,640,128]{2,1,0:T(8,128)(2,1)S(1)} %shard_map.122.own_ref.refs_2_), channel_id=1, source_target_pairs={{0,1},{1,0},{2,3},{3,2},{4,5},{5,4},{6,7},{7,6},{8,9},{9,8},{10,11... | collective-permute-start | bytes 983048 | tf_op jit(solution)/shard_map/ppermute | solution.py:42
  6.5 11.7 %collective-permute-start.12 = (bf16[2,640,128]{2,1,0:T(8,128)(2,1)S(1)}, bf16[2,640,128]{2,1,0:T(8,128)(2,1)S(1)}, u32[]{:S(2)}, u32[]{:S(2)}) collective-permute-start(bf16[2,640,128]{2,1,0:T(8,128)(2,1)S(1)} %shard_map.122.own_ref.refs_2_), channel_id=1, source_target_pairs={{0,2},{1,15},{2,4},{3,1},{4,6},{5,3},{6,8},{7,5},{8,10},{9,7},{10,... | collective-permute-start | bytes 983048 | tf_op jit(solution)/shard_map/ppermute | solution.py:42
  10.4 17.1 %collective-permute-start.6 = (bf16[2,640,128]{2,1,0:T(8,128)(2,1)S(1)}, bf16[2,640,128]{2,1,0:T(8,128)(2,1)S(1)}, u32[]{:S(2)}, u32[]{:S(2)}) collective-permute-start(bf16[2,640,128]{2,1,0:T(8,128)(2,1)S(1)} %shard_map.122.own_ref.refs_2_), channel_id=1, source_target_pairs={{64,0},{128,64},{192,128},{0,192},{65,1},{129,65},{193,129},{1,193... | collective-permute-start | bytes 983048 | tf_op jit(solution)/shard_map/ppermute | solution.py:473
  13.7 6.2 %collective-permute-start.3 = (bf16[1040,128]{1,0:T(8,128)(2,1)S(1)}, bf16[1040,128]{1,0:T(8,128)(2,1)S(1)}, u32[]{:S(2)}, u32[]{:S(2)}) collective-permute-start(bf16[1040,128]{1,0:T(8,128)(2,1)S(1)} %shard_map.123.refs_0_.own_ref), channel_id=1, source_target_pairs={{0,48},{1,49},{2,50},{3,51},{4,52},{5,53},{6,54},{7,55},{8,56},{9,... | collective-permute-start | bytes 798728 | tf_op jit(solution)/shard_map/ppermute | solution.py:42
  16.5 7.1 %collective-permute-start.2 = (bf16[1040,128]{1,0:T(8,128)(2,1)S(1)}, bf16[1040,128]{1,0:T(8,128)(2,1)S(1)}, u32[]{:S(2)}, u32[]{:S(2)}) collective-permute-start(bf16[1040,128]{1,0:T(8,128)(2,1)S(1)} %shard_map.123.refs_0_.own_ref), channel_id=1, source_target_pairs={{0,16},{1,17},{2,18},{3,19},{4,20},{5,21},{6,22},{7,23},{8,24},{9,... | collective-permute-start | bytes 798728 | tf_op jit(solution)/shard_map/ppermute | solution.py:42
  16.5 7.1 %collective-permute-start.1 = (bf16[2,640,128]{2,1,0:T(8,128)(2,1)S(1)}, bf16[2,640,128]{2,1,0:T(8,128)(2,1)S(1)}, u32[]{:S(2)}, u32[]{:S(2)}) collective-permute-start(bf16[2,640,128]{2,1,0:T(8,128)(2,1)S(1)} %collective-permute-done), channel_id=1, source_target_pairs={{0,2},{1,15},{2,4},{3,1},{4,6},{5,3},{6,8},{7,5},{8,10},{9,7},{10,... | collective-permute-start | bytes 983048 | tf_op jit(solution)/shard_map/ppermute | solution.py:42
  18.2 9.8 %collective-permute-start.5 = (bf16[2,640,128]{2,1,0:T(8,128)(2,1)S(1)}, bf16[2,640,128]{2,1,0:T(8,128)(2,1)S(1)}, u32[]{:S(2)}, u32[]{:S(2)}) collective-permute-start(bf16[2,640,128]{2,1,0:T(8,128)(2,1)S(1)} %shard_map.122.own_ref.refs_2_), channel_id=1, source_target_pairs={{0,64},{64,128},{128,192},{192,0},{1,65},{65,129},{129,193},{193,1... | collective-permute-start | bytes 983048 | tf_op jit(solution)/shard_map/ppermute | solution.py:472
  19.9 8.9 %collective-permute-start.13 = (bf16[2,640,128]{2,1,0:T(8,128)(2,1)S(1)}, bf16[2,640,128]{2,1,0:T(8,128)(2,1)}, u32[]{:S(2)}, u32[]{:S(2)}) collective-permute-start(bf16[2,640,128]{2,1,0:T(8,128)(2,1)S(1)} %collective-permute-done.12.refs_3_), channel_id=1, source_target_pairs={{0,2},{1,15},{2,4},{3,1},{4,6},{5,3},{6,8},{7,5},{8,10},{9,7},{10,... | collective-permute-start | bytes 983048 | tf_op jit(solution)/shard_map/ppermute | solution.py:42
  23.6 6.5 %collective-permute-start.7 = (bf16[1040,128]{1,0:T(8,128)(2,1)S(1)}, bf16[1040,128]{1,0:T(8,128)(2,1)S(1)}, u32[]{:S(2)}, u32[]{:S(2)}) collective-permute-start(bf16[1040,128]{1,0:T(8,128)(2,1)S(1)} %broadcast_select_fusion), channel_id=1, source_target_pairs={{0,16},{1,49},{2,18},{3,51},{4,20},{5,53},{6,22},{7,55},{8,24},{9,... | collective-permute-start | bytes 798728 | tf_op jit(solution)/shard_map/ppermute | solution.py:42
  26.8 6.0 %collective-permute-start.4 = (bf16[2,640,128]{2,1,0:T(8,128)(2,1)S(1)}, bf16[2,640,128]{2,1,0:T(8,128)(2,1)}, u32[]{:S(2)}, u32[]{:S(2)}) collective-permute-start(bf16[2,640,128]{2,1,0:T(8,128)(2,1)S(1)} %collective-permute-done.1.refs_4_), channel_id=1, source_target_pairs={{0,2},{1,15},{2,4},{3,1},{4,6},{5,3},{6,8},{7,5},{8,10},{9,7},{10,... | collective-permute-start | bytes 983048 | tf_op jit(solution)/shard_map/ppermute | solution.py:42
  27.5 5.5 %collective-permute-start.8 = (bf16[1040,128]{1,0:T(8,128)(2,1)S(1)}, bf16[1040,128]{1,0:T(8,128)(2,1)S(1)}, u32[]{:S(2)}, u32[]{:S(2)}) collective-permute-start(bf16[1040,128]{1,0:T(8,128)(2,1)S(1)} %shard_map.123.refs_0_.own_ref), channel_id=1, source_target_pairs={{0,1},{1,0},{2,3},{3,2},{4,5},{5,4},{6,7},{7,6},{8,9},{9,8},{10,11... | collective-permute-start | bytes 798728 | tf_op jit(solution)/shard_map/ppermute | solution.py:42
  28.7 6.6 %collective-permute-start.9 = (bf16[1040,128]{1,0:T(8,128)(2,1)S(1)}, bf16[1040,128]{1,0:T(8,128)(2,1)S(1)}, u32[]{:S(2)}, u32[]{:S(2)}) collective-permute-start(bf16[1040,128]{1,0:T(8,128)(2,1)S(1)} %collective-permute-done.2.refs_1_), channel_id=1, source_target_pairs={{0,1},{1,0},{2,3},{3,2},{4,5},{5,4},{6,7},{7,6},{8,9},{9,8},{10,11... | collective-permute-start | bytes 798728 | tf_op jit(solution)/shard_map/ppermute | solution.py:42
  28.8 6.5 %collective-permute-start.11 = (bf16[1040,128]{1,0:T(8,128)(2,1)S(1)}, bf16[1040,128]{1,0:T(8,128)(2,1)S(1)}, u32[]{:S(2)}, u32[]{:S(2)}) collective-permute-start(bf16[1040,128]{1,0:T(8,128)(2,1)S(1)} %collective-permute-done.3.refs_3_), channel_id=1, source_target_pairs={{0,1},{1,0},{2,3},{3,2},{4,5},{5,4},{6,7},{7,6},{8,9},{9,8},{10,11... | collective-permute-start | bytes 798728 | tf_op jit(solution)/shard_map/ppermute | solution.py:42
  30.2 11.6 %collective-permute-start.14 = (bf16[2,640,128]{2,1,0:T(8,128)(2,1)}, bf16[2,640,128]{2,1,0:T(8,128)(2,1)}, u32[]{:S(2)}, u32[]{:S(2)}) collective-permute-start(bf16[2,640,128]{2,1,0:T(8,128)(2,1)} %collective-permute-done.13.refs_5_), channel_id=1, source_target_pairs={{0,2},{1,15},{2,4},{3,1},{4,6},{5,3},{6,8},{7,5},{8,10},{9,7},{10,... | collective-permute-start | bytes 983048 | tf_op jit(solution)/shard_map/ppermute | solution.py:42
  32.8 2.5 %collective-permute-start.10 = (bf16[1040,128]{1,0:T(8,128)(2,1)S(1)}, bf16[1040,128]{1,0:T(8,128)(2,1)S(1)}, u32[]{:S(2)}, u32[]{:S(2)}) collective-permute-start(bf16[1040,128]{1,0:T(8,128)(2,1)S(1)} %collective-permute-done.7.refs_2_), channel_id=1, source_target_pairs={{0,1},{1,0},{2,3},{3,2},{4,5},{5,4},{6,7},{7,6},{8,9},{9,8},{10,11... | collective-permute-start | bytes 798728 | tf_op jit(solution)/shard_map/ppermute | solution.py:42
  32.9 12.4 %collective-permute-start.16 = (bf16[2,640,128]{2,1,0:T(8,128)(2,1)}, bf16[2,640,128]{2,1,0:T(8,128)(2,1)}, u32[]{:S(2)}, u32[]{:S(2)}) collective-permute-start(bf16[2,640,128]{2,1,0:T(8,128)(2,1)} %collective-permute-done.4.refs_6_), channel_id=1, source_target_pairs={{0,2},{1,15},{2,4},{3,1},{4,6},{5,3},{6,8},{7,5},{8,10},{9,7},{10,... | collective-permute-start | bytes 983048 | tf_op jit(solution)/shard_map/ppermute | solution.py:42
  41.8 6.6 %collective-permute-start.15 = (bf16[2,640,128]{2,1,0:T(8,128)(2,1)}, bf16[2,640,128]{2,1,0:T(8,128)(2,1)S(1)}, u32[]{:S(2)}, u32[]{:S(2)}) collective-permute-start(bf16[2,640,128]{2,1,0:T(8,128)(2,1)} %collective-permute-done.14.refs_2_), channel_id=1, source_target_pairs={{0,2},{1,15},{2,4},{3,1},{4,6},{5,3},{6,8},{7,5},{8,10},{9,7},{10,... | collective-permute-start | bytes 983048 | tf_op jit(solution)/shard_map/ppermute | solution.py:42
  50.2 2.4 %collective-permute-start.17 = (bf16[4,2,128,128]{3,2,1,0:T(8,128)(2,1)S(1)}, bf16[4,2,128,128]{3,2,1,0:T(8,128)(2,1)S(1)}, u32[]{:S(2)}, u32[]{:S(2)}) collective-permute-start(bf16[4,2,128,128]{3,2,1,0:T(8,128)(2,1)S(1)} %get-tuple-element.40), channel_id=1, source_target_pairs={{0,1},{1,0},{2,3},{3,2},{4,5},{5,4},{6,7},{7,6},{8,9},{9,8},{10,11... | collective-permute-start | bytes 786440 | tf_op jit(solution)/shard_map/ppermute | solution.py:42
  52.7 5.3 %collective-permute-start.18 = (bf16[2,128,128]{2,1,0:T(8,128)(2,1)S(1)}, bf16[2,128,128]{2,1,0:T(8,128)(2,1)S(1)}, u32[]{:S(2)}, u32[]{:S(2)}) collective-permute-start(bf16[2,128,128]{2,1,0:T(8,128)(2,1)S(1)} %get-tuple-element.63), channel_id=1, source_target_pairs={{0,32},{1,33},{2,34},{3,35},{4,36},{5,37},{6,38},{7,39},{8,40},{9,... | collective-permute-start | bytes 196616 | tf_op jit(solution)/shard_map/ppermute | solution.py:42
  55.4 4.3 %collective-permute-start.20 = (bf16[2,128,128]{2,1,0:T(8,128)(2,1)S(1)}, bf16[2,128,128]{2,1,0:T(8,128)(2,1)S(1)}, u32[]{:S(2)}, u32[]{:S(2)}) collective-permute-start(bf16[2,128,128]{2,1,0:T(8,128)(2,1)S(1)} %get-tuple-element.64), channel_id=1, source_target_pairs={{0,16},{1,17},{2,18},{3,19},{4,20},{5,21},{6,22},{7,23},{8,24},{9,... | collective-permute-start | bytes 196616 | tf_op jit(solution)/shard_map/ppermute | solution.py:42
  56.6 3.2 %collective-permute-start.19 = (bf16[2,128,128]{2,1,0:T(8,128)(2,1)S(1)}, bf16[2,128,128]{2,1,0:T(8,128)(2,1)S(1)}, u32[]{:S(2)}, u32[]{:S(2)}) collective-permute-start(bf16[2,128,128]{2,1,0:T(8,128)(2,1)S(1)} %get-tuple-element.65), channel_id=1, source_target_pairs={{0,48},{1,49},{2,50},{3,51},{4,52},{5,53},{6,54},{7,55},{8,56},{9,... | collective-permute-start | bytes 196616 | tf_op jit(solution)/shard_map/ppermute | solution.py:42
  60.0 3.0 %collective-permute-start.21 = (bf16[2,128,128]{2,1,0:T(8,128)(2,1)S(1)}, bf16[2,128,128]{2,1,0:T(8,128)(2,1)S(1)}, u32[]{:S(2)}, u32[]{:S(2)}) collective-permute-start(bf16[2,128,128]{2,1,0:T(8,128)(2,1)S(1)} %get-tuple-element.45.refs_2_), channel_id=1, source_target_pairs={{0,1},{1,0},{2,3},{3,2},{4,5},{5,4},{6,7},{7,6},{8,9},{9,8},{10,11... | collective-permute-start | bytes 196616 | tf_op jit(solution)/shard_map/ppermute | solution.py:42
  63.0 5.9 %collective-permute-start.22 = (bf16[4,128,128]{2,1,0:T(8,128)(2,1)S(1)}, bf16[4,128,128]{2,1,0:T(8,128)(2,1)S(1)}, u32[]{:S(2)}, u32[]{:S(2)}) collective-permute-start(bf16[4,128,128]{2,1,0:T(8,128)(2,1)S(1)} %pad_maximum_fusion), channel_id=1, source_target_pairs={{0,6},{1,11},{2,8},{3,13},{4,10},{5,15},{6,12},{7,1},{8,14},{9,3},... | collective-permute-start | bytes 393224 | tf_op jit(solution)/shard_map/ppermute | solution.py:42
  65.3 9.4 %collective-permute-start.25 = (bf16[4,128,128]{2,1,0:T(8,128)(2,1)S(1)}, bf16[4,128,128]{2,1,0:T(8,128)(2,1)S(1)}, u32[]{:S(2)}, u32[]{:S(2)}) collective-permute-start(bf16[4,128,128]{2,1,0:T(8,128)(2,1)S(1)} %pad_maximum_fusion), channel_id=1, source_target_pairs={{0,4},{1,13},{2,6},{3,15},{4,8},{5,1},{6,10},{7,3},{8,12},{9,5},{1... | collective-permute-start | bytes 393224 | tf_op jit(solution)/shard_map/ppermute | solution.py:42
  68.5 6.4 %collective-permute-start.24 = (bf16[4,128,128]{2,1,0:T(8,128)(2,1)S(1)}, bf16[4,128,128]{2,1,0:T(8,128)(2,1)S(1)}, u32[]{:S(2)}, u32[]{:S(2)}) collective-permute-start(bf16[4,128,128]{2,1,0:T(8,128)(2,1)S(1)} %pad_maximum_fusion), channel_id=1, source_target_pairs={{0,2},{1,15},{2,4},{3,1},{4,6},{5,3},{6,8},{7,5},{8,10},{9,7},{10,... | collective-permute-start | bytes 393224 | tf_op jit(solution)/shard_map/ppermute | solution.py:42
  68.9 8.4 %collective-permute-start.27 = (bf16[2,128,128]{2,1,0:T(8,128)(2,1)S(1)}, bf16[2,128,128]{2,1,0:T(8,128)(2,1)S(1)}, u32[]{:S(2)}, u32[]{:S(2)}) collective-permute-start(bf16[2,128,128]{2,1,0:T(8,128)(2,1)S(1)} %get-tuple-element.45.refs_2_), channel_id=1, source_target_pairs={{64,0},{128,64},{192,128},{0,192},{65,1},{129,65},{193,129},{1,193... | collective-permute-start | bytes 196616 | tf_op jit(solution)/shard_map/ppermute | solution.py:530
  69.6 7.8 %collective-permute-start.26 = (bf16[2,128,128]{2,1,0:T(8,128)(2,1)S(1)}, bf16[2,128,128]{2,1,0:T(8,128)(2,1)S(1)}, u32[]{:S(2)}, u32[]{:S(2)}) collective-permute-start(bf16[2,128,128]{2,1,0:T(8,128)(2,1)S(1)} %get-tuple-element.45.refs_2_), channel_id=1, source_target_pairs={{0,64},{64,128},{128,192},{192,0},{1,65},{65,129},{129,193},{193,1... | collective-permute-start | bytes 196616 | tf_op jit(solution)/shard_map/ppermute | solution.py:529
  70.6 6.9 %collective-permute-start.23 = (bf16[2,128,128]{2,1,0:T(8,128)(2,1)S(1)}, bf16[2,128,128]{2,1,0:T(8,128)(2,1)S(1)}, u32[]{:S(2)}, u32[]{:S(2)}) collective-permute-start(bf16[2,128,128]{2,1,0:T(8,128)(2,1)S(1)} %slice.119), channel_id=1, source_target_pairs={{0,2},{1,15},{2,4},{3,1},{4,6},{5,3},{6,8},{7,5},{8,10},{9,7},{10,... | collective-permute-start | bytes 196616 | tf_op jit(solution)/shard_map/ppermute | solution.py:42
  79.3 4.9 %collective-permute-start.28 = (bf16[4,2,128,128]{3,2,1,0:T(8,128)(2,1)S(1)}, bf16[4,2,128,128]{3,2,1,0:T(8,128)(2,1)S(1)}, u32[]{:S(2)}, u32[]{:S(2)}) collective-permute-start(bf16[4,2,128,128]{3,2,1,0:T(8,128)(2,1)S(1)} %get-tuple-element.48), channel_id=1, source_target_pairs={{0,1},{1,0},{2,3},{3,2},{4,5},{5,4},{6,7},{7,6},{8,9},{9,8},{10,11... | collective-permute-start | bytes 786440 | tf_op jit(solution)/shard_map/ppermute | solution.py:42
  84.3 4.7 %collective-permute-start.29 = (bf16[2,128,128]{2,1,0:T(8,128)(2,1)S(1)}, bf16[2,128,128]{2,1,0:T(8,128)(2,1)S(1)}, u32[]{:S(2)}, u32[]{:S(2)}) collective-permute-start(bf16[2,128,128]{2,1,0:T(8,128)(2,1)S(1)} %get-tuple-element.60), channel_id=1, source_target_pairs={{0,32},{1,33},{2,34},{3,35},{4,36},{5,37},{6,38},{7,39},{8,40},{9,... | collective-permute-start | bytes 196616 | tf_op jit(solution)/shard_map/ppermute | solution.py:42
  85.3 5.5 %collective-permute-start.31 = (bf16[2,128,128]{2,1,0:T(8,128)(2,1)S(1)}, bf16[2,128,128]{2,1,0:T(8,128)(2,1)S(1)}, u32[]{:S(2)}, u32[]{:S(2)}) collective-permute-start(bf16[2,128,128]{2,1,0:T(8,128)(2,1)S(1)} %get-tuple-element.61), channel_id=1, source_target_pairs={{0,16},{1,17},{2,18},{3,19},{4,20},{5,21},{6,22},{7,23},{8,24},{9,... | collective-permute-start | bytes 196616 | tf_op jit(solution)/shard_map/ppermute | solution.py:42
  87.3 3.5 %collective-permute-start.30 = (bf16[2,128,128]{2,1,0:T(8,128)(2,1)S(1)}, bf16[2,128,128]{2,1,0:T(8,128)(2,1)S(1)}, u32[]{:S(2)}, u32[]{:S(2)}) collective-permute-start(bf16[2,128,128]{2,1,0:T(8,128)(2,1)S(1)} %get-tuple-element.62), channel_id=1, source_target_pairs={{0,48},{1,49},{2,50},{3,51},{4,52},{5,53},{6,54},{7,55},{8,56},{9,... | collective-permute-start | bytes 196616 | tf_op jit(solution)/shard_map/ppermute | solution.py:42
  (14 other events, 126.4 us)

commit v3 on v2

--- a/solution.py
+++ b/solution.py
@@ -185,14 +185,12 @@
             hbuf[at, q, :, pl.ds(j * W, W)] = half[q]
 
 
-def frames_into(outs, prev_ref, hbuf, at, i, inter_of, n):
+def frames_into(out_ref, prev_ref, hbuf, at, i, t, inter_of, n):
     for q in range(2):
         total = frame([hbuf[at, q]], [inter_of(j, q) for j in range(n)])
         if prev_ref is not None:
             total = total + prev_ref[i, q]
-        outs[0][i, q] = total
-        if len(outs) == 2:
-            outs[1][i & 3, q] = total.astype(BF16)
+        out_ref[t, q] = total.astype(out_ref.dtype)
 
 
 def pack_kernel(*refs):
@@ -233,7 +231,7 @@
     return found
 
 
-def first_kernel(chunks, places, n_data, has_prev, n_out, group_of, *refs):
+def first_kernel(chunks, places, n_data, has_prev, span, group_of, *refs):
     n = len(chunks)
     tab_ref = refs[0]
     qbuf = refs[1]
@@ -241,10 +239,12 @@
     rest = refs[2 + n_data :]
     prev_ref = rest[0] if has_prev else None
     rest = rest[1 if has_prev else 0 :]
-    inter_ref, outs, (hbuf, ibuf) = rest[0], rest[1 : 1 + n_out], rest[1 + n_out :]
+    inter_ref, out_ref, hbuf, ibuf = rest
+    begin, count = span
     pos = place_of(tab_ref)
 
-    def intersections(i, at):
+    def intersections(t, at):
+        i = t + begin
         base = pl.multiple_of(i * 2 * OROWS, 2 * OROWS)
         q_id = owner_of(pos, i) * 2
         for j, (slot, row) in enumerate(wanted_rows(pos, tab_ref, chunks, i)):
@@ -254,18 +254,18 @@
                 qbuf, rows, p_refs[places[j][0]][places[j][1] + row, pl.ds(0, OROWS), :]
             )
             ibuf[at, j] = inter
-            inter_ref[i, j] = inter
-
-    def halves(i, at):
-        found = wanted_rows(pos, tab_ref, chunks, i)
+            inter_ref[t, j] = inter
+
+    def halves(t, at):
+        found = wanted_rows(pos, tab_ref, chunks, t + begin)
         amps = lambda j, row: p_refs[places[j][0]][places[j][1] + row, pl.ds(OROWS, W), :]
-        halves_into(hbuf, at, i, tab_ref, found, amps, lambda j: ibuf[at, j])
-
-    def frames(i, at):
+        halves_into(hbuf, at, t + begin, tab_ref, found, amps, lambda j: ibuf[at, j])
+
+    def frames(t, at):
         inter_of = lambda j, q: ibuf[at, j, pl.ds(q * W, W), :]
-        frames_into(outs, prev_ref, hbuf, at, i, inter_of, n)
-
-    in_turn([intersections, halves, frames], 8, group_of, (2, 1, 0))
+        frames_into(out_ref, prev_ref, hbuf, at, t + begin, t, inter_of, n)
+
+    in_turn([intersections, halves, frames], count, group_of, (2, 1, 0))
 
 
 def in_turn(stages, count, group_of, order):
@@ -291,59 +291,62 @@
         tick(s, s % 2)
 
 
-def out_shapes(last):
-    if not last:
-        return (jax.ShapeDtypeStruct((8, 2, W, W), F32),)
-    return (jax.ShapeDtypeStruct((8, 2, W, W), F32), jax.ShapeDtypeStruct((4, 2, W, W), BF16))
-
-
-def first_couple(table, packed, chunks, places, data, prev, last):
-    n = len(chunks)
-    group_of = GROUPS[n]
-    shapes = out_shapes(last)
+def first_couple(table, packed, chunks, places, data, prev, span=(0, 8), out_type=F32):
+    n, count = len(chunks), span[1]
+    group_of = min(GROUPS[n], count // 2)
     kernel = functools.partial(
-        first_kernel, chunks, places, len(data), prev is not None, len(shapes), group_of
+        first_kernel, chunks, places, len(data), prev is not None, span, group_of
     )
     return pl.pallas_call(
         kernel,
-        out_shape=(jax.ShapeDtypeStruct((8, n, 2 * W, W), BF16),) + shapes,
+        out_shape=(
+            jax.ShapeDtypeStruct((count, n, 2 * W, W), BF16),
+            jax.ShapeDtypeStruct((count, 2, W, W), out_type),
+        ),
         in_specs=[SMEM] + [VMEM] * (1 + len(data) + (prev is not None)),
-        out_specs=(VMEM,) * (1 + len(shapes)),
+        out_specs=(VMEM, VMEM),
         scratch_shapes=[
             pltpu.VMEM((2 * group_of, 2, W, n * W), BF16),
             pltpu.VMEM((2 * group_of, n, 2 * W, W), BF16),
         ],
         compiler_params=PARAMS,
-        cost_estimate=cost(0.8 + 0.96 * n),
+        cost_estimate=cost((0.8 + 0.96 * n) * (0.3 + 0.7 * count / 8)),
     )(table, packed, *data, *([prev] if prev is not None else []))
 
 
-def next_kernel(chunks, inter_at, places, n_inter, n_amps, has_prev, n_out, group_of, *refs):
+def next_kernel(chunks, inter_at, places, n_inter, n_amps, has_prev, span, group_of, *refs):
     n = len(chunks)
+    begin, count = span
     tab_ref = refs[0]
     inter_refs = refs[1 : 1 + n_inter]
     amp_refs = refs[1 + n_inter : 1 + n_inter + n_amps]
     prev_ref = refs[1 + n_inter + n_amps] if has_prev else None
-    outs, hbuf = refs[-1 - n_out : -1], refs[-1]
+    out_ref, hbuf = refs[-2:]
     pos = place_of(tab_ref)
 
-    def halves(i, at):
-        found = wanted_rows(pos, tab_ref, chunks, i)
+    def inter_row(j, t):
+        ref = inter_refs[inter_at[j][0]]
+        return ref.at[t + begin if ref.shape[0] == 8 else t, inter_at[j][1]]
+
+    def halves(t, at):
+        found = wanted_rows(pos, tab_ref, chunks, t + begin)
         amps = lambda j, row: amp_refs[places[j][0]][places[j][1] + row]
-        inter_of = lambda j: inter_refs[inter_at[j][0]][i, inter_at[j][1]]
-        halves_into(hbuf, at, i, tab_ref, found, amps, inter_of)
-
-    def frames(i, at):
-        inter_of = lambda j, q: inter_refs[inter_at[j][0]][i, inter_at[j][1], pl.ds(q * W, W), :]
-        frames_into(outs, prev_ref, hbuf, at, i, inter_of, n)
-
-    in_turn([halves, frames], 8, group_of, (0, 1))
-
-
-def next_couple(table, inters, chunks, inter_at, places, amps, prev, last):
-    n = len(chunks)
-    group_of = GROUPS[n]
-    shapes = out_shapes(last)
+        halves_into(
+            hbuf, at, t + begin, tab_ref, found, amps, lambda j: inter_row(j, t)[...]
+        )
+
+    def frames(t, at):
+        inter_of = lambda j, q: inter_row(j, t)[pl.ds(q * W, W), :]
+        frames_into(out_ref, prev_ref, hbuf, at, t + begin, t, inter_of, n)
+
+    in_turn([halves, frames], count, group_of, (0, 1))
+
+
+def next_couple(
+    table, inters, chunks, inter_at, places, amps, prev, span=(0, 8), out_type=F32
+):
+    n, count = len(chunks), span[1]
+    group_of = min(GROUPS[n], count // 2)
     kernel = functools.partial(
         next_kernel,
         chunks,
@@ -352,17 +355,17 @@
         len(inters),
         len(amps),
         prev is not None,
-        len(shapes),
+        span,
         group_of,
     )
     return pl.pallas_call(
         kernel,
-        out_shape=shapes,
+        out_shape=jax.ShapeDtypeStruct((count, 2, W, W), out_type),
         in_specs=[SMEM] + [VMEM] * (len(inters) + len(amps) + (prev is not None)),
-        out_specs=(VMEM,) * len(shapes),
+        out_specs=VMEM,
         scratch_shapes=[pltpu.VMEM((2 * group_of, 2, W, n * W), BF16)],
         compiler_params=PARAMS,
-        cost_estimate=cost(0.4 + 0.4 * n),
+        cost_estimate=cost((0.4 + 0.4 * n) * (0.3 + 0.7 * count / 8)),
     )(table, *inters, *amps, *([prev] if prev is not None else []))
 
 
@@ -495,13 +498,15 @@
 
     first = functools.partial(first_couple, table, packed)
     data_1 = [mine, ring_a[1], ring_b[1], ring_a[2], ring_b[2]]
-    inter_1, part = first(chunks_1, places_1, data_1, None, False)
+    inter_1, part = first(chunks_1, places_1, data_1, None)
     last_hop, part = lax.optimization_barrier((ring_a[3], part))
     ring_a.append(along_z(last_hop, 1))
-    inter_2, part = first(chunks_2, places_2, [ring_a[3], ring_b[3]], part, False)
+    inter_2, part = first(chunks_2, places_2, [ring_a[3], ring_b[3]], part)
     inter_cross, cross = cross_first(cross_table, below, above, turned_mine)
     part, cross = lax.optimization_barrier((part, cross))
-    inter_3, own, others = first(chunks_3, [(0, 0)], [ring_a[4]], part, True)
+    last_part = functools.partial(first, chunks_3, [(0, 0)], [ring_a[4]], part)
+    inter_other, others = last_part((4, 4), BF16)
+    inter_own, own = last_part((0, 4), F32)
 
     denominator = pno_energies[:, :, None] + pno_energies[:, None, :] - occ_energies[:, None, None]
     integrals = exchange_ints.astype(F32)
@@ -515,7 +520,7 @@
     steps = [first_step, second, third]
     far = along_z(third[:2], 1)
 
-    (part,) = next_couple(
+    part = next_couple(
         table,
         [inter_1],
         chunks_1,
@@ -523,22 +528,21 @@
         [(0, 0), (1, 0), (1, 2), (2, 0), (2, 2)],
         [sent, steps[0], steps[1]],
         None,
-        False,
     )
     near, _ = lax.optimization_barrier((sent, third))
     below = lax.ppermute(near, "grp", [(0, 1), (1, 2), (2, 3), (3, 0)])
     above = lax.ppermute(near, "grp", [(1, 0), (2, 1), (3, 2), (0, 3)])
     part, below, above = lax.optimization_barrier((part, below, above))
     cross = cross_next(cross_table, inter_cross, below, above)
-    own, others = next_couple(
-        table,
-        [inter_2, inter_3],
-        chunks_2 + chunks_3,
-        [(0, 0), (0, 1), (1, 0)],
-        [(0, 0), (0, 2), (1, 0)],
-        [steps[2], far],
-        part,
-        True,
+    late = [(0, 0), (0, 1), (1, 0)]
+    late_amps = [(0, 0), (0, 2), (1, 0)]
+    chunks_23 = chunks_2 + chunks_3
+    amps_23 = [steps[2], far]
+    others = next_couple(
+        table, [inter_2, inter_other], chunks_23, late, late_amps, amps_23, part, (4, 4), BF16
+    )
+    own = next_couple(
+        table, [inter_2, inter_own], chunks_23, late, late_amps, amps_23, part, (0, 4), F32
     )
     coupled = gather_shares(own, others) + cross
     residual = integrals + denominator * current - coupled

time: 91.8 us -> 91.5 us (level)
  Pallas kernels: 18.9 us -> 20.9 us
  waiting for transfers between devices: 11.4 us -> 9.54 us
    pallas_call x5 -> x7, Pallas kernels: 14.6 us -> 16.6 us  [the longest x4 11.7 us: first_couple(): pl.pallas_call(kernel, out_shape=(jax.ShapeDtypeStruct((count, n, 2 * W,...]
    ppermute x28, waiting for transfers between devices: 11 us -> 9.1 us  [send(): return lax.ppermute(x, 'dev', routes(move))]
  transfers between devices with their start and end apart: 32 -> 32, of which waited for: 14 -> 12; matrix products, arithmetic and copies ran while one was open for 2% -> 2% of each run, Pallas kernels for 16% -> 19%
where the time goes in v3:
time: 91.5 us; the launch traced here: 91.3 us
  starting transfers between devices  54.3 us (59%)
  Pallas kernels  20.9 us (23%)
  waiting for transfers between devices  9.54 us (10%)
  local copies, waits for them, and re-layouts  4 us (4%)
  other arithmetic  1.49 us (2%)
  between operations  1.05 us (1%)
    ppermute x28, starting transfers between devices, send(): return lax.ppermute(x, 'dev', routes(move))  50.1 us
    pallas_call x4, Pallas kernels, first_couple(): pl.pallas_call(kernel, out_shape=(jax.ShapeDtypeStruct((count, n, 2 * W,...  11.7 us
    ppermute x28, waiting for transfers between devices, send(): return lax.ppermute(x, 'dev', routes(move))  9.1 us
    pallas_call x3, Pallas kernels, next_couple(): pl.pallas_call(kernel, out_shape=jax.ShapeDtypeStruct((count, 2, W, W), o...  4.93 us
    unnamed x35, local copies, waits for them, and re-layouts  2.68 us
    ppermute x1, starting transfers between devices, on_device(): above = lax.ppermute(mine, 'grp', [(1, 0), (2, 1), (3, 2), (0, 3)])  2.48 us
  transfers between devices with their start and end apart: 32, of which 12 were waited for; matrix products, arithmetic and copies ran while one was open for 2% of the time, Pallas kernels for 19%

profile of v3, /device:TPU:1, one launch (start us, length us, event | category | flops | bytes accessed | tf_op | source)
XLA Modules:
  0.0 91.3 jit_solution(15884773551145091008)
XLA Ops:
  3.2 3.3 %collective-permute-start = (bf16[2,640,128]{2,1,0:T(8,128)(2,1)S(1)}, bf16[2,640,128]{2,1,0:T(8,128)(2,1)S(1)}, u32[]{:S(2)}, u32[]{:S(2)}) collective-permute-start(bf16[2,640,128]{2,1,0:T(8,128)(2,1)S(1)} %shard_map.122.own_ref.refs_2_), channel_id=1, source_target_pairs={{0,1},{1,0},{2,3},{3,2},{4,5},{5,4},{6,7},{7,6},{8,9},{9,8},{10,11... | collective-permute-start | bytes 983048 | tf_op jit(solution)/shard_map/ppermute | solution.py:42
  6.5 3.8 %collective-permute-start.12 = (bf16[2,640,128]{2,1,0:T(8,128)(2,1)S(1)}, bf16[2,640,128]{2,1,0:T(8,128)(2,1)S(1)}, u32[]{:S(2)}, u32[]{:S(2)}) collective-permute-start(bf16[2,640,128]{2,1,0:T(8,128)(2,1)S(1)} %shard_map.122.own_ref.refs_2_), channel_id=1, source_target_pairs={{0,2},{1,15},{2,4},{3,1},{4,6},{5,3},{6,8},{7,5},{8,10},{9,7},{10,... | collective-permute-start | bytes 983048 | tf_op jit(solution)/shard_map/ppermute | solution.py:42
  10.4 2.5 %collective-permute-start.6 = (bf16[2,640,128]{2,1,0:T(8,128)(2,1)S(1)}, bf16[2,640,128]{2,1,0:T(8,128)(2,1)S(1)}, u32[]{:S(2)}, u32[]{:S(2)}) collective-permute-start(bf16[2,640,128]{2,1,0:T(8,128)(2,1)S(1)} %shard_map.122.own_ref.refs_2_), channel_id=1, source_target_pairs={{64,0},{128,64},{192,128},{0,192},{65,1},{129,65},{193,129},{1,193... | collective-permute-start | bytes 983048 | tf_op jit(solution)/shard_map/ppermute | solution.py:476
  13.7 2.8 %collective-permute-start.3 = (bf16[1040,128]{1,0:T(8,128)(2,1)S(1)}, bf16[1040,128]{1,0:T(8,128)(2,1)S(1)}, u32[]{:S(2)}, u32[]{:S(2)}) collective-permute-start(bf16[1040,128]{1,0:T(8,128)(2,1)S(1)} %shard_map.123.refs_0_.own_ref), channel_id=1, source_target_pairs={{0,48},{1,49},{2,50},{3,51},{4,52},{5,53},{6,54},{7,55},{8,56},{9,... | collective-permute-start | bytes 798728 | tf_op jit(solution)/shard_map/ppermute | solution.py:42
  18.3 1.6 %collective-permute-done.3.refs_3_ = bf16[1040,128]{1,0:T(8,128)(2,1)S(1)} collective-permute-done((bf16[1040,128]{1,0:T(8,128)(2,1)S(1)}, bf16[1040,128]{1,0:T(8,128)(2,1)S(1)}, u32[]{:S(2)}, u32[]{:S(2)}) %collective-permute-start.3) | collective-permute-done | bytes 266272 | tf_op jit(solution)/shard_map/ppermute | solution.py:42
  19.9 3.4 %collective-permute-start.13 = (bf16[2,640,128]{2,1,0:T(8,128)(2,1)S(1)}, bf16[2,640,128]{2,1,0:T(8,128)(2,1)}, u32[]{:S(2)}, u32[]{:S(2)}) collective-permute-start(bf16[2,640,128]{2,1,0:T(8,128)(2,1)S(1)} %collective-permute-done.12.refs_3_), channel_id=1, source_target_pairs={{0,2},{1,15},{2,4},{3,1},{4,6},{5,3},{6,8},{7,5},{8,10},{9,7},{10,... | collective-permute-start | bytes 983048 | tf_op jit(solution)/shard_map/ppermute | solution.py:42
  23.6 3.2 %collective-permute-start.7 = (bf16[1040,128]{1,0:T(8,128)(2,1)S(1)}, bf16[1040,128]{1,0:T(8,128)(2,1)S(1)}, u32[]{:S(2)}, u32[]{:S(2)}) collective-permute-start(bf16[1040,128]{1,0:T(8,128)(2,1)S(1)} %broadcast_select_fusion), channel_id=1, source_target_pairs={{0,16},{1,49},{2,18},{3,51},{4,20},{5,53},{6,22},{7,55},{8,24},{9,... | collective-permute-start | bytes 798728 | tf_op jit(solution)/shard_map/ppermute | solution.py:42
  30.2 2.1 %collective-permute-start.14 = (bf16[2,640,128]{2,1,0:T(8,128)(2,1)}, bf16[2,640,128]{2,1,0:T(8,128)(2,1)}, u32[]{:S(2)}, u32[]{:S(2)}) collective-permute-start(bf16[2,640,128]{2,1,0:T(8,128)(2,1)} %collective-permute-done.13.refs_5_), channel_id=1, source_target_pairs={{0,2},{1,15},{2,4},{3,1},{4,6},{5,3},{6,8},{7,5},{8,10},{9,7},{10,... | collective-permute-start | bytes 983048 | tf_op jit(solution)/shard_map/ppermute | solution.py:42
  32.9 2.4 %collective-permute-start.16 = (bf16[2,640,128]{2,1,0:T(8,128)(2,1)}, bf16[2,640,128]{2,1,0:T(8,128)(2,1)}, u32[]{:S(2)}, u32[]{:S(2)}) collective-permute-start(bf16[2,640,128]{2,1,0:T(8,128)(2,1)} %collective-permute-done.4.refs_6_), channel_id=1, source_target_pairs={{0,2},{1,15},{2,4},{3,1},{4,6},{5,3},{6,8},{7,5},{8,10},{9,7},{10,... | collective-permute-start | bytes 983048 | tf_op jit(solution)/shard_map/ppermute | solution.py:42
  36.1 5.7 %shard_map.125 = (bf16[8,5,256,128]{3,2,1,0:T(8,128)(2,1)S(1)}, f32[8,2,128,128]{3,2,1,0:T(8,128)S(1)}) custom-call(f32[904]{0:T(1024)S(1)} %concatenate.12.refs_0_, bf16[8320,128]{1,0:T(8,128)(2,1)S(1)} %shard_map.124.refs_1_, bf16[2,640,128]{2,1,0:T(8,128)(2,1)S(1)} %shard_map.122.own_ref.refs_2_, ...), custom_call_target="tpu_custom_call" | custom-call | flops 6440000000 | bytes 1024 | tf_op jit(solution)/shard_map/pallas_call | solution.py:300
  41.8 1.8 %collective-permute-start.15 = (bf16[2,640,128]{2,1,0:T(8,128)(2,1)}, bf16[2,640,128]{2,1,0:T(8,128)(2,1)S(1)}, u32[]{:S(2)}, u32[]{:S(2)}) collective-permute-start(bf16[2,640,128]{2,1,0:T(8,128)(2,1)} %collective-permute-done.14.refs_2_), channel_id=1, source_target_pairs={{0,2},{1,15},{2,4},{3,1},{4,6},{5,3},{6,8},{7,5},{8,10},{9,7},{10,... | collective-permute-start | bytes 983048 | tf_op jit(solution)/shard_map/ppermute | solution.py:42
  43.6 1.7 %shard_map.127 = (bf16[4,256,128]{2,1,0:T(8,128)(2,1)S(1)}, f32[2,128,128]{2,1,0:T(8,128)S(1)}) custom-call(f32[2064]{0:T(1024)S(1)} %concatenate.13.tab_ref, bf16[2,640,128]{2,1,0:T(8,128)(2,1)S(1)} %copy-done.5, bf16[2,640,128]{2,1,0:T(8,128)(2,1)S(1)} %collective-permute-done.6.above_ref, bf16[1040,128]{1,0:T(8,128)(2,1)S(1)} %shard_map.123.refs_0_.own_ref), custom_call_target="tpu_custom_call" | custom-call | flops 2300000000 | bytes 1024 | tf_op jit(solution)/shard_map/pallas_call | solution.py:397
  45.3 2.9 %shard_map.126 = (bf16[8,2,256,128]{3,2,1,0:T(8,128)(2,1)S(1)}, f32[8,2,128,128]{3,2,1,0:T(8,128)S(1)}) custom-call(f32[904]{0:T(1024)S(1)} %concatenate.12.refs_0_, bf16[8320,128]{1,0:T(8,128)(2,1)S(1)} %shard_map.124.refs_1_, bf16[2,640,128]{2,1,0:T(8,128)(2,1)} %collective-permute-done.14.refs_2_, bf16[2,640,128]{2,1,0:T(8,128)(2,1)} %collective-permute-done.16.refs_3_, ...), custom_call_target="tpu_custom_call" | custom-call | flops 3128000000 | bytes 1024 | tf_op jit(solution)/shard_map/pallas_call | solution.py:300
  48.3 1.5 %shard_map.129 = (bf16[4,1,256,128]{3,2,1,0:T(8,128)(2,1)S(1)}, bf16[4,2,128,128]{3,2,1,0:T(8,128)(2,1)S(1)}) custom-call(f32[904]{0:T(1024)S(1)} %concatenate.12.refs_0_, bf16[8320,128]{1,0:T(8,128)(2,1)S(1)} %shard_map.124.refs_1_, bf16[2,640,128]{2,1,0:T(8,128)(2,1)S(1)} %collective-permute-done.15.refs_2_, f32[8,2,128,128]{3,2,1,0:T(8,128)S(1)} %get-tuple-element.37.refs_3_), custom_call_target="tpu_custom_call" | custom-call | flops 1315600000 | bytes 1024 | tf_op jit(solution)/shard_map/pallas_call | solution.py:300
  49.9 1.3 %collective-permute-start.17 = (bf16[4,2,128,128]{3,2,1,0:T(8,128)(2,1)S(1)}, bf16[4,2,128,128]{3,2,1,0:T(8,128)(2,1)S(1)}, u32[]{:S(2)}, u32[]{:S(2)}) collective-permute-start(bf16[4,2,128,128]{3,2,1,0:T(8,128)(2,1)S(1)} %get-tuple-element.39), channel_id=1, source_target_pairs={{0,1},{1,0},{2,3},{3,2},{4,5},{5,4},{6,7},{7,6},{8,9},{9,8},{10,11... | collective-permute-start | bytes 786440 | tf_op jit(solution)/shard_map/ppermute | solution.py:42
  51.2 1.5 %shard_map.128 = (bf16[4,1,256,128]{3,2,1,0:T(8,128)(2,1)S(1)}, f32[4,2,128,128]{3,2,1,0:T(8,128)S(1)}) custom-call(f32[904]{0:T(1024)S(1)} %concatenate.12.refs_0_, bf16[8320,128]{1,0:T(8,128)(2,1)S(1)} %shard_map.124.refs_1_, bf16[2,640,128]{2,1,0:T(8,128)(2,1)S(1)} %collective-permute-done.15.refs_2_, f32[8,2,128,128]{3,2,1,0:T(8,128)S(1)} %get-tuple-element.37.refs_3_), custom_call_target="tpu_custom_call" | custom-call | flops 1315600000 | bytes 1024 | tf_op jit(solution)/shard_map/pallas_call | solution.py:300
  52.9 2.6 %collective-permute-start.18 = (bf16[2,128,128]{2,1,0:T(8,128)(2,1)S(1)}, bf16[2,128,128]{2,1,0:T(8,128)(2,1)S(1)}, u32[]{:S(2)}, u32[]{:S(2)}) collective-permute-start(bf16[2,128,128]{2,1,0:T(8,128)(2,1)S(1)} %get-tuple-element.61), channel_id=1, source_target_pairs={{0,32},{1,33},{2,34},{3,35},{4,36},{5,37},{6,38},{7,39},{8,40},{9,... | collective-permute-start | bytes 196616 | tf_op jit(solution)/shard_map/ppermute | solution.py:42
  55.5 1.3 %collective-permute-start.20 = (bf16[2,128,128]{2,1,0:T(8,128)(2,1)S(1)}, bf16[2,128,128]{2,1,0:T(8,128)(2,1)S(1)}, u32[]{:S(2)}, u32[]{:S(2)}) collective-permute-start(bf16[2,128,128]{2,1,0:T(8,128)(2,1)S(1)} %get-tuple-element.62), channel_id=1, source_target_pairs={{0,16},{1,17},{2,18},{3,19},{4,20},{5,21},{6,22},{7,23},{8,24},{9,... | collective-permute-start | bytes 196616 | tf_op jit(solution)/shard_map/ppermute | solution.py:42
  56.8 1.4 %collective-permute-start.19 = (bf16[2,128,128]{2,1,0:T(8,128)(2,1)S(1)}, bf16[2,128,128]{2,1,0:T(8,128)(2,1)S(1)}, u32[]{:S(2)}, u32[]{:S(2)}) collective-permute-start(bf16[2,128,128]{2,1,0:T(8,128)(2,1)S(1)} %get-tuple-element.63), channel_id=1, source_target_pairs={{0,48},{1,49},{2,50},{3,51},{4,52},{5,53},{6,54},{7,55},{8,56},{9,... | collective-permute-start | bytes 196616 | tf_op jit(solution)/shard_map/ppermute | solution.py:42
  58.2 1.6 %collective-permute-done.20 = bf16[2,128,128]{2,1,0:T(8,128)(2,1)S(1)} collective-permute-done((bf16[2,128,128]{2,1,0:T(8,128)(2,1)S(1)}, bf16[2,128,128]{2,1,0:T(8,128)(2,1)S(1)}, u32[]{:S(2)}, u32[]{:S(2)}) %collective-permute-start.20) | collective-permute-done | bytes 65568 | tf_op jit(solution)/shard_map/ppermute | solution.py:42
  60.3 1.5 %collective-permute-start.21 = (bf16[2,128,128]{2,1,0:T(8,128)(2,1)S(1)}, bf16[2,128,128]{2,1,0:T(8,128)(2,1)S(1)}, u32[]{:S(2)}, u32[]{:S(2)}) collective-permute-start(bf16[2,128,128]{2,1,0:T(8,128)(2,1)S(1)} %get-tuple-element.44.refs_2_), channel_id=1, source_target_pairs={{0,1},{1,0},{2,3},{3,2},{4,5},{5,4},{6,7},{7,6},{8,9},{9,8},{10,11... | collective-permute-start | bytes 196616 | tf_op jit(solution)/shard_map/ppermute | solution.py:42
  62.8 2.4 %collective-permute-start.22 = (bf16[4,128,128]{2,1,0:T(8,128)(2,1)S(1)}, bf16[4,128,128]{2,1,0:T(8,128)(2,1)S(1)}, u32[]{:S(2)}, u32[]{:S(2)}) collective-permute-start(bf16[4,128,128]{2,1,0:T(8,128)(2,1)S(1)} %pad_maximum_fusion), channel_id=1, source_target_pairs={{0,6},{1,11},{2,8},{3,13},{4,10},{5,15},{6,12},{7,1},{8,14},{9,3},... | collective-permute-start | bytes 393224 | tf_op jit(solution)/shard_map/ppermute | solution.py:42
  65.2 3.1 %collective-permute-start.25 = (bf16[4,128,128]{2,1,0:T(8,128)(2,1)S(1)}, bf16[4,128,128]{2,1,0:T(8,128)(2,1)S(1)}, u32[]{:S(2)}, u32[]{:S(2)}) collective-permute-start(bf16[4,128,128]{2,1,0:T(8,128)(2,1)S(1)} %pad_maximum_fusion), channel_id=1, source_target_pairs={{0,4},{1,13},{2,6},{3,15},{4,8},{5,1},{6,10},{7,3},{8,12},{9,5},{1... | collective-permute-start | bytes 393224 | tf_op jit(solution)/shard_map/ppermute | solution.py:42
  70.3 3.9 %collective-permute-start.23 = (bf16[2,128,128]{2,1,0:T(8,128)(2,1)S(1)}, bf16[2,128,128]{2,1,0:T(8,128)(2,1)S(1)}, u32[]{:S(2)}, u32[]{:S(2)}) collective-permute-start(bf16[2,128,128]{2,1,0:T(8,128)(2,1)S(1)} %slice.111), channel_id=1, source_target_pairs={{0,2},{1,15},{2,4},{3,1},{4,6},{5,3},{6,8},{7,5},{8,10},{9,7},{10,... | collective-permute-start | bytes 196616 | tf_op jit(solution)/shard_map/ppermute | solution.py:42
  74.8 2.4 %shard_map.130.refs_5_ = f32[8,2,128,128]{3,2,1,0:T(8,128)S(1)} custom-call(f32[904]{0:T(1024)S(1)} %concatenate.12.refs_0_, bf16[8,5,256,128]{3,2,1,0:T(8,128)(2,1)S(1)} %get-tuple-element.43.refs_1_, bf16[2,128,128]{2,1,0:T(8,128)(2,1)S(1)} %get-tuple-element.44.refs_2_, bf16[4,128,128]{2,1,0:T(8,128)(2,1)S(1)} %collective-permute-done.24.refs_3_, ...), custom_call_target="tpu_custom_call" | custom-call | flops 2760000000 | bytes 1024 | tf_op jit(solution)/shard_map/pallas_call | solution.py:361
  77.4 1.3 %shard_map.132 = bf16[4,2,128,128]{3,2,1,0:T(8,128)(2,1)S(1)} custom-call(f32[904]{0:T(1024)S(1)} %concatenate.12.refs_0_, bf16[8,2,256,128]{3,2,1,0:T(8,128)(2,1)S(1)} %get-tuple-element.41.refs_1_, bf16[4,1,256,128]{3,2,1,0:T(8,128)(2,1)S(1)} %get-tuple-element.46.refs_2_, bf16[4,128,128]{2,1,0:T(8,128)(2,1)S(1)} %collective-permute-done.22.refs_3_, ...), custom_call_target="tpu_custom_call" | custom-call | flops 1196000000 | bytes 1024 | tf_op jit(solution)/shard_map/pallas_call | solution.py:361
  78.7 3.7 %collective-permute-start.28 = (bf16[4,2,128,128]{3,2,1,0:T(8,128)(2,1)S(1)}, bf16[4,2,128,128]{3,2,1,0:T(8,128)(2,1)S(1)}, u32[]{:S(2)}, u32[]{:S(2)}) collective-permute-start(bf16[4,2,128,128]{3,2,1,0:T(8,128)(2,1)S(1)} %shard_map.132), channel_id=1, source_target_pairs={{0,1},{1,0},{2,3},{3,2},{4,5},{5,4},{6,7},{7,6},{8,9},{9,8},{10,11... | collective-permute-start | bytes 786440 | tf_op jit(solution)/shard_map/ppermute | solution.py:42
  82.4 1.3 %shard_map.131 = f32[4,2,128,128]{3,2,1,0:T(8,128)S(1)} custom-call(f32[904]{0:T(1024)S(1)} %concatenate.12.refs_0_, bf16[8,2,256,128]{3,2,1,0:T(8,128)(2,1)S(1)} %get-tuple-element.41.refs_1_, bf16[4,1,256,128]{3,2,1,0:T(8,128)(2,1)S(1)} %get-tuple-element.42.refs_2_, bf16[4,128,128]{2,1,0:T(8,128)(2,1)S(1)} %collective-permute-done.22.refs_3_, ...), custom_call_target="tpu_custom_call" | custom-call | flops 1196000000 | bytes 1024 | tf_op jit(solution)/shard_map/pallas_call | solution.py:361
  83.8 1.3 %collective-permute-start.29 = (bf16[2,128,128]{2,1,0:T(8,128)(2,1)S(1)}, bf16[2,128,128]{2,1,0:T(8,128)(2,1)S(1)}, u32[]{:S(2)}, u32[]{:S(2)}) collective-permute-start(bf16[2,128,128]{2,1,0:T(8,128)(2,1)S(1)} %get-tuple-element.58), channel_id=1, source_target_pairs={{0,32},{1,33},{2,34},{3,35},{4,36},{5,37},{6,38},{7,39},{8,40},{9,... | collective-permute-start | bytes 196616 | tf_op jit(solution)/shard_map/ppermute | solution.py:42
  85.1 1.8 %collective-permute-start.31 = (bf16[2,128,128]{2,1,0:T(8,128)(2,1)S(1)}, bf16[2,128,128]{2,1,0:T(8,128)(2,1)S(1)}, u32[]{:S(2)}, u32[]{:S(2)}) collective-permute-start(bf16[2,128,128]{2,1,0:T(8,128)(2,1)S(1)} %get-tuple-element.59), channel_id=1, source_target_pairs={{0,16},{1,17},{2,18},{3,19},{4,20},{5,21},{6,22},{7,23},{8,24},{9,... | collective-permute-start | bytes 196616 | tf_op jit(solution)/shard_map/ppermute | solution.py:42
  87.8 1.0 %shard_map.133 = f32[2,128,128]{2,1,0:T(8,128)S(1)} custom-call(f32[2064]{0:T(1024)S(1)} %concatenate.13.tab_ref, bf16[4,256,128]{2,1,0:T(8,128)(2,1)S(1)} %get-tuple-element.47.inter_ref, bf16[2,128,128]{2,1,0:T(8,128)(2,1)S(1)} %collective-permute-done.26.below_ref, bf16[2,128,128]{2,1,0:T(8,128)(2,1)S(1)} %collective-permute-done.27.above_ref), custom_call_target="tpu_custom_call" | custom-call | flops 1150000000 | bytes 1024 | tf_op jit(solution)/shard_map/pallas_call | solution.py:425
  88.8 1.7 %collective-permute-done.31 = bf16[2,128,128]{2,1,0:T(8,128)(2,1)S(1)} collective-permute-done((bf16[2,128,128]{2,1,0:T(8,128)(2,1)S(1)}, bf16[2,128,128]{2,1,0:T(8,128)(2,1)S(1)}, u32[]{:S(2)}, u32[]{:S(2)}) %collective-permute-start.31) | collective-permute-done | bytes 65568 | tf_op jit(solution)/shard_map/ppermute | solution.py:42
  (111 shorter events, 16.4 us)
Async XLA Ops:
  3.2 9.8 %collective-permute-start = (bf16[2,640,128]{2,1,0:T(8,128)(2,1)S(1)}, bf16[2,640,128]{2,1,0:T(8,128)(2,1)S(1)}, u32[]{:S(2)}, u32[]{:S(2)}) collective-permute-start(bf16[2,640,128]{2,1,0:T(8,128)(2,1)S(1)} %shard_map.122.own_ref.refs_2_), channel_id=1, source_target_pairs={{0,1},{1,0},{2,3},{3,2},{4,5},{5,4},{6,7},{7,6},{8,9},{9,8},{10,11... | collective-permute-start | bytes 983048 | tf_op jit(solution)/shard_map/ppermute | solution.py:42
  6.5 11.7 %collective-permute-start.12 = (bf16[2,640,128]{2,1,0:T(8,128)(2,1)S(1)}, bf16[2,640,128]{2,1,0:T(8,128)(2,1)S(1)}, u32[]{:S(2)}, u32[]{:S(2)}) collective-permute-start(bf16[2,640,128]{2,1,0:T(8,128)(2,1)S(1)} %shard_map.122.own_ref.refs_2_), channel_id=1, source_target_pairs={{0,2},{1,15},{2,4},{3,1},{4,6},{5,3},{6,8},{7,5},{8,10},{9,7},{10,... | collective-permute-start | bytes 983048 | tf_op jit(solution)/shard_map/ppermute | solution.py:42
  10.4 17.1 %collective-permute-start.6 = (bf16[2,640,128]{2,1,0:T(8,128)(2,1)S(1)}, bf16[2,640,128]{2,1,0:T(8,128)(2,1)S(1)}, u32[]{:S(2)}, u32[]{:S(2)}) collective-permute-start(bf16[2,640,128]{2,1,0:T(8,128)(2,1)S(1)} %shard_map.122.own_ref.refs_2_), channel_id=1, source_target_pairs={{64,0},{128,64},{192,128},{0,192},{65,1},{129,65},{193,129},{1,193... | collective-permute-start | bytes 983048 | tf_op jit(solution)/shard_map/ppermute | solution.py:476
  13.7 6.2 %collective-permute-start.3 = (bf16[1040,128]{1,0:T(8,128)(2,1)S(1)}, bf16[1040,128]{1,0:T(8,128)(2,1)S(1)}, u32[]{:S(2)}, u32[]{:S(2)}) collective-permute-start(bf16[1040,128]{1,0:T(8,128)(2,1)S(1)} %shard_map.123.refs_0_.own_ref), channel_id=1, source_target_pairs={{0,48},{1,49},{2,50},{3,51},{4,52},{5,53},{6,54},{7,55},{8,56},{9,... | collective-permute-start | bytes 798728 | tf_op jit(solution)/shard_map/ppermute | solution.py:42
  16.5 7.1 %collective-permute-start.2 = (bf16[1040,128]{1,0:T(8,128)(2,1)S(1)}, bf16[1040,128]{1,0:T(8,128)(2,1)S(1)}, u32[]{:S(2)}, u32[]{:S(2)}) collective-permute-start(bf16[1040,128]{1,0:T(8,128)(2,1)S(1)} %shard_map.123.refs_0_.own_ref), channel_id=1, source_target_pairs={{0,16},{1,17},{2,18},{3,19},{4,20},{5,21},{6,22},{7,23},{8,24},{9,... | collective-permute-start | bytes 798728 | tf_op jit(solution)/shard_map/ppermute | solution.py:42
  16.5 7.1 %collective-permute-start.1 = (bf16[2,640,128]{2,1,0:T(8,128)(2,1)S(1)}, bf16[2,640,128]{2,1,0:T(8,128)(2,1)S(1)}, u32[]{:S(2)}, u32[]{:S(2)}) collective-permute-start(bf16[2,640,128]{2,1,0:T(8,128)(2,1)S(1)} %collective-permute-done), channel_id=1, source_target_pairs={{0,2},{1,15},{2,4},{3,1},{4,6},{5,3},{6,8},{7,5},{8,10},{9,7},{10,... | collective-permute-start | bytes 983048 | tf_op jit(solution)/shard_map/ppermute | solution.py:42
  18.2 9.8 %collective-permute-start.5 = (bf16[2,640,128]{2,1,0:T(8,128)(2,1)S(1)}, bf16[2,640,128]{2,1,0:T(8,128)(2,1)S(1)}, u32[]{:S(2)}, u32[]{:S(2)}) collective-permute-start(bf16[2,640,128]{2,1,0:T(8,128)(2,1)S(1)} %shard_map.122.own_ref.refs_2_), channel_id=1, source_target_pairs={{0,64},{64,128},{128,192},{192,0},{1,65},{65,129},{129,193},{193,1... | collective-permute-start | bytes 983048 | tf_op jit(solution)/shard_map/ppermute | solution.py:475
  19.9 8.9 %collective-permute-start.13 = (bf16[2,640,128]{2,1,0:T(8,128)(2,1)S(1)}, bf16[2,640,128]{2,1,0:T(8,128)(2,1)}, u32[]{:S(2)}, u32[]{:S(2)}) collective-permute-start(bf16[2,640,128]{2,1,0:T(8,128)(2,1)S(1)} %collective-permute-done.12.refs_3_), channel_id=1, source_target_pairs={{0,2},{1,15},{2,4},{3,1},{4,6},{5,3},{6,8},{7,5},{8,10},{9,7},{10,... | collective-permute-start | bytes 983048 | tf_op jit(solution)/shard_map/ppermute | solution.py:42
  23.6 6.5 %collective-permute-start.7 = (bf16[1040,128]{1,0:T(8,128)(2,1)S(1)}, bf16[1040,128]{1,0:T(8,128)(2,1)S(1)}, u32[]{:S(2)}, u32[]{:S(2)}) collective-permute-start(bf16[1040,128]{1,0:T(8,128)(2,1)S(1)} %broadcast_select_fusion), channel_id=1, source_target_pairs={{0,16},{1,49},{2,18},{3,51},{4,20},{5,53},{6,22},{7,55},{8,24},{9,... | collective-permute-start | bytes 798728 | tf_op jit(solution)/shard_map/ppermute | solution.py:42
  26.8 6.0 %collective-permute-start.4 = (bf16[2,640,128]{2,1,0:T(8,128)(2,1)S(1)}, bf16[2,640,128]{2,1,0:T(8,128)(2,1)}, u32[]{:S(2)}, u32[]{:S(2)}) collective-permute-start(bf16[2,640,128]{2,1,0:T(8,128)(2,1)S(1)} %collective-permute-done.1.refs_4_), channel_id=1, source_target_pairs={{0,2},{1,15},{2,4},{3,1},{4,6},{5,3},{6,8},{7,5},{8,10},{9,7},{10,... | collective-permute-start | bytes 983048 | tf_op jit(solution)/shard_map/ppermute | solution.py:42
  27.5 5.5 %collective-permute-start.8 = (bf16[1040,128]{1,0:T(8,128)(2,1)S(1)}, bf16[1040,128]{1,0:T(8,128)(2,1)S(1)}, u32[]{:S(2)}, u32[]{:S(2)}) collective-permute-start(bf16[1040,128]{1,0:T(8,128)(2,1)S(1)} %shard_map.123.refs_0_.own_ref), channel_id=1, source_target_pairs={{0,1},{1,0},{2,3},{3,2},{4,5},{5,4},{6,7},{7,6},{8,9},{9,8},{10,11... | collective-permute-start | bytes 798728 | tf_op jit(solution)/shard_map/ppermute | solution.py:42
  28.7 6.6 %collective-permute-start.9 = (bf16[1040,128]{1,0:T(8,128)(2,1)S(1)}, bf16[1040,128]{1,0:T(8,128)(2,1)S(1)}, u32[]{:S(2)}, u32[]{:S(2)}) collective-permute-start(bf16[1040,128]{1,0:T(8,128)(2,1)S(1)} %collective-permute-done.2.refs_1_), channel_id=1, source_target_pairs={{0,1},{1,0},{2,3},{3,2},{4,5},{5,4},{6,7},{7,6},{8,9},{9,8},{10,11... | collective-permute-start | bytes 798728 | tf_op jit(solution)/shard_map/ppermute | solution.py:42
  28.8 6.5 %collective-permute-start.11 = (bf16[1040,128]{1,0:T(8,128)(2,1)S(1)}, bf16[1040,128]{1,0:T(8,128)(2,1)S(1)}, u32[]{:S(2)}, u32[]{:S(2)}) collective-permute-start(bf16[1040,128]{1,0:T(8,128)(2,1)S(1)} %collective-permute-done.3.refs_3_), channel_id=1, source_target_pairs={{0,1},{1,0},{2,3},{3,2},{4,5},{5,4},{6,7},{7,6},{8,9},{9,8},{10,11... | collective-permute-start | bytes 798728 | tf_op jit(solution)/shard_map/ppermute | solution.py:42
  30.2 11.6 %collective-permute-start.14 = (bf16[2,640,128]{2,1,0:T(8,128)(2,1)}, bf16[2,640,128]{2,1,0:T(8,128)(2,1)}, u32[]{:S(2)}, u32[]{:S(2)}) collective-permute-start(bf16[2,640,128]{2,1,0:T(8,128)(2,1)} %collective-permute-done.13.refs_5_), channel_id=1, source_target_pairs={{0,2},{1,15},{2,4},{3,1},{4,6},{5,3},{6,8},{7,5},{8,10},{9,7},{10,... | collective-permute-start | bytes 983048 | tf_op jit(solution)/shard_map/ppermute | solution.py:42
  32.8 2.5 %collective-permute-start.10 = (bf16[1040,128]{1,0:T(8,128)(2,1)S(1)}, bf16[1040,128]{1,0:T(8,128)(2,1)S(1)}, u32[]{:S(2)}, u32[]{:S(2)}) collective-permute-start(bf16[1040,128]{1,0:T(8,128)(2,1)S(1)} %collective-permute-done.7.refs_2_), channel_id=1, source_target_pairs={{0,1},{1,0},{2,3},{3,2},{4,5},{5,4},{6,7},{7,6},{8,9},{9,8},{10,11... | collective-permute-start | bytes 798728 | tf_op jit(solution)/shard_map/ppermute | solution.py:42
  32.9 12.4 %collective-permute-start.16 = (bf16[2,640,128]{2,1,0:T(8,128)(2,1)}, bf16[2,640,128]{2,1,0:T(8,128)(2,1)}, u32[]{:S(2)}, u32[]{:S(2)}) collective-permute-start(bf16[2,640,128]{2,1,0:T(8,128)(2,1)} %collective-permute-done.4.refs_6_), channel_id=1, source_target_pairs={{0,2},{1,15},{2,4},{3,1},{4,6},{5,3},{6,8},{7,5},{8,10},{9,7},{10,... | collective-permute-start | bytes 983048 | tf_op jit(solution)/shard_map/ppermute | solution.py:42
  41.8 6.5 %collective-permute-start.15 = (bf16[2,640,128]{2,1,0:T(8,128)(2,1)}, bf16[2,640,128]{2,1,0:T(8,128)(2,1)S(1)}, u32[]{:S(2)}, u32[]{:S(2)}) collective-permute-start(bf16[2,640,128]{2,1,0:T(8,128)(2,1)} %collective-permute-done.14.refs_2_), channel_id=1, source_target_pairs={{0,2},{1,15},{2,4},{3,1},{4,6},{5,3},{6,8},{7,5},{8,10},{9,7},{10,... | collective-permute-start | bytes 983048 | tf_op jit(solution)/shard_map/ppermute | solution.py:42
  49.9 2.9 %collective-permute-start.17 = (bf16[4,2,128,128]{3,2,1,0:T(8,128)(2,1)S(1)}, bf16[4,2,128,128]{3,2,1,0:T(8,128)(2,1)S(1)}, u32[]{:S(2)}, u32[]{:S(2)}) collective-permute-start(bf16[4,2,128,128]{3,2,1,0:T(8,128)(2,1)S(1)} %get-tuple-element.39), channel_id=1, source_target_pairs={{0,1},{1,0},{2,3},{3,2},{4,5},{5,4},{6,7},{7,6},{8,9},{9,8},{10,11... | collective-permute-start | bytes 786440 | tf_op jit(solution)/shard_map/ppermute | solution.py:42
  52.9 5.3 %collective-permute-start.18 = (bf16[2,128,128]{2,1,0:T(8,128)(2,1)S(1)}, bf16[2,128,128]{2,1,0:T(8,128)(2,1)S(1)}, u32[]{:S(2)}, u32[]{:S(2)}) collective-permute-start(bf16[2,128,128]{2,1,0:T(8,128)(2,1)S(1)} %get-tuple-element.61), channel_id=1, source_target_pairs={{0,32},{1,33},{2,34},{3,35},{4,36},{5,37},{6,38},{7,39},{8,40},{9,... | collective-permute-start | bytes 196616 | tf_op jit(solution)/shard_map/ppermute | solution.py:42
  55.5 4.3 %collective-permute-start.20 = (bf16[2,128,128]{2,1,0:T(8,128)(2,1)S(1)}, bf16[2,128,128]{2,1,0:T(8,128)(2,1)S(1)}, u32[]{:S(2)}, u32[]{:S(2)}) collective-permute-start(bf16[2,128,128]{2,1,0:T(8,128)(2,1)S(1)} %get-tuple-element.62), channel_id=1, source_target_pairs={{0,16},{1,17},{2,18},{3,19},{4,20},{5,21},{6,22},{7,23},{8,24},{9,... | collective-permute-start | bytes 196616 | tf_op jit(solution)/shard_map/ppermute | solution.py:42
  56.8 3.4 %collective-permute-start.19 = (bf16[2,128,128]{2,1,0:T(8,128)(2,1)S(1)}, bf16[2,128,128]{2,1,0:T(8,128)(2,1)S(1)}, u32[]{:S(2)}, u32[]{:S(2)}) collective-permute-start(bf16[2,128,128]{2,1,0:T(8,128)(2,1)S(1)} %get-tuple-element.63), channel_id=1, source_target_pairs={{0,48},{1,49},{2,50},{3,51},{4,52},{5,53},{6,54},{7,55},{8,56},{9,... | collective-permute-start | bytes 196616 | tf_op jit(solution)/shard_map/ppermute | solution.py:42
  60.3 2.4 %collective-permute-start.21 = (bf16[2,128,128]{2,1,0:T(8,128)(2,1)S(1)}, bf16[2,128,128]{2,1,0:T(8,128)(2,1)S(1)}, u32[]{:S(2)}, u32[]{:S(2)}) collective-permute-start(bf16[2,128,128]{2,1,0:T(8,128)(2,1)S(1)} %get-tuple-element.44.refs_2_), channel_id=1, source_target_pairs={{0,1},{1,0},{2,3},{3,2},{4,5},{5,4},{6,7},{7,6},{8,9},{9,8},{10,11... | collective-permute-start | bytes 196616 | tf_op jit(solution)/shard_map/ppermute | solution.py:42
  62.8 5.9 %collective-permute-start.22 = (bf16[4,128,128]{2,1,0:T(8,128)(2,1)S(1)}, bf16[4,128,128]{2,1,0:T(8,128)(2,1)S(1)}, u32[]{:S(2)}, u32[]{:S(2)}) collective-permute-start(bf16[4,128,128]{2,1,0:T(8,128)(2,1)S(1)} %pad_maximum_fusion), channel_id=1, source_target_pairs={{0,6},{1,11},{2,8},{3,13},{4,10},{5,15},{6,12},{7,1},{8,14},{9,3},... | collective-permute-start | bytes 393224 | tf_op jit(solution)/shard_map/ppermute | solution.py:42
  65.2 9.0 %collective-permute-start.25 = (bf16[4,128,128]{2,1,0:T(8,128)(2,1)S(1)}, bf16[4,128,128]{2,1,0:T(8,128)(2,1)S(1)}, u32[]{:S(2)}, u32[]{:S(2)}) collective-permute-start(bf16[4,128,128]{2,1,0:T(8,128)(2,1)S(1)} %pad_maximum_fusion), channel_id=1, source_target_pairs={{0,4},{1,13},{2,6},{3,15},{4,8},{5,1},{6,10},{7,3},{8,12},{9,5},{1... | collective-permute-start | bytes 393224 | tf_op jit(solution)/shard_map/ppermute | solution.py:42
  68.3 6.5 %collective-permute-start.24 = (bf16[4,128,128]{2,1,0:T(8,128)(2,1)S(1)}, bf16[4,128,128]{2,1,0:T(8,128)(2,1)S(1)}, u32[]{:S(2)}, u32[]{:S(2)}) collective-permute-start(bf16[4,128,128]{2,1,0:T(8,128)(2,1)S(1)} %pad_maximum_fusion), channel_id=1, source_target_pairs={{0,2},{1,15},{2,4},{3,1},{4,6},{5,3},{6,8},{7,5},{8,10},{9,7},{10,... | collective-permute-start | bytes 393224 | tf_op jit(solution)/shard_map/ppermute | solution.py:42
  68.7 8.5 %collective-permute-start.27 = (bf16[2,128,128]{2,1,0:T(8,128)(2,1)S(1)}, bf16[2,128,128]{2,1,0:T(8,128)(2,1)S(1)}, u32[]{:S(2)}, u32[]{:S(2)}) collective-permute-start(bf16[2,128,128]{2,1,0:T(8,128)(2,1)S(1)} %get-tuple-element.44.refs_2_), channel_id=1, source_target_pairs={{64,0},{128,64},{192,128},{0,192},{65,1},{129,65},{193,129},{1,193... | collective-permute-start | bytes 196616 | tf_op jit(solution)/shard_map/ppermute | solution.py:534
  69.3 7.9 %collective-permute-start.26 = (bf16[2,128,128]{2,1,0:T(8,128)(2,1)S(1)}, bf16[2,128,128]{2,1,0:T(8,128)(2,1)S(1)}, u32[]{:S(2)}, u32[]{:S(2)}) collective-permute-start(bf16[2,128,128]{2,1,0:T(8,128)(2,1)S(1)} %get-tuple-element.44.refs_2_), channel_id=1, source_target_pairs={{0,64},{64,128},{128,192},{192,0},{1,65},{65,129},{129,193},{193,1... | collective-permute-start | bytes 196616 | tf_op jit(solution)/shard_map/ppermute | solution.py:533
  70.3 7.1 %collective-permute-start.23 = (bf16[2,128,128]{2,1,0:T(8,128)(2,1)S(1)}, bf16[2,128,128]{2,1,0:T(8,128)(2,1)S(1)}, u32[]{:S(2)}, u32[]{:S(2)}) collective-permute-start(bf16[2,128,128]{2,1,0:T(8,128)(2,1)S(1)} %slice.111), channel_id=1, source_target_pairs={{0,2},{1,15},{2,4},{3,1},{4,6},{5,3},{6,8},{7,5},{8,10},{9,7},{10,... | collective-permute-start | bytes 196616 | tf_op jit(solution)/shard_map/ppermute | solution.py:42
  78.7 5.0 %collective-permute-start.28 = (bf16[4,2,128,128]{3,2,1,0:T(8,128)(2,1)S(1)}, bf16[4,2,128,128]{3,2,1,0:T(8,128)(2,1)S(1)}, u32[]{:S(2)}, u32[]{:S(2)}) collective-permute-start(bf16[4,2,128,128]{3,2,1,0:T(8,128)(2,1)S(1)} %shard_map.132), channel_id=1, source_target_pairs={{0,1},{1,0},{2,3},{3,2},{4,5},{5,4},{6,7},{7,6},{8,9},{9,8},{10,11... | collective-permute-start | bytes 786440 | tf_op jit(solution)/shard_map/ppermute | solution.py:42
  83.8 5.0 %collective-permute-start.29 = (bf16[2,128,128]{2,1,0:T(8,128)(2,1)S(1)}, bf16[2,128,128]{2,1,0:T(8,128)(2,1)S(1)}, u32[]{:S(2)}, u32[]{:S(2)}) collective-permute-start(bf16[2,128,128]{2,1,0:T(8,128)(2,1)S(1)} %get-tuple-element.58), channel_id=1, source_target_pairs={{0,32},{1,33},{2,34},{3,35},{4,36},{5,37},{6,38},{7,39},{8,40},{9,... | collective-permute-start | bytes 196616 | tf_op jit(solution)/shard_map/ppermute | solution.py:42
  85.1 5.4 %collective-permute-start.31 = (bf16[2,128,128]{2,1,0:T(8,128)(2,1)S(1)}, bf16[2,128,128]{2,1,0:T(8,128)(2,1)S(1)}, u32[]{:S(2)}, u32[]{:S(2)}) collective-permute-start(bf16[2,128,128]{2,1,0:T(8,128)(2,1)S(1)} %get-tuple-element.59), channel_id=1, source_target_pairs={{0,16},{1,17},{2,18},{3,19},{4,20},{5,21},{6,22},{7,23},{8,24},{9,... | collective-permute-start | bytes 196616 | tf_op jit(solution)/shard_map/ppermute | solution.py:42
  86.9 3.6 %collective-permute-start.30 = (bf16[2,128,128]{2,1,0:T(8,128)(2,1)S(1)}, bf16[2,128,128]{2,1,0:T(8,128)(2,1)S(1)}, u32[]{:S(2)}, u32[]{:S(2)}) collective-permute-start(bf16[2,128,128]{2,1,0:T(8,128)(2,1)S(1)} %get-tuple-element.60), channel_id=1, source_target_pairs={{0,48},{1,49},{2,50},{3,51},{4,52},{5,53},{6,54},{7,55},{8,56},{9,... | collective-permute-start | bytes 196616 | tf_op jit(solution)/shard_map/ppermute | solution.py:42
  (14 other events, 121.6 us)
